TPU v7x, 32 devices: a whole 2x2x4 slice. The times are simulated.
32 devices in a mesh: groups: 2 (over y), dp: 8 (over z, x), tensor: 2 (over core).
Axes of the slice: x: 2, y: 2, z: 4, core: 2. Of those that a mesh axis runs over, the one named last changes fastest.
Arguments:
- requests: bfloat16 [6144, 8192], P(('groups', 'dp'), 'tensor'), parts along dimension 0, may hold values from -6 to 6
- adapter_index: int32 [6144, 1], P(('groups', 'dp')), parts along dimension 0, may hold values from 0 to 7; in each aligned block of 384 rows (0 to 383, 384 to 767, ...) at most 96 rows name the same one
- storage_slot_index: int32 [16], P('groups'), parts along dimension 0, may hold values from 0 to 7, each once
- key_base_weight: bfloat16 [8192, 1024], P('tensor'), may hold values from -0.0625 to 0.0625
- adapter_down_factor: bfloat16 [16, 8192, 64], P(('groups', 'dp'), 'tensor'), parts along dimension 0, may hold values from -0.0625 to 0.0625
- adapter_up_factor: bfloat16 [16, 64, 1024], P(('groups', 'dp')), parts along dimension 0, may hold values from -0.75 to 0.75
Outputs:
- key_rows: bfloat16 [6144, 1024], P(('groups', 'dp'), 'tensor'), parts along dimension 0
There are 2 independent parts, one for each index of `groups`. A program takes and returns all parts, laid end to end along the dimension named above; an argument that names none is the same for every part. Nothing has to cross between parts.
Inputs may be any that keep to these rules, and one draw needn't show every extreme that they name: `adapter_index`: in each aligned block of 384 rows (the requests of one index of dp) no adapter is named by more than 96 rows, a bound that some block reaches; every adapter is named by some request. `storage_slot_index`: each slot holds exactly one adapter; slot s is stored on index s of dp.
All inputs are finite; a program needn't handle non-finite values.
Results may differ from a plain program's by a relative error of at most 0.001.
Values may be sent and summed in bfloat16 or wider, within the bound.
No kernel may reach another device: no remote copies, remote signals or barrier semaphores. Data moves between devices by JAX's collectives and lax.ppermute only.
A program may use at most 128 MiB of HBM per device.

v0:
```python
import jax
import jax.numpy as jnp
from jax import lax
from jax.sharding import PartitionSpec as P


def shards(
    requests,
    adapter_index,
    storage_slot_index,
    key_base_weight,
    adapter_down_factor,
    adapter_up_factor,
):
    rows_here = requests.shape[0]
    table_index = jnp.arange(storage_slot_index.shape[0], dtype=jnp.int32)
    matched = adapter_index == table_index[None, :]
    owner_of = jnp.sum(jnp.where(matched, storage_slot_index[None, :], 0), axis=1)
    partial_value = jnp.dot(requests, key_base_weight, preferred_element_type=jnp.float32)
    rank_width = adapter_down_factor.shape[2]
    a_piece = lax.all_gather(adapter_down_factor, "dp", axis=0, tiled=True)
    b_piece = lax.all_gather(adapter_up_factor, "dp", axis=0, tiled=True)
    piece_count = a_piece.shape[0]
    down_part = jnp.einsum("td,ndr->tnr", requests, a_piece, preferred_element_type=jnp.float32)
    chosen = owner_of[:, None] == jnp.arange(piece_count, dtype=jnp.int32)[None, :]
    weights = jnp.where(chosen[:, :, None], down_part, 0.0).reshape(
        rows_here, piece_count * rank_width
    )
    b_flat = b_piece.reshape(piece_count * rank_width, b_piece.shape[2]).astype(jnp.float32)
    extra = jnp.dot(weights, b_flat, precision=lax.Precision.HIGHEST)
    key_rows = lax.psum_scatter(
        partial_value + extra, "tensor", scatter_dimension=1, tiled=True
    ).astype(jnp.bfloat16)
    return key_rows


def solution(mesh):
    placed = (
        P(("groups", "dp"), "tensor"),
        P(("groups", "dp"), None),
        P("groups"),
        P("tensor", None),
        P(("groups", "dp"), "tensor", None),
        P(("groups", "dp"), None, None),
    )
    return jax.shard_map(
        shards, mesh=mesh, in_specs=placed, out_specs=P(("groups", "dp"), "tensor"), check_vma=False
    )
```

profile of v0, /device:TPU:0, one launch (start us, length us, event | category | flops | bytes accessed | tf_op | source)
XLA Modules:
  0.0 147.2 jit_solution(4704566618285670580)
XLA Ops:
  6.5 0.0 copy-start
  6.5 0.0 all-gather.3.cloned.1.call-start
  6.5 0.7 all-gather.3.cloned.1.call-update
  7.3 0.0 all-gather.5.cloned.1.call-start
  7.3 0.7 all-gather.5.cloned.1.call-update
  8.0 0.0 reduce-scatter.2.cloned.1.call-start
  8.1 0.7 reduce
  8.8 0.7 select_reduce_fusion
  9.5 0.0 copy-done
  9.5 7.0 %fusion.4 = f32[384,1024]{1,0:T(8,128)} fusion(bf16[384,4096]{1,0:T(8,128)(2,1)S(1)} %copy-done, bf16[4096,1024]{1,0:T(8,128)(2,1)} %param.9), kind=kOutput, calls=%fused_computation.8 | convolution fusion | flops 3221225472 | bytes 13107200 | tf_op jit(solution)/shard_map/dot_general | solution.py:19
  16.5 69.1 %all-gather.3.cloned.1.call-done = bf16[8,4096,64]{1,2,0:T(8,128)(2,1)} async-done(((bf16[1,4096,64]{1,2,0:T(8,128)(2,1)}), bf16[8,4096,64]{1,2,0:T(8,128)(2,1)}) %all-gather.3.cloned.1.call-update) | async-done | bytes 4194320 | tf_op jit(solution)/shard_map/all_gather | solution.py:21
  85.6 5.4 %fusion.5 = f32[384,512]{0,1} fusion(bf16[384,4096]{1,0:T(8,128)(2,1)S(1)} %copy-done, bf16[4096,512]{0,1:T(8,128)(2,1)} %bitcast.11), kind=kOutput, calls=%fused_computation.9 | convolution fusion | flops 1610612736 | bytes 8126464
  91.0 35.2 %all-gather.5.cloned.1.call-done = bf16[8,64,1024]{2,1,0:T(8,128)(2,1)} async-done(((bf16[1,64,1024]{2,1,0:T(8,128)(2,1)}), bf16[8,64,1024]{2,1,0:T(8,128)(2,1)}) %all-gather.5.cloned.1.call-update) | async-done | bytes 1048592 | tf_op jit(solution)/shard_map/all_gather | solution.py:22
  126.2 4.6 %bitcast_add_fusion = f32[384,1024]{1,0:T(8,128)} fusion(f32[384,1024]{1,0:T(8,128)} %fusion.4, bf16[8,64,1024]{2,1,0:T(8,128)(2,1)} %all-gather.5.cloned.1.call-done, f32[384,8,64]{0,2,1:T(8,128)} %bitcast.12, pred[384,8]{0,1:T(8,128)(4,1)S(1)} %iota_compare_fusion), kind=kOutput, calls=%fused_computation | convolution fusion | flops 2416508928 | bytes 4983808 | tf_op jit(solution)/shard_map/dot_general | solution.py:30
  130.8 0.0 reduce-scatter.2.cloned.1.call-update
  130.8 8.0 %reduce-scatter.2.cloned.1.call-done = f32[384,512]{1,0:T(8,128)} async-done(((f32[384,1024]{1,0:T(8,128)}), f32[384,512]{1,0:T(8,128)}) %reduce-scatter.2.cloned.1.call-update) | async-done | bytes 786448 | tf_op jit(solution)/shard_map/reduce_scatter | solution.py:31
  138.8 1.9 %convert_element_type.4 = bf16[384,512]{1,0:T(8,128)(2,1)} convert(f32[384,512]{1,0:T(8,128)} %reduce-scatter.2.cloned.1.call-done) | non-fusion elementwise | flops 196608 | bytes 1179648 | tf_op jit(solution)/shard_map/convert_element_type | solution.py:33
  (1 shorter events, 0.0 us)
Async XLA Ops:
  6.5 3.0 %copy-start = (bf16[384,4096]{1,0:T(8,128)(2,1)S(1)}, bf16[384,4096]{1,0:T(8,128)(2,1)}, u32[]{:S(2)}) copy-start(bf16[384,4096]{1,0:T(8,128)(2,1)} %param.6) | copy-start | bytes 9437188
  6.5 79.1 %all-gather.3.cloned.1.call-start = ((), (), s32[]{:S(2)}) async-start(), calls=%async_computation.1 | async-start | bytes 4718592 | tf_op jit(solution)/shard_map/all_gather | solution.py:21
  7.3 118.9 %all-gather.5.cloned.1.call-start = ((), (), s32[]{:S(2)}) async-start(), calls=%async_computation.2 | async-start | bytes 1179648 | tf_op jit(solution)/shard_map/all_gather | solution.py:22
  8.0 130.8 %reduce-scatter.2.cloned.1.call-start = ((), (), s32[]{:S(2)}) async-start(), calls=%async_computation.3 | async-start | bytes 2359296 | tf_op jit(solution)/shard_map/reduce_scatter | solution.py:31
Sparse Core Ops, SparseCore 0:
  9.5 76.0 all-gather.2
  87.7 38.4 all-gather.4
  130.9 7.8 reduce-scatter.1
where the time goes:
time: 147 us
  waiting for transfers between devices  114 us (78%)
  matrix products  17 us (12%)
  between operations  13.1 us (9%)
  other arithmetic  3.37 us (2%)
    all_gather x1, waiting for transfers between devices, shards(): a_piece = lax.all_gather(adapter_down_factor, 'dp', axis=0, tiled=True)  69.1 us
    all_gather x1, waiting for transfers between devices, shards(): b_piece = lax.all_gather(adapter_up_factor, 'dp', axis=0, tiled=True)  35.2 us
    reduce_scatter x1, waiting for transfers between devices, shards(): lax.psum_scatter(partial_value + extra, 'tensor', scatter_dimension=1, ti...  7.98 us
    dot_general x1, matrix products, shards(): jnp.dot(requests, key_base_weight, preferred_element_type=jnp.float32)  6.97 us
    unnamed x1, matrix products  5.42 us
    dot_general x1, matrix products, shards(): extra = jnp.dot(weights, b_flat, precision=lax.Precision.HIGHEST)  4.58 us
  transfers between devices with their start and end apart: 3, of which 3 were waited for; matrix products, arithmetic and copies ran while one was open for 9% of the time, Pallas kernels for 0%

commit v1 on v0

v1 whole, which is shorter than its diff:
```python
import jax
import jax.numpy as jnp
from jax import lax
from jax.sharding import PartitionSpec as P

CHUNKS = 2


def ring_of(n):
    if n % 2 == 0 and n <= 16:
        return list(range(0, n, 2)) + list(range(n - 1, 0, -2))
    return list(range(n))


def shards(n, requests, adapter_index, storage_slot_index, key_base_weight, down_factor, up_factor):
    rows, half = requests.shape
    rank = down_factor.shape[2]
    keys = up_factor.shape[2]
    out_keys = keys // 2
    order = ring_of(n)
    place = [order.index(i) for i in range(n)]
    me = lax.axis_index("dp")
    core = lax.axis_index("tensor")

    moves = []
    for j in range(n):
        a, b = order[j], order[(j + 1) % n]
        moves += [(2 * a, 2 * b), (2 * b + 1, 2 * a + 1)]

    table = jnp.arange(storage_slot_index.shape[0], dtype=jnp.int32)
    slot = jnp.sum(
        jnp.where(adapter_index == table[None, :], storage_slot_index[None, :], 0), axis=1, keepdims=True
    )

    a_t = down_factor[0].T
    b_own = lax.dynamic_slice_in_dim(up_factor[0], core * out_keys, out_keys, axis=1)
    own = jnp.concatenate([a_t, b_own], axis=1)
    step_rows = rank // CHUNKS
    held = [[own[c * step_rows : (c + 1) * step_rows] for c in range(CHUNKS)]]
    for _ in range(n - 1):
        held.append([lax.ppermute(h, ("dp", "tensor"), moves) for h in held[-1]])

    w_there = lax.dynamic_slice_in_dim(key_base_weight, (1 - core) * out_keys, out_keys, axis=1)
    w_here = lax.dynamic_slice_in_dim(key_base_weight, core * out_keys, out_keys, axis=1)
    there = jnp.dot(requests, w_there, preferred_element_type=jnp.float32)
    swap = [(0, 1), (1, 0)]
    base = jnp.dot(requests, w_here, preferred_element_type=jnp.float32) + lax.ppermute(there, "tensor", swap)

    pos = jnp.array(place, jnp.int32)[me]
    way = jnp.where(core == 0, -1, 1)
    total = jnp.zeros((rows, rank), jnp.float32)
    origins = []
    for s in range(n):
        origin = jnp.array(order, jnp.int32)[(pos + way * s + n) % n]
        origins.append(origin)
        block = jnp.concatenate([h[:, :half] for h in held[s]], axis=0)
        part = lax.dot_general(
            requests, block, (((1,), (1,)), ((), ())), preferred_element_type=jnp.float32
        )
        total = jnp.where(slot == origin, part, total)
    total = total + lax.ppermute(total, "tensor", swap)

    high = total.astype(jnp.bfloat16)
    rest = total - high.astype(jnp.float32)
    mid = rest.astype(jnp.bfloat16)
    low = (rest - mid.astype(jnp.float32)).astype(jnp.bfloat16)
    b_flat = jnp.concatenate([h[:, half:] for hs in held for h in hs], axis=0)
    lifted = base
    for piece in (low, mid, high):
        wide = jnp.concatenate([jnp.where(slot == o, piece, jnp.bfloat16(0)) for o in origins], axis=1)
        lifted = lifted + jnp.dot(wide, b_flat, preferred_element_type=jnp.float32)
    return lifted.astype(jnp.bfloat16)


def solution(mesh):
    placed = (
        P(("groups", "dp"), "tensor"),
        P(("groups", "dp"), None),
        P("groups"),
        P("tensor", None),
        P(("groups", "dp"), "tensor", None),
        P(("groups", "dp"), None, None),
    )
    n = mesh.shape["dp"]
    return jax.shard_map(
        lambda *a: shards(n, *a),
        mesh=mesh,
        in_specs=placed,
        out_specs=P(("groups", "dp"), "tensor"),
        check_vma=False,
    )
```

time: 147 us -> 83.4 us (0.57)
  waiting for transfers between devices: 114 us -> 20.3 us
  starting transfers between devices: 0.08 us -> 22.6 us
  between operations: 13.1 us -> 5.15 us
  local copies, waits for them, and re-layouts: 0.01 us -> 5.93 us
  matrix products: 17 us -> 21.5 us
  other arithmetic: 3.37 us -> 7.54 us
    all_gather x2 -> x0, waiting for transfers between devices: 104 us -> none  [the longest x1 69.1 us: shards(): a_piece = lax.all_gather(adapter_down_factor, 'dp', axis=0, tiled=True)]
    ppermute x0 -> x16, starting transfers between devices: none -> 22.6 us  [the longest x14 22.5 us: shards(): held.append([lax.ppermute(h, ('dp', 'tensor'), moves) for h in held[-1]])]
    ppermute x0 -> x16, waiting for transfers between devices: none -> 20.3 us  [the longest x14 19 us: shards(): held.append([lax.ppermute(h, ('dp', 'tensor'), moves) for h in held[-1]])]
    dot_general x2 -> x13, matrix products: 11.5 us -> 21.5 us  [the longest x8 9.7 us: shards(): lax.dot_general(requests, block, (((1,), (1,)), ((), ())), preferred_elem...]
    reduce_scatter x1 -> x0, waiting for transfers between devices: 7.98 us -> none  [shards(): lax.psum_scatter(partial_value + extra, 'tensor', scatter_dimension=1, ti...]
    unnamed x1 -> x0, matrix products: 5.42 us -> none
    eq x1, other arithmetic: 0.01 us -> 5.05 us  [shards(): total = jnp.where(slot == origin, part, total)]
    unnamed x2 -> x26, local copies, waits for them, and re-layouts: 0.01 us -> 2.44 us
  transfers between devices with their start and end apart: 3 -> 16, of which waited for: 3 -> 11; matrix products, arithmetic and copies ran while one was open for 9% -> 33% of each run, Pallas kernels for 0% -> 0%
where the time goes in v1:
time: 83.4 us; the launch traced here: 83 us
  starting transfers between devices  22.6 us (27%)
  matrix products  21.5 us (26%)
  waiting for transfers between devices  20.3 us (24%)
  other arithmetic  7.54 us (9%)
  local copies, waits for them, and re-layouts  5.93 us (7%)
  between operations  5.15 us (6%)
    ppermute x14, starting transfers between devices, shards(): held.append([lax.ppermute(h, ('dp', 'tensor'), moves) for h in held[-1]])  22.5 us
    ppermute x14, waiting for transfers between devices, shards(): held.append([lax.ppermute(h, ('dp', 'tensor'), moves) for h in held[-1]])  19 us
    dot_general x8, matrix products, shards(): lax.dot_general(requests, block, (((1,), (1,)), ((), ())), preferred_elem...  9.7 us
    dot_general x1, matrix products, shards(): there = jnp.dot(requests, w_there, preferred_element_type=jnp.float32)  5.49 us
    eq x1, other arithmetic, shards(): total = jnp.where(slot == origin, part, total)  5.05 us
    dot_general x1, matrix products, shards(): jnp.dot(requests, w_here, preferred_element_type=jnp.float32)  4.87 us
    unnamed x26, local copies, waits for them, and re-layouts  2.44 us
    concatenate x1, other arithmetic, shards(): own = jnp.concatenate([a_t, b_own], axis=1)  1.89 us
  transfers between devices with their start and end apart: 16, of which 11 were waited for; matrix products, arithmetic and copies ran while one was open for 33% of the time, Pallas kernels for 0%

profile of v1, /device:TPU:0, one launch (start us, length us, event | category | flops | bytes accessed | tf_op | source)
XLA Modules:
  0.0 83.0 jit_solution(16213343524231447085)
XLA Ops:
  0.0 0.0 copy-start
  0.0 1.6 %constant_dynamic-update-slice_fusion.22 = (bf16[512,512]{1,0:T(8,128)(2,1)}, bf16[64,512]{1,0:T(8,128)(2,1)S(1)}) fusion(bf16[1,64,1024]{2,1,0:T(8,128)(2,1)} %param.20, s32[]{:T(128)S(6)} %select_n.175), kind=kLoop, calls=%fused_computation.76 | loop fusion | bytes 196612
  1.6 1.9 %fusion.43 = (bf16[32,4608]{1,0:T(8,128)(2,1)}, bf16[32,4608]{1,0:T(8,128)(2,1)}) fusion(bf16[64,4096]{1,0:T(8,128)(2,1)} %bitcast.67, bf16[64,512]{1,0:T(8,128)(2,1)S(1)} %get-tuple-element.10), kind=kLoop, calls=%fused_computation.50 | loop fusion | flops 1179648 | bytes 1179648 | tf_op jit(solution)/shard_map/concatenate | solution.py:37
  3.5 3.0 %collective-permute-start.1 = (bf16[32,4608]{1,0:T(8,128)(2,1)}, bf16[32,4608]{1,0:T(8,128)(2,1)}, u32[]{:S(2)}, u32[]{:S(2)}) collective-permute-start(bf16[32,4608]{1,0:T(8,128)(2,1)} %get-tuple-element.13), channel_id=1, source_target_pairs={{0,4},{5,1},{4,8},{9,5},{8,12},{13,9},{12,14},{15,13},{14,10},{11,... | collective-permute-start | bytes 884744 | tf_op jit(solution)/shard_map/ppermute | solution.py:41
  6.5 1.6 %collective-permute-start.8 = (bf16[32,4608]{1,0:T(8,128)(2,1)}, bf16[32,4608]{1,0:T(8,128)(2,1)S(1)}, u32[]{:S(2)}, u32[]{:S(2)}) collective-permute-start(bf16[32,4608]{1,0:T(8,128)(2,1)} %get-tuple-element.14), channel_id=1, source_target_pairs={{0,4},{5,1},{4,8},{9,5},{8,12},{13,9},{12,14},{15,13},{14,10},{11,... | collective-permute-start | bytes 884744 | tf_op jit(solution)/shard_map/ppermute | solution.py:41
  8.1 0.0 copy-done
  8.1 0.0 copy-start.2
  8.1 5.5 %fusion.7 = f32[384,512]{0,1:T(8,128)} fusion(bf16[384,4096]{1,0:T(8,128)(2,1)S(1)} %copy-done, bf16[4096,1024]{1,0:T(8,128)(2,1)} %param.18, s32[]{:T(128)S(6)} %select_n.176), kind=kOutput, calls=%fused_computation.8 | convolution fusion | flops 1610612736 | bytes 8126468 | tf_op jit(solution)/shard_map/dot_general | solution.py:45
  13.6 0.0 collective-permute-start
  13.6 0.0 copy-done.5
  13.6 0.6 dynamic_slice.40
  19.0 0.0 copy-done.3
  19.0 0.0 copy-done.4
  19.0 0.1 select_reduce_fusion
  19.1 0.0 copy-done.2
  19.1 0.7 fusion.55
  19.8 5.1 %broadcast_compare_fusion.6 = (pred[384]{0:T(512)(128)(4,1)S(1)}, pred[384]{0:T(512)(128)(4,1)S(1)}, pred[384]{0:T(512)(128)(4,1)S(1)}, pred[384]{0:T(512)(128)(...) fusion(s32[384]{0:T(512)S(1)} %select_reduce_fusion, ...), kind=kLoop, calls=%fused_computation.103 | loop fusion | flops 3072 | bytes 4640 | tf_op jit(solution)/shard_map/eq | solution.py:60
  24.9 2.1 %convolution_select_fusion = f32[384,64]{0,1:T(8,128)S(1)} fusion(bf16[384,4096]{1,0:T(8,128)(2,1)S(1)} %copy-done, bf16[1,4096,64]{1,2,0:T(8,128)(2,1)} %param.19, pred[384]{0:T(512)(128)(4,1)S(1)} %get-tuple-element.25), kind=kOutput, calls=%fused_computation.25 | convolution fusion | flops 201351168 | bytes 3768704 | tf_op jit(solution)/shard_map/dot_general | solution.py:57
  27.0 0.0 copy-start.1
  27.0 0.0 collective-permute-done.1
  27.0 1.0 %slice.144 = bf16[32,4096]{1,0:T(8,128)(2,1)S(1)} slice(bf16[32,4608]{1,0:T(8,128)(2,1)} %collective-permute-done.1), slice={[0:32], [0:4096]} | slice | bytes 524288 | tf_op jit(solution)/shard_map/slice | solution.py:56
  28.1 0.0 collective-permute-done.8
  28.1 1.1 %fusion.20 = f32[384,64]{0,1:T(8,128)S(1)} fusion(f32[384,64]{0,1:T(8,128)S(1)} %convolution_select_fusion, bf16[384,4096]{1,0:T(8,128)(2,1)S(1)} %copy-done, bf16[32,4096]{1,0:T(8,128)(2,1)S(1)} %slice.145, bf16[32,4096]{1,0:T(8,128)(2,1)S(1)} %slice.144, pred[384]{0:T(512)(128)(4,1)S(1)} %get-tuple-element.19), kind=kOutput, calls=%fused_computation.24 | convolution fusion | flops 202399744 | bytes 3867008 | tf_op jit(solution)/shard_map/dot_general | solution.py:57
  29.2 1.6 %collective-permute-start.2 = (bf16[32,4608]{1,0:T(8,128)(2,1)}, bf16[32,4608]{1,0:T(8,128)(2,1)S(1)}, u32[]{:S(2)}, u32[]{:S(2)}) collective-permute-start(bf16[32,4608]{1,0:T(8,128)(2,1)} %collective-permute-done.1), channel_id=1, source_target_pairs={{0,4},{5,1},{4,8},{9,5},{8,12},{13,9},{12,14},{15,13},{14,10},{11,... | collective-permute-start | bytes 884744 | tf_op jit(solution)/shard_map/ppermute | solution.py:41
  30.8 1.5 %collective-permute-start.9 = (bf16[32,4608]{1,0:T(8,128)(2,1)S(1)}, bf16[32,4608]{1,0:T(8,128)(2,1)S(1)}, u32[]{:S(2)}, u32[]{:S(2)}) collective-permute-start(bf16[32,4608]{1,0:T(8,128)(2,1)S(1)} %collective-permute-done.8), channel_id=1, source_target_pairs={{0,4},{5,1},{4,8},{9,5},{8,12},{13,9},{12,14},{15,13},{14,10},{11,... | collective-permute-start | bytes 884744 | tf_op jit(solution)/shard_map/ppermute | solution.py:41
  32.3 0.0 copy-done.1
  32.3 0.8 constant_dynamic-update-slice_fusion.21
  33.1 3.1 %collective-permute-done.2 = bf16[32,4608]{1,0:T(8,128)(2,1)S(1)} collective-permute-done((bf16[32,4608]{1,0:T(8,128)(2,1)}, bf16[32,4608]{1,0:T(8,128)(2,1)S(1)}, u32[]{:S(2)}, u32[]{:S(2)}) %collective-permute-start.2) | collective-permute-done | bytes 294944 | tf_op jit(solution)/shard_map/ppermute | solution.py:41
  36.2 1.6 %collective-permute-start.3 = (bf16[32,4608]{1,0:T(8,128)(2,1)S(1)}, bf16[32,4608]{1,0:T(8,128)(2,1)S(1)}, u32[]{:S(2)}, u32[]{:S(2)}) collective-permute-start(bf16[32,4608]{1,0:T(8,128)(2,1)S(1)} %collective-permute-done.2), channel_id=1, source_target_pairs={{0,4},{5,1},{4,8},{9,5},{8,12},{13,9},{12,14},{15,13},{14,10},{11,... | collective-permute-start | bytes 884744 | tf_op jit(solution)/shard_map/ppermute | solution.py:41
  37.8 1.5 %collective-permute-done.9 = bf16[32,4608]{1,0:T(8,128)(2,1)S(1)} collective-permute-done((bf16[32,4608]{1,0:T(8,128)(2,1)S(1)}, bf16[32,4608]{1,0:T(8,128)(2,1)S(1)}, u32[]{:S(2)}, u32[]{:S(2)}) %collective-permute-start.9) | collective-permute-done | bytes 294944 | tf_op jit(solution)/shard_map/ppermute | solution.py:41
  39.4 1.6 %collective-permute-start.10 = (bf16[32,4608]{1,0:T(8,128)(2,1)S(1)}, bf16[32,4608]{1,0:T(8,128)(2,1)S(1)}, u32[]{:S(2)}, u32[]{:S(2)}) collective-permute-start(bf16[32,4608]{1,0:T(8,128)(2,1)S(1)} %collective-permute-done.9), channel_id=1, source_target_pairs={{0,4},{5,1},{4,8},{9,5},{8,12},{13,9},{12,14},{15,13},{14,10},{11,... | collective-permute-start | bytes 884744 | tf_op jit(solution)/shard_map/ppermute | solution.py:41
  41.0 1.1 %fusion.19 = f32[384,64]{0,1:T(8,128)S(1)} fusion(f32[384,64]{0,1:T(8,128)S(1)} %fusion.20, bf16[384,4096]{1,0:T(8,128)(2,1)S(1)} %copy-done, bf16[32,4096]{1,0:T(8,128)(2,1)S(1)} %slice.143, bf16[32,4096]{1,0:T(8,128)(2,1)S(1)} %slice.142, pred[384]{0:T(512)(128)(4,1)S(1)} %get-tuple-element.20), kind=kOutput, calls=%fused_computation.23 | convolution fusion | flops 202399744 | bytes 3867008 | tf_op jit(solution)/shard_map/dot_general | solution.py:57
  42.1 0.0 collective-permute-done
  42.1 4.9 %fusion.10 = f32[384,512]{0,1:T(8,128)S(1)} fusion(f32[384,512]{0,1:T(8,128)} %collective-permute-done, bf16[384,4096]{1,0:T(8,128)(2,1)S(1)} %copy-done, bf16[4096,1024]{1,0:T(8,128)(2,1)} %param.18, s32[]{:T(128)S(6)} %select_n.175), kind=kOutput, calls=%fused_computation.9 | convolution fusion | flops 1610809344 | bytes 8912900 | tf_op jit(solution)/shard_map/dot_general | solution.py:47
  47.0 0.0 collective-permute-done.3
  47.0 1.5 %collective-permute-start.4 = (bf16[32,4608]{1,0:T(8,128)(2,1)S(1)}, bf16[32,4608]{1,0:T(8,128)(2,1)S(1)}, u32[]{:S(2)}, u32[]{:S(2)}) collective-permute-start(bf16[32,4608]{1,0:T(8,128)(2,1)S(1)} %collective-permute-done.3), channel_id=1, source_target_pairs={{0,4},{5,1},{4,8},{9,5},{8,12},{13,9},{12,14},{15,13},{14,10},{11,... | collective-permute-start | bytes 884744 | tf_op jit(solution)/shard_map/ppermute | solution.py:41
  48.6 0.0 collective-permute-done.10
  48.6 0.5 collective-permute-start.11
  49.1 1.1 %fusion.18 = f32[384,64]{0,1:T(8,128)S(1)} fusion(f32[384,64]{0,1:T(8,128)S(1)} %fusion.19, bf16[384,4096]{1,0:T(8,128)(2,1)S(1)} %copy-done, bf16[32,4096]{1,0:T(8,128)(2,1)S(1)} %slice.141, bf16[32,4096]{1,0:T(8,128)(2,1)S(1)} %slice.140, pred[384]{0:T(512)(128)(4,1)S(1)} %get-tuple-element.21), kind=kOutput, calls=%fused_computation.22 | convolution fusion | flops 202399744 | bytes 3867008 | tf_op jit(solution)/shard_map/dot_general | solution.py:57
  50.2 3.6 %collective-permute-done.4 = bf16[32,4608]{1,0:T(8,128)(2,1)S(1)} collective-permute-done((bf16[32,4608]{1,0:T(8,128)(2,1)S(1)}, bf16[32,4608]{1,0:T(8,128)(2,1)S(1)}, u32[]{:S(2)}, u32[]{:S(2)}) %collective-permute-start.4) | collective-permute-done | bytes 294944 | tf_op jit(solution)/shard_map/ppermute | solution.py:41
  53.8 1.5 %collective-permute-start.5 = (bf16[32,4608]{1,0:T(8,128)(2,1)S(1)}, bf16[32,4608]{1,0:T(8,128)(2,1)S(1)}, u32[]{:S(2)}, u32[]{:S(2)}) collective-permute-start(bf16[32,4608]{1,0:T(8,128)(2,1)S(1)} %collective-permute-done.4), channel_id=1, source_target_pairs={{0,4},{5,1},{4,8},{9,5},{8,12},{13,9},{12,14},{15,13},{14,10},{11,... | collective-permute-start | bytes 884744 | tf_op jit(solution)/shard_map/ppermute | solution.py:41
  55.4 1.6 %collective-permute-done.11 = bf16[32,4608]{1,0:T(8,128)(2,1)S(1)} collective-permute-done((bf16[32,4608]{1,0:T(8,128)(2,1)S(1)}, bf16[32,4608]{1,0:T(8,128)(2,1)S(1)}, u32[]{:S(2)}, u32[]{:S(2)}) %collective-permute-start.11) | collective-permute-done | bytes 294944 | tf_op jit(solution)/shard_map/ppermute | solution.py:41
  57.0 1.5 %collective-permute-start.12 = (bf16[32,4608]{1,0:T(8,128)(2,1)S(1)}, bf16[32,4608]{1,0:T(8,128)(2,1)S(1)}, u32[]{:S(2)}, u32[]{:S(2)}) collective-permute-start(bf16[32,4608]{1,0:T(8,128)(2,1)S(1)} %collective-permute-done.11), channel_id=1, source_target_pairs={{0,4},{5,1},{4,8},{9,5},{8,12},{13,9},{12,14},{15,13},{14,10},{11,... | collective-permute-start | bytes 884744 | tf_op jit(solution)/shard_map/ppermute | solution.py:41
  58.5 1.1 %fusion.17 = f32[384,64]{0,1:T(8,128)S(1)} fusion(f32[384,64]{0,1:T(8,128)S(1)} %fusion.18, bf16[384,4096]{1,0:T(8,128)(2,1)S(1)} %copy-done, bf16[32,4096]{1,0:T(8,128)(2,1)S(1)} %slice.139, bf16[32,4096]{1,0:T(8,128)(2,1)S(1)} %slice.138, pred[384]{0:T(512)(128)(4,1)S(1)} %get-tuple-element.22), kind=kOutput, calls=%fused_computation.21 | convolution fusion | flops 202399744 | bytes 3867008 | tf_op jit(solution)/shard_map/dot_general | solution.py:57
  59.6 1.0 %collective-permute-done.5 = bf16[32,4608]{1,0:T(8,128)(2,1)S(1)} collective-permute-done((bf16[32,4608]{1,0:T(8,128)(2,1)S(1)}, bf16[32,4608]{1,0:T(8,128)(2,1)S(1)}, u32[]{:S(2)}, u32[]{:S(2)}) %collective-permute-start.5) | collective-permute-done | bytes 294944 | tf_op jit(solution)/shard_map/ppermute | solution.py:41
  60.6 1.5 %collective-permute-start.6 = (bf16[32,4608]{1,0:T(8,128)(2,1)S(1)}, bf16[32,4608]{1,0:T(8,128)(2,1)S(1)}, u32[]{:S(2)}, u32[]{:S(2)}) collective-permute-start(bf16[32,4608]{1,0:T(8,128)(2,1)S(1)} %collective-permute-done.5), channel_id=1, source_target_pairs={{0,4},{5,1},{4,8},{9,5},{8,12},{13,9},{12,14},{15,13},{14,10},{11,... | collective-permute-start | bytes 884744 | tf_op jit(solution)/shard_map/ppermute | solution.py:41
  62.1 1.6 %collective-permute-done.12 = bf16[32,4608]{1,0:T(8,128)(2,1)S(1)} collective-permute-done((bf16[32,4608]{1,0:T(8,128)(2,1)S(1)}, bf16[32,4608]{1,0:T(8,128)(2,1)S(1)}, u32[]{:S(2)}, u32[]{:S(2)}) %collective-permute-start.12) | collective-permute-done | bytes 294944 | tf_op jit(solution)/shard_map/ppermute | solution.py:41
  63.8 1.5 %collective-permute-start.13 = (bf16[32,4608]{1,0:T(8,128)(2,1)S(1)}, bf16[32,4608]{1,0:T(8,128)(2,1)S(1)}, u32[]{:S(2)}, u32[]{:S(2)}) collective-permute-start(bf16[32,4608]{1,0:T(8,128)(2,1)S(1)} %collective-permute-done.12), channel_id=1, source_target_pairs={{0,4},{5,1},{4,8},{9,5},{8,12},{13,9},{12,14},{15,13},{14,10},{11,... | collective-permute-start | bytes 884744 | tf_op jit(solution)/shard_map/ppermute | solution.py:41
  65.3 1.1 %fusion.16 = f32[384,64]{0,1:T(8,128)S(1)} fusion(f32[384,64]{0,1:T(8,128)S(1)} %fusion.17, bf16[384,4096]{1,0:T(8,128)(2,1)S(1)} %copy-done, bf16[32,4096]{1,0:T(8,128)(2,1)S(1)} %slice.137, bf16[32,4096]{1,0:T(8,128)(2,1)S(1)} %slice.136, pred[384]{0:T(512)(128)(4,1)S(1)} %get-tuple-element.23), kind=kOutput, calls=%fused_computation.20 | convolution fusion | flops 202399744 | bytes 3867008 | tf_op jit(solution)/shard_map/dot_general | solution.py:57
  66.4 1.0 %collective-permute-done.6 = bf16[32,4608]{1,0:T(8,128)(2,1)S(1)} collective-permute-done((bf16[32,4608]{1,0:T(8,128)(2,1)S(1)}, bf16[32,4608]{1,0:T(8,128)(2,1)S(1)}, u32[]{:S(2)}, u32[]{:S(2)}) %collective-permute-start.6) | collective-permute-done | bytes 294944 | tf_op jit(solution)/shard_map/ppermute | solution.py:41
  67.4 1.5 %collective-permute-start.7 = (bf16[32,4608]{1,0:T(8,128)(2,1)S(1)}, bf16[32,4608]{1,0:T(8,128)(2,1)S(1)}, u32[]{:S(2)}, u32[]{:S(2)}) collective-permute-start(bf16[32,4608]{1,0:T(8,128)(2,1)S(1)} %collective-permute-done.6), channel_id=1, source_target_pairs={{0,4},{5,1},{4,8},{9,5},{8,12},{13,9},{12,14},{15,13},{14,10},{11,... | collective-permute-start | bytes 884744 | tf_op jit(solution)/shard_map/ppermute | solution.py:41
  68.9 1.6 %collective-permute-done.13 = bf16[32,4608]{1,0:T(8,128)(2,1)S(1)} collective-permute-done((bf16[32,4608]{1,0:T(8,128)(2,1)S(1)}, bf16[32,4608]{1,0:T(8,128)(2,1)S(1)}, u32[]{:S(2)}, u32[]{:S(2)}) %collective-permute-start.13) | collective-permute-done | bytes 294944 | tf_op jit(solution)/shard_map/ppermute | solution.py:41
  70.6 1.7 %collective-permute-start.14 = (bf16[32,4608]{1,0:T(8,128)(2,1)S(1)}, bf16[32,4608]{1,0:T(8,128)(2,1)S(1)}, u32[]{:S(2)}, u32[]{:S(2)}) collective-permute-start(bf16[32,4608]{1,0:T(8,128)(2,1)S(1)} %collective-permute-done.13), channel_id=1, source_target_pairs={{0,4},{5,1},{4,8},{9,5},{8,12},{13,9},{12,14},{15,13},{14,10},{11,... | collective-permute-start | bytes 884744 | tf_op jit(solution)/shard_map/ppermute | solution.py:41
  72.3 1.1 %fusion.15 = f32[384,64]{0,1:T(8,128)S(1)} fusion(f32[384,64]{0,1:T(8,128)S(1)} %fusion.16, bf16[384,4096]{1,0:T(8,128)(2,1)S(1)} %copy-done, bf16[32,4096]{1,0:T(8,128)(2,1)S(1)} %slice.135, bf16[32,4096]{1,0:T(8,128)(2,1)S(1)} %slice.134, pred[384]{0:T(512)(128)(4,1)S(1)} %get-tuple-element.24), kind=kOutput, calls=%fused_computation.19 | convolution fusion | flops 202399744 | bytes 3867008 | tf_op jit(solution)/shard_map/dot_general | solution.py:57
  73.4 0.8 collective-permute-done.7
  74.2 3.3 %collective-permute-done.14 = bf16[32,4608]{1,0:T(8,128)(2,1)S(1)} collective-permute-done((bf16[32,4608]{1,0:T(8,128)(2,1)S(1)}, bf16[32,4608]{1,0:T(8,128)(2,1)S(1)}, u32[]{:S(2)}, u32[]{:S(2)}) %collective-permute-start.14) | collective-permute-done | bytes 294944 | tf_op jit(solution)/shard_map/ppermute | solution.py:41
  77.5 1.1 %fusion.14 = f32[384,64]{0,1:T(8,128)S(1)} fusion(f32[384,64]{0,1:T(8,128)S(1)} %fusion.15, bf16[384,4096]{1,0:T(8,128)(2,1)S(1)} %copy-done, bf16[32,4096]{1,0:T(8,128)(2,1)S(1)} %slice.133, bf16[32,4096]{1,0:T(8,128)(2,1)S(1)} %slice.132, pred[384]{0:T(512)(128)(4,1)S(1)} %get-tuple-element.18), kind=kOutput, calls=%fused_computation.18 | convolution fusion | flops 202399744 | bytes 3867008 | tf_op jit(solution)/shard_map/dot_general | solution.py:57
  78.6 0.1 collective-permute-start.15
  78.7 1.3 %collective-permute-done.15 = f32[384,64]{0,1:T(8,128)S(1)} collective-permute-done((f32[384,64]{0,1:T(8,128)S(1)}, f32[384,64]{0,1:T(8,128)S(1)}, u32[]{:S(2)}, u32[]{:S(2)}) %collective-permute-start.15) | collective-permute-done | bytes 98336 | tf_op jit(solution)/shard_map/ppermute | solution.py:61
  80.3 0.1 constant_dynamic-update-slice_fusion.7
  80.6 0.5 convolution_add_fusion.2
  81.1 0.5 convolution_add_fusion.1
  81.6 0.5 fusion.13
  82.1 0.9 %copy.23 = bf16[384,512]{1,0:T(8,128)(2,1)} copy(bf16[384,512]{0,1:T(8,128)(2,1)S(1)} %fusion.13) | data formatting | bytes 786432 | tf_op jit(solution)/shard_map/convert_element_type | solution.py:72
  (50 shorter events, 0.7 us)
Async XLA Ops:
  0.0 8.1 %copy-start = (bf16[384,4096]{1,0:T(8,128)(2,1)S(1)}, bf16[384,4096]{1,0:T(8,128)(2,1)}, u32[]{:S(2)}) copy-start(bf16[384,4096]{1,0:T(8,128)(2,1)} %param.15) | copy-start | bytes 9437188
  3.5 23.5 %collective-permute-start.1 = (bf16[32,4608]{1,0:T(8,128)(2,1)}, bf16[32,4608]{1,0:T(8,128)(2,1)}, u32[]{:S(2)}, u32[]{:S(2)}) collective-permute-start(bf16[32,4608]{1,0:T(8,128)(2,1)} %get-tuple-element.13), channel_id=1, source_target_pairs={{0,4},{5,1},{4,8},{9,5},{8,12},{13,9},{12,14},{15,13},{14,10},{11,... | collective-permute-start | bytes 884744 | tf_op jit(solution)/shard_map/ppermute | solution.py:41
  6.5 21.5 %collective-permute-start.8 = (bf16[32,4608]{1,0:T(8,128)(2,1)}, bf16[32,4608]{1,0:T(8,128)(2,1)S(1)}, u32[]{:S(2)}, u32[]{:S(2)}) collective-permute-start(bf16[32,4608]{1,0:T(8,128)(2,1)} %get-tuple-element.14), channel_id=1, source_target_pairs={{0,4},{5,1},{4,8},{9,5},{8,12},{13,9},{12,14},{15,13},{14,10},{11,... | collective-permute-start | bytes 884744 | tf_op jit(solution)/shard_map/ppermute | solution.py:41
  8.1 5.5 %copy-start.5 = (s32[8]{0:T(128)S(1)}, s32[8]{0:T(128)}, u32[]{:S(2)}) copy-start(s32[8]{0:T(128)} %constant.78.clone) | copy-start | bytes 100
  8.1 10.8 %copy-start.3 = (s32[384,1]{0,1:T(1,128)S(1)}, s32[384,1]{0,1:T(1,128)}, u32[]{:S(2)}) copy-start(s32[384,1]{0,1:T(1,128)} %param.16) | copy-start | bytes 4612
  8.1 10.9 %copy-start.4 = (s32[8]{0:T(128)S(1)}, s32[8]{0:T(128)}, u32[]{:S(2)}) copy-start(s32[8]{0:T(128)} %param.17) | copy-start | bytes 100
  8.1 11.0 %copy-start.2 = (s32[8]{0:T(128)S(1)}, s32[8]{0:T(128)}, u32[]{:S(2)}) copy-start(s32[8]{0:T(128)} %constant.79.clone) | copy-start | bytes 100
  13.6 28.5 %collective-permute-start = (f32[384,512]{0,1:T(8,128)}, f32[384,512]{0,1:T(8,128)}, u32[]{:S(2)}, u32[]{:S(2)}) collective-permute-start(f32[384,512]{0,1:T(8,128)} %fusion.7), channel_id=1, source_target_pairs={{0,1},{1,0},{2,3},{3,2},{4,5},{5,4},{6,7},{7,6},{8,9},{9,8},{10,11... | collective-permute-start | bytes 2359304 | tf_op jit(solution)/shard_map/ppermute | solution.py:47
  27.0 5.3 %copy-start.1 = (bf16[512,512]{1,0:T(8,128)(2,1)S(1)}, bf16[512,512]{1,0:T(8,128)(2,1)}, u32[]{:S(2)}) copy-start(bf16[512,512]{1,0:T(8,128)(2,1)} %get-tuple-element.9) | copy-start | bytes 1572868
  29.2 7.0 %collective-permute-start.2 = (bf16[32,4608]{1,0:T(8,128)(2,1)}, bf16[32,4608]{1,0:T(8,128)(2,1)S(1)}, u32[]{:S(2)}, u32[]{:S(2)}) collective-permute-start(bf16[32,4608]{1,0:T(8,128)(2,1)} %collective-permute-done.1), channel_id=1, source_target_pairs={{0,4},{5,1},{4,8},{9,5},{8,12},{13,9},{12,14},{15,13},{14,10},{11,... | collective-permute-start | bytes 884744 | tf_op jit(solution)/shard_map/ppermute | solution.py:41
  30.8 8.5 %collective-permute-start.9 = (bf16[32,4608]{1,0:T(8,128)(2,1)S(1)}, bf16[32,4608]{1,0:T(8,128)(2,1)S(1)}, u32[]{:S(2)}, u32[]{:S(2)}) collective-permute-start(bf16[32,4608]{1,0:T(8,128)(2,1)S(1)} %collective-permute-done.8), channel_id=1, source_target_pairs={{0,4},{5,1},{4,8},{9,5},{8,12},{13,9},{12,14},{15,13},{14,10},{11,... | collective-permute-start | bytes 884744 | tf_op jit(solution)/shard_map/ppermute | solution.py:41
  36.2 10.8 %collective-permute-start.3 = (bf16[32,4608]{1,0:T(8,128)(2,1)S(1)}, bf16[32,4608]{1,0:T(8,128)(2,1)S(1)}, u32[]{:S(2)}, u32[]{:S(2)}) collective-permute-start(bf16[32,4608]{1,0:T(8,128)(2,1)S(1)} %collective-permute-done.2), channel_id=1, source_target_pairs={{0,4},{5,1},{4,8},{9,5},{8,12},{13,9},{12,14},{15,13},{14,10},{11,... | collective-permute-start | bytes 884744 | tf_op jit(solution)/shard_map/ppermute | solution.py:41
  39.4 9.2 %collective-permute-start.10 = (bf16[32,4608]{1,0:T(8,128)(2,1)S(1)}, bf16[32,4608]{1,0:T(8,128)(2,1)S(1)}, u32[]{:S(2)}, u32[]{:S(2)}) collective-permute-start(bf16[32,4608]{1,0:T(8,128)(2,1)S(1)} %collective-permute-done.9), channel_id=1, source_target_pairs={{0,4},{5,1},{4,8},{9,5},{8,12},{13,9},{12,14},{15,13},{14,10},{11,... | collective-permute-start | bytes 884744 | tf_op jit(solution)/shard_map/ppermute | solution.py:41
  47.0 6.8 %collective-permute-start.4 = (bf16[32,4608]{1,0:T(8,128)(2,1)S(1)}, bf16[32,4608]{1,0:T(8,128)(2,1)S(1)}, u32[]{:S(2)}, u32[]{:S(2)}) collective-permute-start(bf16[32,4608]{1,0:T(8,128)(2,1)S(1)} %collective-permute-done.3), channel_id=1, source_target_pairs={{0,4},{5,1},{4,8},{9,5},{8,12},{13,9},{12,14},{15,13},{14,10},{11,... | collective-permute-start | bytes 884744 | tf_op jit(solution)/shard_map/ppermute | solution.py:41
  48.6 8.4 %collective-permute-start.11 = (bf16[32,4608]{1,0:T(8,128)(2,1)S(1)}, bf16[32,4608]{1,0:T(8,128)(2,1)S(1)}, u32[]{:S(2)}, u32[]{:S(2)}) collective-permute-start(bf16[32,4608]{1,0:T(8,128)(2,1)S(1)} %collective-permute-done.10), channel_id=1, source_target_pairs={{0,4},{5,1},{4,8},{9,5},{8,12},{13,9},{12,14},{15,13},{14,10},{11,... | collective-permute-start | bytes 884744 | tf_op jit(solution)/shard_map/ppermute | solution.py:41
  53.8 6.8 %collective-permute-start.5 = (bf16[32,4608]{1,0:T(8,128)(2,1)S(1)}, bf16[32,4608]{1,0:T(8,128)(2,1)S(1)}, u32[]{:S(2)}, u32[]{:S(2)}) collective-permute-start(bf16[32,4608]{1,0:T(8,128)(2,1)S(1)} %collective-permute-done.4), channel_id=1, source_target_pairs={{0,4},{5,1},{4,8},{9,5},{8,12},{13,9},{12,14},{15,13},{14,10},{11,... | collective-permute-start | bytes 884744 | tf_op jit(solution)/shard_map/ppermute | solution.py:41
  57.0 6.8 %collective-permute-start.12 = (bf16[32,4608]{1,0:T(8,128)(2,1)S(1)}, bf16[32,4608]{1,0:T(8,128)(2,1)S(1)}, u32[]{:S(2)}, u32[]{:S(2)}) collective-permute-start(bf16[32,4608]{1,0:T(8,128)(2,1)S(1)} %collective-permute-done.11), channel_id=1, source_target_pairs={{0,4},{5,1},{4,8},{9,5},{8,12},{13,9},{12,14},{15,13},{14,10},{11,... | collective-permute-start | bytes 884744 | tf_op jit(solution)/shard_map/ppermute | solution.py:41
  60.6 6.8 %collective-permute-start.6 = (bf16[32,4608]{1,0:T(8,128)(2,1)S(1)}, bf16[32,4608]{1,0:T(8,128)(2,1)S(1)}, u32[]{:S(2)}, u32[]{:S(2)}) collective-permute-start(bf16[32,4608]{1,0:T(8,128)(2,1)S(1)} %collective-permute-done.5), channel_id=1, source_target_pairs={{0,4},{5,1},{4,8},{9,5},{8,12},{13,9},{12,14},{15,13},{14,10},{11,... | collective-permute-start | bytes 884744 | tf_op jit(solution)/shard_map/ppermute | solution.py:41
  63.8 6.8 %collective-permute-start.13 = (bf16[32,4608]{1,0:T(8,128)(2,1)S(1)}, bf16[32,4608]{1,0:T(8,128)(2,1)S(1)}, u32[]{:S(2)}, u32[]{:S(2)}) collective-permute-start(bf16[32,4608]{1,0:T(8,128)(2,1)S(1)} %collective-permute-done.12), channel_id=1, source_target_pairs={{0,4},{5,1},{4,8},{9,5},{8,12},{13,9},{12,14},{15,13},{14,10},{11,... | collective-permute-start | bytes 884744 | tf_op jit(solution)/shard_map/ppermute | solution.py:41
  67.4 6.8 %collective-permute-start.7 = (bf16[32,4608]{1,0:T(8,128)(2,1)S(1)}, bf16[32,4608]{1,0:T(8,128)(2,1)S(1)}, u32[]{:S(2)}, u32[]{:S(2)}) collective-permute-start(bf16[32,4608]{1,0:T(8,128)(2,1)S(1)} %collective-permute-done.6), channel_id=1, source_target_pairs={{0,4},{5,1},{4,8},{9,5},{8,12},{13,9},{12,14},{15,13},{14,10},{11,... | collective-permute-start | bytes 884744 | tf_op jit(solution)/shard_map/ppermute | solution.py:41
  70.6 7.0 %collective-permute-start.14 = (bf16[32,4608]{1,0:T(8,128)(2,1)S(1)}, bf16[32,4608]{1,0:T(8,128)(2,1)S(1)}, u32[]{:S(2)}, u32[]{:S(2)}) collective-permute-start(bf16[32,4608]{1,0:T(8,128)(2,1)S(1)} %collective-permute-done.13), channel_id=1, source_target_pairs={{0,4},{5,1},{4,8},{9,5},{8,12},{13,9},{12,14},{15,13},{14,10},{11,... | collective-permute-start | bytes 884744 | tf_op jit(solution)/shard_map/ppermute | solution.py:41
  78.6 1.4 %collective-permute-start.15 = (f32[384,64]{0,1:T(8,128)S(1)}, f32[384,64]{0,1:T(8,128)S(1)}, u32[]{:S(2)}, u32[]{:S(2)}) collective-permute-start(f32[384,64]{0,1:T(8,128)S(1)} %fusion.14), channel_id=1, source_target_pairs={{0,1},{1,0},{2,3},{3,2},{4,5},{5,4},{6,7},{7,6},{8,9},{9,8},{10,11... | collective-permute-start | bytes 294920 | tf_op jit(solution)/shard_map/ppermute | solution.py:61

commit v2 on v1

v2 whole, which is shorter than its diff:
```python
import jax
import jax.numpy as jnp
from jax import lax
from jax.sharding import PartitionSpec as P


def ring_of(n):
    if n % 2 == 0 and n <= 16:
        return list(range(0, n, 2)) + list(range(n - 1, 0, -2))
    return list(range(n))


def shards(n, requests, adapter_index, storage_slot_index, key_base_weight, down_factor, up_factor):
    rows, half = requests.shape
    rank = down_factor.shape[2]
    keys = up_factor.shape[2]
    out_keys = keys // 2
    order = ring_of(n)
    place = [order.index(i) for i in range(n)]
    me = lax.axis_index("dp")
    core = lax.axis_index("tensor")

    forth, back = [], []
    for j in range(n):
        a, b = order[j], order[(j + 1) % n]
        forth += [(2 * a, 2 * b), (2 * b + 1, 2 * a + 1)]
        back += [(2 * b, 2 * a), (2 * a + 1, 2 * b + 1)]
    swap = [(0, 1), (1, 0)]

    steps = [[(place[d] - place[s]) * (1 - 2 * c) % n for s in range(n)] for d in range(n) for c in range(2)]
    steps_here = lax.dynamic_index_in_dim(jnp.array(steps, jnp.int32), 2 * me + core, 0, keepdims=False)
    slots = jnp.arange(n, dtype=jnp.int32)
    steps_of = jnp.sum(jnp.where(storage_slot_index[:, None] == slots[None, :], steps_here[None, :], 0), axis=1)
    far = jnp.sum(jnp.where(adapter_index == slots[None, :], steps_of[None, :], 0), axis=1)

    a_t = down_factor[0].T
    b_own = lax.dynamic_slice_in_dim(up_factor[0], core * out_keys, out_keys, axis=1)
    own = jnp.concatenate([a_t, b_own], axis=1)

    w_there = lax.dynamic_slice_in_dim(key_base_weight, (1 - core) * out_keys, out_keys, axis=1)
    w_here = lax.dynamic_slice_in_dim(key_base_weight, core * out_keys, out_keys, axis=1)
    there = jnp.dot(requests, w_there, preferred_element_type=jnp.float32)
    there, own_late = lax.optimization_barrier((there, own))
    here = jnp.dot(requests, w_here, preferred_element_type=jnp.float32)

    pieces = [(0, 0, own)]
    p, q = own, own_late
    for s in range(1, (n - 1) // 2 + 1):
        p = lax.ppermute(p, ("dp", "tensor"), forth)
        q = lax.ppermute(q, ("dp", "tensor"), back)
        if s == 1:
            here, p = lax.optimization_barrier((here, p))
        pieces += [(s, 0, p), (n - s, 0, q)]
    if n % 2 == 0:
        mid = rank // 2
        pieces += [
            (n // 2, 0, lax.ppermute(p[:mid], ("dp", "tensor"), forth)),
            (n // 2, mid, lax.ppermute(q[mid:], ("dp", "tensor"), back)),
        ]

    base = here + lax.ppermute(there, "tensor", swap)

    total = jnp.zeros((rank, rows), jnp.float32)
    for s, first, piece in pieces:
        last = first + piece.shape[0]
        part = lax.dot_general(
            piece[:, :half], requests, (((1,), (1,)), ((), ())), preferred_element_type=jnp.float32
        )
        part = jnp.where((far == s)[None, :], part, total[first:last])
        total = part if first == 0 and last == rank else total.at[first:last].set(part)
    total = total + lax.ppermute(total, "tensor", swap)

    rounded = lax.reduce_precision(total, exponent_bits=8, mantissa_bits=7)
    high = rounded.astype(jnp.bfloat16)
    low = (total - rounded).astype(jnp.bfloat16)
    b_flat = jnp.concatenate([piece[:, half:] for _, _, piece in pieces], axis=0)
    lifted = base
    for part in (low, high):
        wide = jnp.concatenate(
            [
                jnp.where((far == s)[None, :], part[f : f + h.shape[0]], jnp.bfloat16(0))
                for s, f, h in pieces
            ],
            axis=0,
        )
        lifted = lifted + lax.dot_general(
            wide, b_flat, (((0,), (0,)), ((), ())), preferred_element_type=jnp.float32
        )
    return lifted.astype(jnp.bfloat16)


def solution(mesh):
    placed = (
        P(("groups", "dp"), "tensor"),
        P(("groups", "dp"), None),
        P("groups"),
        P("tensor", None),
        P(("groups", "dp"), "tensor", None),
        P(("groups", "dp"), None, None),
    )
    n = mesh.shape["dp"]
    return jax.shard_map(
        lambda *a: shards(n, *a),
        mesh=mesh,
        in_specs=placed,
        out_specs=P(("groups", "dp"), "tensor"),
        check_vma=False,
    )
```

time: 83.4 us -> 67.2 us (0.81)
  starting transfers between devices: 22.6 us -> 11.3 us
  other arithmetic: 7.54 us -> 2.47 us
  between operations: 5.15 us -> 0.3 us
  matrix products: 21.5 us -> 26 us
  waiting for transfers between devices: 20.3 us -> 21.6 us
  local copies, waits for them, and re-layouts: 5.93 us -> 5.03 us
    ppermute x15 -> x9, starting transfers between devices: 22.5 us -> 11.2 us  [the longest x3 7.48 us: shards(): p = lax.ppermute(p, ('dp', 'tensor'), forth)]
    eq x1, other arithmetic: 5.05 us -> 0.01 us  [shards(): part = jnp.where((far == s)[None, :], part, total[first:last])]
    dot_general x12, matrix products: 16.1 us -> 20.5 us  [the longest x9 12.9 us: shards(): lax.dot_general(piece[:, :half], requests, (((1,), (1,)), ((), ())), pref...]
    ppermute x15 -> x9, waiting for transfers between devices: 19 us -> 20.4 us  [the longest x3 15.3 us: shards(): p = lax.ppermute(p, ('dp', 'tensor'), forth)]
    dynamic_slice x2 -> x0, local copies, waits for them, and re-layouts: 1.29 us -> none  [the longest x1 0.7 us: shards(): origin = jnp.array(order, jnp.int32)[(pos + way * s + n) % n]]
    slice x14 -> x2, local copies, waits for them, and re-layouts: 1.26 us -> 0.04 us  [the longest x1 0.02 us: shards(): p[:mid]]
    unnamed x26 -> x18, local copies, waits for them, and re-layouts: 2.44 us -> 3.36 us
  transfers between devices with their start and end apart: 16 -> 10, of which waited for: 11 -> 5; matrix products, arithmetic and copies ran while one was open for 33% -> 41% of each run, Pallas kernels for 0% -> 0%
where the time goes in v2:
time: 67.2 us; the launch traced here: 66.7 us
  matrix products  26 us (39%)
  waiting for transfers between devices  21.6 us (32%)
  starting transfers between devices  11.3 us (17%)
  local copies, waits for them, and re-layouts  5.03 us (7%)
  other arithmetic  2.47 us (4%)
    ppermute x3, waiting for transfers between devices, shards(): p = lax.ppermute(p, ('dp', 'tensor'), forth)  15.3 us
    dot_general x9, matrix products, shards(): lax.dot_general(piece[:, :half], requests, (((1,), (1,)), ((), ())), pref...  12.9 us
    ppermute x3, starting transfers between devices, shards(): p = lax.ppermute(p, ('dp', 'tensor'), forth)  7.48 us
    dot_general x1, matrix products, shards(): here = jnp.dot(requests, w_here, preferred_element_type=jnp.float32)  5.47 us
    dot_general x1, matrix products, shards(): there = jnp.dot(requests, w_there, preferred_element_type=jnp.float32)  5.46 us
    ppermute x1, waiting for transfers between devices, shards(): lax.ppermute(p[:mid], ('dp', 'tensor'), forth)  4.6 us
    unnamed x18, local copies, waits for them, and re-layouts  3.36 us
    ppermute x1, starting transfers between devices, shards(): lax.ppermute(p[:mid], ('dp', 'tensor'), forth)  2.53 us
  transfers between devices with their start and end apart: 10, of which 5 were waited for; matrix products, arithmetic and copies ran while one was open for 41% of the time, Pallas kernels for 0%

profile of v2, /device:TPU:0, one launch (start us, length us, event | category | flops | bytes accessed | tf_op | source)
XLA Modules:
  0.0 66.7 jit_solution(5212294014066128565)
XLA Ops:
  0.0 0.0 copy-start
  0.0 1.6 %constant_dynamic-update-slice_fusion.11 = (bf16[512,512]{1,0:T(8,128)(2,1)}, bf16[64,512]{1,0:T(8,128)(2,1)S(1)}) fusion(bf16[1,64,1024]{2,1,0:T(8,128)(2,1)} %param.16, s32[]{:T(128)S(6)} %select_n.104), kind=kLoop, calls=%fused_computation.47 | loop fusion | bytes 196612
  1.6 1.9 %pad_maximum_fusion = bf16[64,4608]{1,0:T(8,128)(2,1)} fusion(bf16[64,512]{1,0:T(8,128)(2,1)S(1)} %get-tuple-element.40, bf16[64,4096]{1,0:T(8,128)(2,1)} %bitcast.29), kind=kLoop, calls=%fused_computation.14 | loop fusion | flops 1179648 | bytes 1179648 | tf_op jit(solution)/shard_map/concatenate | solution.py:38
  3.5 3.0 %collective-permute-start = (bf16[64,4608]{1,0:T(8,128)(2,1)}, bf16[64,4608]{1,0:T(8,128)(2,1)}, u32[]{:S(2)}, u32[]{:S(2)}) collective-permute-start(bf16[64,4608]{1,0:T(8,128)(2,1)} %pad_maximum_fusion), channel_id=1, source_target_pairs={{0,4},{5,1},{4,8},{9,5},{8,12},{13,9},{12,14},{15,13},{14,10},{11,... | collective-permute-start | bytes 1769480 | tf_op jit(solution)/shard_map/ppermute | solution.py:49
  6.5 0.0 copy-done
  6.5 5.5 %fusion.7 = f32[384,512]{0,1:T(8,128)} fusion(bf16[384,4096]{1,0:T(8,128)(2,1)S(1)} %copy-done, bf16[4096,1024]{1,0:T(8,128)(2,1)} %param.14, s32[]{:T(128)S(6)} %select_n.105), kind=kOutput, calls=%fused_computation.5 | convolution fusion | flops 1610612736 | bytes 8126468 | tf_op jit(solution)/shard_map/dot_general | solution.py:42
  12.0 0.0 collective-permute-start.2
  12.0 0.0 collective-permute-start.1
  12.0 0.0 copy-start.3
  12.0 0.0 copy-start.4
  12.0 5.5 %fusion.4 = f32[384,512]{0,1:T(8,128)} fusion(bf16[384,4096]{1,0:T(8,128)(2,1)S(1)} %copy-done, bf16[4096,1024]{1,0:T(8,128)(2,1)} %param.14, s32[]{:T(128)S(6)} %select_n.104), kind=kOutput, calls=%fused_computation.4 | convolution fusion | flops 1610612736 | bytes 8126468 | tf_op jit(solution)/shard_map/dot_general | solution.py:44
  17.5 0.0 copy-done.3
  17.5 0.7 %fusion.26 = s32[8]{0:T(128)S(1)} fusion(s32[16,8]{1,0:T(8,128)} %constant.98.clone, s32[]{:T(128)S(6)} %select_n.106), kind=kLoop, calls=%fused_computation.80 | loop fusion | bytes 68 | tf_op jit(solution)/shard_map/jit(_where)/broadcast_in_dim | solution.py:33
  18.2 0.0 copy-done.4
  18.2 0.2 select_reduce_fusion.1
  18.4 0.1 select_reduce_fusion
  18.5 0.0 copy-start.1
  18.5 2.2 %convolution_select_fusion = f32[64,384]{1,0:T(8,128)S(1)} fusion(bf16[384,4096]{1,0:T(8,128)(2,1)S(1)} %copy-done, bf16[1,4096,64]{1,2,0:T(8,128)(2,1)} %param.15, pred[384]{0:T(512)(128)(4,1)S(1)} %get-tuple-element.52), kind=kOutput, calls=%fused_computation.6 | convolution fusion | flops 201351168 | bytes 3768704 | tf_op jit(solution)/shard_map/dot_general | solution.py:66
  20.7 0.0 collective-permute-done
  20.7 2.1 %collective-permute-start.5 = (bf16[64,4608]{1,0:T(8,128)(2,1)}, bf16[64,4608]{1,0:T(8,128)(2,1)S(1)}, u32[]{:S(2)}, u32[]{:S(2)}) collective-permute-start(bf16[64,4608]{1,0:T(8,128)(2,1)} %collective-permute-done), channel_id=1, source_target_pairs={{0,4},{5,1},{4,8},{9,5},{8,12},{13,9},{12,14},{15,13},{14,10},{11,... | collective-permute-start | bytes 1769480 | tf_op jit(solution)/shard_map/ppermute | solution.py:49
  22.8 2.2 %convolution_select_fusion.1 = f32[64,384]{1,0:T(8,128)S(1)} fusion(f32[64,384]{1,0:T(8,128)S(1)} %convolution_select_fusion, bf16[384,4096]{1,0:T(8,128)(2,1)S(1)} %copy-done, bf16[64,4608]{1,0:T(8,128)(2,1)} %collective-permute-done, pred[384]{0:T(512)(128)(4,1)S(1)} %get-tuple-element.46), kind=kOutput, calls=%fused_computation.7 | convolution fusion | flops 201351168 | bytes 3867008 | tf_op jit(solution)/shard_map/dot_general | solution.py:66
  24.9 0.0 collective-permute-done.2
  24.9 0.1 collective-permute-start.3
  25.0 0.0 copy-done.1
  25.0 0.8 %slice_dynamic-update-slice_fusion.5 = bf16[512,512]{1,0:T(8,128)(2,1)S(1)} fusion(bf16[512,512]{1,0:T(8,128)(2,1)S(1)} %copy-done.1, bf16[64,4608]{1,0:T(8,128)(2,1)} %collective-permute-done), kind=kLoop, calls=%fused_computation.34 | loop fusion | bytes 131072
  25.9 0.8 %slice_dynamic-update-slice_fusion.4 = bf16[512,512]{1,0:T(8,128)(2,1)S(1)} fusion(bf16[512,512]{1,0:T(8,128)(2,1)S(1)} %slice_dynamic-update-slice_fusion.5, bf16[64,4608]{1,0:T(8,128)(2,1)} %collective-permute-done.2), kind=kLoop, calls=%fused_computation.33 | loop fusion | bytes 131072
  26.7 2.1 %convolution_select_fusion.2 = f32[64,384]{1,0:T(8,128)S(1)} fusion(f32[64,384]{1,0:T(8,128)S(1)} %convolution_select_fusion.1, bf16[384,4096]{1,0:T(8,128)(2,1)S(1)} %copy-done, bf16[64,4608]{1,0:T(8,128)(2,1)} %collective-permute-done.2, pred[384]{0:T(512)(128)(4,1)S(1)} %get-tuple-element.47), kind=kOutput, calls=%fused_computation.8 | convolution fusion | flops 201351168 | bytes 3867008 | tf_op jit(solution)/shard_map/dot_general | solution.py:66
  28.8 6.1 %collective-permute-done.5 = bf16[64,4608]{1,0:T(8,128)(2,1)S(1)} collective-permute-done((bf16[64,4608]{1,0:T(8,128)(2,1)}, bf16[64,4608]{1,0:T(8,128)(2,1)S(1)}, u32[]{:S(2)}, u32[]{:S(2)}) %collective-permute-start.5) | collective-permute-done | bytes 589856 | tf_op jit(solution)/shard_map/ppermute | solution.py:49
  35.0 2.4 %collective-permute-start.6 = (bf16[64,4608]{1,0:T(8,128)(2,1)S(1)}, bf16[64,4608]{1,0:T(8,128)(2,1)S(1)}, u32[]{:S(2)}, u32[]{:S(2)}) collective-permute-start(bf16[64,4608]{1,0:T(8,128)(2,1)S(1)} %collective-permute-done.5), channel_id=1, source_target_pairs={{0,4},{5,1},{4,8},{9,5},{8,12},{13,9},{12,14},{15,13},{14,10},{11,... | collective-permute-start | bytes 1769480 | tf_op jit(solution)/shard_map/ppermute | solution.py:49
  37.4 0.4 collective-permute-done.3
  37.8 0.9 %collective-permute-start.4 = (bf16[64,4608]{1,0:T(8,128)(2,1)S(1)}, bf16[64,4608]{1,0:T(8,128)(2,1)S(1)}, u32[]{:S(2)}, u32[]{:S(2)}) collective-permute-start(bf16[64,4608]{1,0:T(8,128)(2,1)S(1)} %collective-permute-done.3), channel_id=1, source_target_pairs={{4,0},{1,5},{8,4},{5,9},{12,8},{9,13},{14,12},{13,15},{10,14},{15,... | collective-permute-start | bytes 1769480 | tf_op jit(solution)/shard_map/ppermute | solution.py:50
  38.7 1.1 %convolution_select_fusion.3 = f32[64,384]{1,0:T(8,128)S(1)} fusion(f32[64,384]{1,0:T(8,128)S(1)} %convolution_select_fusion.2, bf16[384,4096]{1,0:T(8,128)(2,1)S(1)} %copy-done, bf16[64,4608]{1,0:T(8,128)(2,1)S(1)} %collective-permute-done.5, pred[384]{0:T(512)(128)(4,1)S(1)} %get-tuple-element.48), kind=kOutput, calls=%fused_computation.9 | convolution fusion | flops 201351168 | bytes 3867136 | tf_op jit(solution)/shard_map/dot_general | solution.py:66
  39.8 1.1 %convolution_select_fusion.4 = f32[64,384]{1,0:T(8,128)S(1)} fusion(f32[64,384]{1,0:T(8,128)S(1)} %convolution_select_fusion.3, bf16[384,4096]{1,0:T(8,128)(2,1)S(1)} %copy-done, bf16[64,4608]{1,0:T(8,128)(2,1)S(1)} %collective-permute-done.3, pred[384]{0:T(512)(128)(4,1)S(1)} %get-tuple-element.49), kind=kOutput, calls=%fused_computation.10 | convolution fusion | flops 201351168 | bytes 3867136 | tf_op jit(solution)/shard_map/dot_general | solution.py:66
  40.9 9.2 %collective-permute-done.6 = bf16[64,4608]{1,0:T(8,128)(2,1)S(1)} collective-permute-done((bf16[64,4608]{1,0:T(8,128)(2,1)S(1)}, bf16[64,4608]{1,0:T(8,128)(2,1)S(1)}, u32[]{:S(2)}, u32[]{:S(2)}) %collective-permute-start.6) | collective-permute-done | bytes 589856 | tf_op jit(solution)/shard_map/ppermute | solution.py:49
  50.1 2.5 %collective-permute-start.7 = (bf16[32,4608]{1,0:T(8,128)(2,1)S(1)}, bf16[32,4608]{1,0:T(8,128)(2,1)S(1)}, u32[]{:S(2)}, u32[]{:S(2)}) collective-permute-start(bf16[32,4608]{1,0:T(8,128)(2,1)S(1)} %slice.135), channel_id=1, source_target_pairs={{0,4},{5,1},{4,8},{9,5},{8,12},{13,9},{12,14},{15,13},{14,10},{11,... | collective-permute-start | bytes 884744 | tf_op jit(solution)/shard_map/ppermute | solution.py:57
  52.7 0.0 collective-permute-done.4
  52.7 0.2 collective-permute-start.8
  53.0 1.1 %convolution_select_fusion.5 = f32[64,384]{1,0:T(8,128)S(1)} fusion(f32[64,384]{1,0:T(8,128)S(1)} %convolution_select_fusion.4, bf16[384,4096]{1,0:T(8,128)(2,1)S(1)} %copy-done, bf16[64,4608]{1,0:T(8,128)(2,1)S(1)} %collective-permute-done.6, pred[384]{0:T(512)(128)(4,1)S(1)} %get-tuple-element.50), kind=kOutput, calls=%fused_computation.11 | convolution fusion | flops 201351168 | bytes 3867136 | tf_op jit(solution)/shard_map/dot_general | solution.py:66
  54.1 1.1 %convolution_select_fusion.6 = f32[64,384]{1,0:T(8,128)S(1)} fusion(f32[64,384]{1,0:T(8,128)S(1)} %convolution_select_fusion.5, bf16[384,4096]{1,0:T(8,128)(2,1)S(1)} %copy-done, bf16[64,4608]{1,0:T(8,128)(2,1)S(1)} %collective-permute-done.4, pred[384]{0:T(512)(128)(4,1)S(1)} %get-tuple-element.51), kind=kOutput, calls=%fused_computation.12 | convolution fusion | flops 201351168 | bytes 3867136 | tf_op jit(solution)/shard_map/dot_general | solution.py:66
  55.2 4.6 %collective-permute-done.7 = bf16[32,4608]{1,0:T(8,128)(2,1)S(1)} collective-permute-done((bf16[32,4608]{1,0:T(8,128)(2,1)S(1)}, bf16[32,4608]{1,0:T(8,128)(2,1)S(1)}, u32[]{:S(2)}, u32[]{:S(2)}) %collective-permute-start.7) | collective-permute-done | bytes 294944 | tf_op jit(solution)/shard_map/ppermute | solution.py:57
  59.8 1.0 %fusion.23 = f32[64,384]{1,0:T(8,128)S(1)} fusion(f32[64,384]{1,0:T(8,128)S(1)} %convolution_select_fusion.6, pred[384]{0:T(512)(128)(4,1)S(1)} %get-tuple-element.45, bf16[384,4096]{1,0:T(8,128)(2,1)S(1)} %copy-done, bf16[32,4608]{1,0:T(8,128)(2,1)S(1)} %collective-permute-done.7), kind=kOutput, calls=%fused_computation.60 | convolution fusion | flops 100675584 | bytes 3506688 | tf_op jit(solution)/shard_map/dot_general | solution.py:66
  60.8 0.0 copy-start.2
  60.8 0.0 collective-permute-done.8
  60.8 1.0 %fusion.22 = f32[64,384]{1,0:T(8,128)S(1)} fusion(f32[64,384]{1,0:T(8,128)S(1)} %fusion.23, pred[384]{0:T(512)(128)(4,1)S(1)} %get-tuple-element.45, bf16[384,4096]{1,0:T(8,128)(2,1)S(1)} %copy-done, bf16[32,4608]{1,0:T(8,128)(2,1)S(1)} %collective-permute-done.8), kind=kOutput, calls=%fused_computation.58 | convolution fusion | flops 100675584 | bytes 3506688 | tf_op jit(solution)/shard_map/dot_general | solution.py:66
  61.9 0.1 collective-permute-start.9
  62.0 1.3 %collective-permute-done.9 = f32[64,384]{1,0:T(8,128)S(1)} collective-permute-done((f32[64,384]{1,0:T(8,128)S(1)}, f32[64,384]{1,0:T(8,128)S(1)}, u32[]{:S(2)}, u32[]{:S(2)}) %collective-permute-start.9) | collective-permute-done | bytes 98336 | tf_op jit(solution)/shard_map/ppermute | solution.py:71
  63.6 0.5 fusion.28
  64.1 0.0 collective-permute-done.1
  64.1 0.0 copy-done.2
  64.1 1.7 %add_convert_fusion = bf16[384,512]{0,1:T(8,128)(2,1)S(1)} fusion(f32[384,512]{0,1:T(8,128)S(1)} %fusion.28, f32[384,512]{0,1:T(8,128)S(1)} %copy-done.2, f32[384,512]{0,1:T(8,128)} %collective-permute-done.1, bf16[512,384]{1,0:T(8,128)(2,1)S(1)} %constant_dynamic-update-slice_fusion.12, bf16[512,512]{1,0:T(8,128)(2,1)S(1)} %constant_dynamic-update-slice_fusion.9), kind=kOutput, calls=%fused_computation.13 | convolution fusion | flops 202113024 | bytes 3670016 | tf_op jit(solution)/shard_map/dot_general | solution.py:86
  65.8 0.9 %copy.13 = bf16[384,512]{1,0:T(8,128)(2,1)} copy(bf16[384,512]{0,1:T(8,128)(2,1)S(1)} %add_convert_fusion) | data formatting | bytes 786432 | tf_op jit(solution)/shard_map/convert_element_type | solution.py:89
  (20 shorter events, 0.4 us)
Async XLA Ops:
  0.0 6.5 %copy-start = (bf16[384,4096]{1,0:T(8,128)(2,1)S(1)}, bf16[384,4096]{1,0:T(8,128)(2,1)}, u32[]{:S(2)}) copy-start(bf16[384,4096]{1,0:T(8,128)(2,1)} %param.11) | copy-start | bytes 9437188
  3.5 17.2 %collective-permute-start = (bf16[64,4608]{1,0:T(8,128)(2,1)}, bf16[64,4608]{1,0:T(8,128)(2,1)}, u32[]{:S(2)}, u32[]{:S(2)}) collective-permute-start(bf16[64,4608]{1,0:T(8,128)(2,1)} %pad_maximum_fusion), channel_id=1, source_target_pairs={{0,4},{5,1},{4,8},{9,5},{8,12},{13,9},{12,14},{15,13},{14,10},{11,... | collective-permute-start | bytes 1769480 | tf_op jit(solution)/shard_map/ppermute | solution.py:49
  12.0 12.9 %collective-permute-start.2 = (bf16[64,4608]{1,0:T(8,128)(2,1)}, bf16[64,4608]{1,0:T(8,128)(2,1)}, u32[]{:S(2)}, u32[]{:S(2)}) collective-permute-start(bf16[64,4608]{1,0:T(8,128)(2,1)} %pad_maximum_fusion), channel_id=1, source_target_pairs={{4,0},{1,5},{8,4},{5,9},{12,8},{9,13},{14,12},{13,15},{10,14},{15,... | collective-permute-start | bytes 1769480 | tf_op jit(solution)/shard_map/ppermute | solution.py:50
  12.0 52.1 %collective-permute-start.1 = (f32[384,512]{0,1:T(8,128)}, f32[384,512]{0,1:T(8,128)}, u32[]{:S(2)}, u32[]{:S(2)}) collective-permute-start(f32[384,512]{0,1:T(8,128)} %fusion.7), channel_id=1, source_target_pairs={{0,1},{1,0},{2,3},{3,2},{4,5},{5,4},{6,7},{7,6},{8,9},{9,8},{10,11... | collective-permute-start | bytes 2359304 | tf_op jit(solution)/shard_map/ppermute | solution.py:61
  12.0 5.5 %copy-start.3 = (s32[384,1]{0,1:T(1,128)S(1)}, s32[384,1]{0,1:T(1,128)}, u32[]{:S(2)}) copy-start(s32[384,1]{0,1:T(1,128)} %param.12) | copy-start | bytes 4612
  12.0 6.2 %copy-start.4 = (s32[8]{0:T(128)S(1)}, s32[8]{0:T(128)}, u32[]{:S(2)}) copy-start(s32[8]{0:T(128)} %param.13) | copy-start | bytes 100
  18.5 6.5 %copy-start.1 = (bf16[512,512]{1,0:T(8,128)(2,1)S(1)}, bf16[512,512]{1,0:T(8,128)(2,1)}, u32[]{:S(2)}) copy-start(bf16[512,512]{1,0:T(8,128)(2,1)} %get-tuple-element.39) | copy-start | bytes 1572868
  20.7 14.3 %collective-permute-start.5 = (bf16[64,4608]{1,0:T(8,128)(2,1)}, bf16[64,4608]{1,0:T(8,128)(2,1)S(1)}, u32[]{:S(2)}, u32[]{:S(2)}) collective-permute-start(bf16[64,4608]{1,0:T(8,128)(2,1)} %collective-permute-done), channel_id=1, source_target_pairs={{0,4},{5,1},{4,8},{9,5},{8,12},{13,9},{12,14},{15,13},{14,10},{11,... | collective-permute-start | bytes 1769480 | tf_op jit(solution)/shard_map/ppermute | solution.py:49
  24.9 12.8 %collective-permute-start.3 = (bf16[64,4608]{1,0:T(8,128)(2,1)}, bf16[64,4608]{1,0:T(8,128)(2,1)S(1)}, u32[]{:S(2)}, u32[]{:S(2)}) collective-permute-start(bf16[64,4608]{1,0:T(8,128)(2,1)} %collective-permute-done.2), channel_id=1, source_target_pairs={{4,0},{1,5},{8,4},{5,9},{12,8},{9,13},{14,12},{13,15},{10,14},{15,... | collective-permute-start | bytes 1769480 | tf_op jit(solution)/shard_map/ppermute | solution.py:50
  35.0 15.1 %collective-permute-start.6 = (bf16[64,4608]{1,0:T(8,128)(2,1)S(1)}, bf16[64,4608]{1,0:T(8,128)(2,1)S(1)}, u32[]{:S(2)}, u32[]{:S(2)}) collective-permute-start(bf16[64,4608]{1,0:T(8,128)(2,1)S(1)} %collective-permute-done.5), channel_id=1, source_target_pairs={{0,4},{5,1},{4,8},{9,5},{8,12},{13,9},{12,14},{15,13},{14,10},{11,... | collective-permute-start | bytes 1769480 | tf_op jit(solution)/shard_map/ppermute | solution.py:49
  37.8 14.9 %collective-permute-start.4 = (bf16[64,4608]{1,0:T(8,128)(2,1)S(1)}, bf16[64,4608]{1,0:T(8,128)(2,1)S(1)}, u32[]{:S(2)}, u32[]{:S(2)}) collective-permute-start(bf16[64,4608]{1,0:T(8,128)(2,1)S(1)} %collective-permute-done.3), channel_id=1, source_target_pairs={{4,0},{1,5},{8,4},{5,9},{12,8},{9,13},{14,12},{13,15},{10,14},{15,... | collective-permute-start | bytes 1769480 | tf_op jit(solution)/shard_map/ppermute | solution.py:50
  50.1 9.6 %collective-permute-start.7 = (bf16[32,4608]{1,0:T(8,128)(2,1)S(1)}, bf16[32,4608]{1,0:T(8,128)(2,1)S(1)}, u32[]{:S(2)}, u32[]{:S(2)}) collective-permute-start(bf16[32,4608]{1,0:T(8,128)(2,1)S(1)} %slice.135), channel_id=1, source_target_pairs={{0,4},{5,1},{4,8},{9,5},{8,12},{13,9},{12,14},{15,13},{14,10},{11,... | collective-permute-start | bytes 884744 | tf_op jit(solution)/shard_map/ppermute | solution.py:57
  52.7 8.1 %collective-permute-start.8 = (bf16[32,4608]{1,0:T(8,128)(2,1)S(1)}, bf16[32,4608]{1,0:T(8,128)(2,1)S(1)}, u32[]{:S(2)}, u32[]{:S(2)}) collective-permute-start(bf16[32,4608]{1,0:T(8,128)(2,1)S(1)} %slice.138), channel_id=1, source_target_pairs={{4,0},{1,5},{8,4},{5,9},{12,8},{9,13},{14,12},{13,15},{10,14},{15,... | collective-permute-start | bytes 884744 | tf_op jit(solution)/shard_map/ppermute | solution.py:58
  60.8 3.3 %copy-start.2 = (f32[384,512]{0,1:T(8,128)S(1)}, f32[384,512]{0,1:T(8,128)}, u32[]{:S(2)}) copy-start(f32[384,512]{0,1:T(8,128)} %fusion.4) | copy-start | bytes 2359300
  61.9 1.4 %collective-permute-start.9 = (f32[64,384]{1,0:T(8,128)S(1)}, f32[64,384]{1,0:T(8,128)S(1)}, u32[]{:S(2)}, u32[]{:S(2)}) collective-permute-start(f32[64,384]{1,0:T(8,128)S(1)} %fusion.22), channel_id=1, source_target_pairs={{0,1},{1,0},{2,3},{3,2},{4,5},{5,4},{6,7},{7,6},{8,9},{9,8},{10,11... | collective-permute-start | bytes 294920 | tf_op jit(solution)/shard_map/ppermute | solution.py:71

commit v3 on v1

v3 whole, which is shorter than its diff:
```python
import functools

import jax
import jax.numpy as jnp
from jax import lax
from jax.experimental import pallas as pl
from jax.experimental.pallas import tpu as pltpu
from jax.sharding import PartitionSpec as P

BASE_PARTS = 2
LANES = 128
tie = lax.optimization_barrier
VMEM = pl.BlockSpec(memory_space=pltpu.VMEM)
SMEM = pl.BlockSpec(memory_space=pltpu.SMEM)
HBM = pl.BlockSpec(memory_space=pl.ANY)
SMALL = pl.CostEstimate(flops=1000, bytes_accessed=1000, transcendentals=0)


def ring_of(n):
    if n % 2 == 0 and n <= 16:
        return list(range(0, n, 2)) + list(range(n - 1, 0, -2))
    return list(range(n))


def call(kernel, shape, dtype, in_specs, *args, mib=24, scratch=()):
    return pl.pallas_call(
        kernel,
        in_specs=in_specs,
        out_specs=VMEM,
        out_shape=jax.ShapeDtypeStruct(shape, dtype),
        scratch_shapes=scratch,
        compiler_params=pltpu.CompilerParams(vmem_limit_bytes=mib << 20),
        cost_estimate=SMALL,
    )(*args)


def pack_kernel(half, out_keys, a_ref, b_ref, o_ref, a_sem, b_sem):
    first = pl.multiple_of(lax.axis_index("tensor") * out_keys, out_keys)
    a_copy = pltpu.make_async_copy(a_ref, o_ref.at[:, :half], a_sem)
    b_copy = pltpu.make_async_copy(b_ref.at[:, pl.ds(first, out_keys)], o_ref.at[:, half:], b_sem)
    a_copy.start()
    b_copy.start()
    a_copy.wait()
    b_copy.wait()


def far_kernel(n, index_ref, storage_ref, steps_ref, o_ref):
    row = (2 * lax.axis_index("dp") + lax.axis_index("tensor")) * n
    index = index_ref[...]

    def look(j, far):
        return jnp.where(index == j, steps_ref[row + storage_ref[j]], far)

    far = lax.fori_loop(0, n, look, jnp.zeros_like(index))
    o_ref[...] = jnp.broadcast_to(far, o_ref.shape)


def base_kernel(other, offset, out_keys, x_ref, w_ref, o_ref):
    core = lax.axis_index("tensor")
    core = 1 - core if other else core
    width = o_ref.shape[1]
    first = pl.multiple_of(core * out_keys + offset, width)
    o_ref[...] = jnp.dot(x_ref[...], w_ref[:, pl.ds(first, width)], preferred_element_type=jnp.float32)


def down_kernel(half, s, x_ref, m_ref, far_ref, *rest):
    o_ref = rest[-1]
    part = lax.dot_general(
        x_ref[...], m_ref[:, :half], (((1,), (1,)), ((), ())), preferred_element_type=jnp.float32
    )
    if s is not None:
        kept = rest[0][...] if len(rest) > 1 else 0.0
        o_ref[...] = jnp.where(far_ref[:, : part.shape[1]] == s, part, kept)
    elif len(rest) > 1:
        o_ref[...] = jnp.concatenate([rest[0][...], part], axis=1)
    else:
        o_ref[...] = part


def lift(steps, far_ref, total, b_refs, out_of):
    high = total.astype(jnp.bfloat16)
    low = (total - high.astype(jnp.float32)).astype(jnp.bfloat16)
    rank = total.shape[1]
    far = far_ref[:, :rank]
    out_keys = out_of.shape[1]
    b_all = jnp.concatenate([b[:, b.shape[1] - out_keys :] for b in b_refs], axis=0)
    out = None
    for part in (low, high):
        part = part.astype(jnp.float32)
        wide = jnp.concatenate([jnp.where(far == s, part, 0.0).astype(jnp.bfloat16) for s in steps], axis=1)
        product = jnp.dot(wide, b_all, preferred_element_type=jnp.float32)
        out = product if out is None else out + product
    return out


def up_kernel(steps, parts, far_ref, own_ref, other_ref, there_ref, *rest):
    o_ref = rest[-1]
    lifted = lift(steps, far_ref, own_ref[...] + other_ref[...], rest[parts:-1], o_ref)
    here = jnp.concatenate([h[...] for h in rest[:parts]], axis=1)
    o_ref[...] = here + there_ref[...] + lifted


def last_kernel(steps, far_ref, own_ref, other_ref, base_ref, *rest):
    lifted = lift(steps, far_ref, own_ref[...] + other_ref[...], rest[:-1], rest[-1])
    rest[-1][...] = (base_ref[...] + lifted).astype(jnp.bfloat16)


def shards(n, requests, adapter_index, storage_slot_index, key_base_weight, down_factor, up_factor):
    rows, half = requests.shape
    rank = down_factor.shape[2]
    keys = up_factor.shape[2]
    out_keys = keys // 2
    order = ring_of(n)
    place = [order.index(i) for i in range(n)]

    forth, back = [], []
    for j in range(n):
        a, b = order[j], order[(j + 1) % n]
        forth += [(2 * a, 2 * b), (2 * b + 1, 2 * a + 1)]
        back += [(2 * b, 2 * a), (2 * a + 1, 2 * b + 1)]
    swap = [(0, 1), (1, 0)]
    both = ("dp", "tensor")

    steps = [(place[d] - place[s]) * (1 - 2 * c) % n for d in range(n) for c in range(2) for s in range(n)]

    def base_of(x, other, offset, width):
        kernel = functools.partial(base_kernel, other, offset, out_keys)
        return call(kernel, (rows, width), jnp.float32, [VMEM, VMEM], x, key_base_weight)

    def down_of(x, message, s, *total):
        width = message.shape[0] + (total[0].shape[1] if total and s is None else 0)
        kernel = functools.partial(down_kernel, half, s)
        return call(
            kernel, (rows, width), jnp.float32, [VMEM] * (3 + len(total)), x, message, far, *total, mib=16
        )

    own = call(
        functools.partial(pack_kernel, half, out_keys),
        (rank, half + out_keys),
        jnp.bfloat16,
        [HBM, HBM],
        down_factor[0].T,
        up_factor[0],
        mib=8,
        scratch=[pltpu.SemaphoreType.DMA] * 2,
    )

    there = base_of(requests, True, 0, out_keys)
    far = call(
        functools.partial(far_kernel, n),
        (rows, LANES),
        jnp.int32,
        [VMEM, SMEM, SMEM],
        adapter_index,
        storage_slot_index,
        jnp.array(steps, jnp.int32),
        mib=8,
    )
    total = down_of(requests, own, 0)
    there, total, q = tie((there, total, own))
    from_there = lax.ppermute(there, "tensor", swap)
    here = []
    width = out_keys // BASE_PARTS

    def base_part(x):
        return [base_of(x, False, len(here) * width, width)] if len(here) < BASE_PARTS else []

    p = own
    pieces = [(0, own)]
    waiting = None
    for s in range(1, (n - 1) // 2 + 1):
        p = lax.ppermute(p, both, forth)
        q = lax.ppermute(q, both, back)
        for turn in range(2):
            arrived = q if turn else p
            x = requests
            work = []
            if waiting is not None:
                _, x = tie((waiting[1], requests))
                work.append(down_of(x, waiting[1], waiting[0], total))
            more = base_part(x)
            arrived, *work = tie((arrived, *work, *more))
            here += work[len(work) - len(more) :]
            if waiting is not None:
                total = work[0]
            waiting = (n - s, arrived) if turn else (s, arrived)
            pieces.append(waiting)
            if turn:
                q = arrived
            else:
                p = arrived
    while len(here) < BASE_PARTS:
        here += base_part(requests)

    opposite = n % 2 == 0 and n > 1
    if opposite:
        mid = rank // 2
        p = lax.ppermute(p[:mid], both, forth)
        q = lax.ppermute(q[mid:], both, back)
    if waiting is not None:
        _, x = tie((waiting[1], requests))
        total = down_of(x, waiting[1], waiting[0], total)
    other = lax.ppermute(total, "tensor", swap)
    messages = [m if n <= 16 else m[:, half:] for _, m in pieces]
    base = call(
        functools.partial(up_kernel, [s for s, _ in pieces], BASE_PARTS),
        (rows, out_keys),
        jnp.float32,
        [VMEM] * (4 + BASE_PARTS + len(messages)),
        far,
        total,
        other,
        from_there,
        *here,
        *messages,
        mib=32,
    )
    if not opposite:
        return base.astype(jnp.bfloat16)
    base, p = tie((base, p))
    total = down_of(requests, p, None)
    total, q = tie((total, q))
    total = down_of(requests, q, None, total)
    other = lax.ppermute(total, "tensor", swap)
    return call(
        functools.partial(last_kernel, [n // 2]),
        (rows, out_keys),
        jnp.bfloat16,
        [VMEM] * 6,
        far,
        total,
        other,
        base,
        p,
        q,
        mib=16,
    )


def solution(mesh):
    placed = (
        P(("groups", "dp"), "tensor"),
        P(("groups", "dp"), None),
        P("groups"),
        P("tensor", None),
        P(("groups", "dp"), "tensor", None),
        P(("groups", "dp"), None, None),
    )
    n = mesh.shape["dp"]
    return jax.shard_map(
        functools.partial(shards, n),
        mesh=mesh,
        in_specs=placed,
        out_specs=P(("groups", "dp"), "tensor"),
        check_vma=False,
    )
```

time: 83.4 us -> 73 us (0.88)
  matrix products: 21.5 us -> 0 us
  waiting for transfers between devices: 20.3 us -> 35.9 us
  Pallas kernels: 0 us -> 15.2 us
  starting transfers between devices: 22.6 us -> 10.1 us
  other arithmetic: 7.54 us -> 0 us
  local copies, waits for them, and re-layouts: 5.93 us -> 11.3 us
  between operations: 5.15 us -> 0.25 us
    dot_general x13 -> x0, matrix products: 21.5 us -> none  [the longest x8 9.7 us: shards(): lax.dot_general(requests, block, (((1,), (1,)), ((), ())), preferred_elem...]
    ppermute x16 -> x11, waiting for transfers between devices: 20.3 us -> 35.9 us  [the longest x3 30.9 us: shards(): q = lax.ppermute(q, both, back)]
    pallas_call x0 -> x16, Pallas kernels: none -> 15.2 us  [call(): pl.pallas_call(kernel, in_specs=in_specs, out_specs=VMEM, out_shape=jax.S...]
    ppermute x16 -> x11, starting transfers between devices: 22.6 us -> 10.1 us  [the longest x3 7.21 us: shards(): p = lax.ppermute(p, both, forth)]
    unnamed x26 -> x17, local copies, waits for them, and re-layouts: 2.44 us -> 11.2 us
    eq x1 -> x0, other arithmetic: 5.05 us -> none  [shards(): total = jnp.where(slot == origin, part, total)]
    concatenate x2 -> x0, other arithmetic: 1.91 us -> none  [the longest x1 1.89 us: shards(): own = jnp.concatenate([a_t, b_own], axis=1)]
    dynamic_slice x2 -> x0, local copies, waits for them, and re-layouts: 1.29 us -> none  [the longest x1 0.7 us: shards(): origin = jnp.array(order, jnp.int32)[(pos + way * s + n) % n]]
  transfers between devices with their start and end apart: 16 -> 11, of which waited for: 11 -> 6; matrix products, arithmetic and copies ran while one was open for 33% -> 1% of each run, Pallas kernels for 0% -> 18%
where the time goes in v3:
time: 73 us; the launch traced here: 72.6 us
  waiting for transfers between devices  35.9 us (49%)
  Pallas kernels  15.2 us (21%)
  local copies, waits for them, and re-layouts  11.3 us (15%)
  starting transfers between devices  10.1 us (14%)
    ppermute x3, waiting for transfers between devices, shards(): q = lax.ppermute(q, both, back)  30.9 us
    pallas_call x16, Pallas kernels, call(): pl.pallas_call(kernel, in_specs=in_specs, out_specs=VMEM, out_shape=jax.S...  15.2 us
    unnamed x17, local copies, waits for them, and re-layouts  11.2 us
    ppermute x3, starting transfers between devices, shards(): p = lax.ppermute(p, both, forth)  7.21 us
    ppermute x2, waiting for transfers between devices, shards(): other = lax.ppermute(total, 'tensor', swap)  2.85 us
    ppermute x1, waiting for transfers between devices, shards(): q = lax.ppermute(q[mid:], both, back)  2.11 us
    ppermute x1, starting transfers between devices, shards(): p = lax.ppermute(p[:mid], both, forth)  1.55 us
  transfers between devices with their start and end apart: 11, of which 6 were waited for; matrix products, arithmetic and copies ran while one was open for 1% of the time, Pallas kernels for 18%

profile of v3, /device:TPU:0, one launch (start us, length us, event | category | flops | bytes accessed | tf_op | source)
XLA Modules:
  0.0 72.6 jit_solution(8365426772437921799)
XLA Ops:
  0.0 0.0 copy-start.4
  0.0 1.0 %copy-done.4 = bf16[1,4096,64]{1,2,0:T(8,128)(2,1)S(1)} copy-done((bf16[1,4096,64]{1,2,0:T(8,128)(2,1)S(1)}, bf16[1,4096,64]{1,2,0:T(8,128)(2,1)}, u32[]{:S(2)}) %copy-start.4) | copy-done | bytes 524312
  1.0 0.0 copy-start.5
  1.0 0.9 %copy-done.5 = bf16[1,64,1024]{2,1,0:T(8,128)(2,1)S(1)} copy-done((bf16[1,64,1024]{2,1,0:T(8,128)(2,1)S(1)}, bf16[1,64,1024]{2,1,0:T(8,128)(2,1)}, u32[]{:S(2)}) %copy-start.5) | copy-done | bytes 131096
  1.9 0.1 shard_map.75.m_ref.rest_2_
  2.0 3.1 %collective-permute-start.1 = (bf16[64,4608]{1,0:T(8,128)(2,1)S(1)}, bf16[64,4608]{1,0:T(8,128)(2,1)S(1)}, u32[]{:S(2)}, u32[]{:S(2)}) collective-permute-start(bf16[64,4608]{1,0:T(8,128)(2,1)S(1)} %shard_map.75.m_ref.rest_2_), channel_id=1, source_target_pairs={{0,4},{5,1},{4,8},{9,5},{8,12},{13,9},{12,14},{15,13},{14,10},{11,... | collective-permute-start | bytes 1769480 | tf_op jit(solution)/shard_map/ppermute | solution.py:172
  5.1 0.8 %copy.8.index_ref = s32[384,1]{1,0:T(8,128)S(1)} copy(s32[384,1]{0,1:T(1,128)} %param.8) | data formatting | bytes 3072 | tf_op args[1]
  5.9 0.0 copy-start.6
  5.9 0.6 copy-done.6
  6.6 0.0 copy-start.7
  6.6 0.7 copy-done.7
  7.2 0.9 %shard_map.73.far_ref = s32[384,128]{1,0:T(8,128)S(1)} custom-call(s32[384,1]{1,0:T(8,128)S(1)} %copy.8.index_ref, s32[8]{0:T(128)S(1)} %copy-done.6, s32[128]{0:T(128)S(1)} %copy-done.7), custom_call_target="tpu_custom_call" | custom-call | flops 1000 | bytes 1000 | tf_op jit(solution)/shard_map/pallas_call | solution.py:26
  8.1 0.0 copy-start
  8.1 1.9 %copy-done = bf16[384,4096]{1,0:T(8,128)(2,1)S(1)} copy-done((bf16[384,4096]{1,0:T(8,128)(2,1)S(1)}, bf16[384,4096]{1,0:T(8,128)(2,1)}, u32[]{:S(2)}) %copy-start) | copy-done | bytes 3145752
  10.0 1.0 %shard_map.76.rest_0_ = f32[384,64]{1,0:T(8,128)S(1)} custom-call(bf16[384,4096]{1,0:T(8,128)(2,1)S(1)} %copy-done, bf16[64,4608]{1,0:T(8,128)(2,1)S(1)} %shard_map.75.m_ref.rest_2_, s32[384,128]{1,0:T(8,128)S(1)} %shard_map.73.far_ref), custom_call_target="tpu_custom_call" | custom-call | flops 1000 | bytes 1000 | tf_op jit(solution)/shard_map/pallas_call | solution.py:26
  11.0 0.0 copy-start.1
  11.0 1.9 %copy-done.1 = bf16[384,4096]{1,0:T(8,128)(2,1)S(1)} copy-done((bf16[384,4096]{1,0:T(8,128)(2,1)S(1)}, bf16[384,4096]{1,0:T(8,128)(2,1)}, u32[]{:S(2)}) %copy-start.1) | copy-done | bytes 3145752
  12.9 0.0 copy-start.3
  12.9 3.4 %copy-done.3 = bf16[4096,1024]{1,0:T(8,128)(2,1)S(1)} copy-done((bf16[4096,1024]{1,0:T(8,128)(2,1)S(1)}, bf16[4096,1024]{1,0:T(8,128)(2,1)}, u32[]{:S(2)}) %copy-start.3) | copy-done | bytes 8388632
  16.3 1.8 %shard_map.74 = f32[384,512]{1,0:T(8,128)S(1)} custom-call(bf16[384,4096]{1,0:T(8,128)(2,1)S(1)} %copy-done.1, bf16[4096,1024]{1,0:T(8,128)(2,1)S(1)} %copy-done.3), custom_call_target="tpu_custom_call" | custom-call | flops 1000 | bytes 1000 | tf_op jit(solution)/shard_map/pallas_call | solution.py:26
  18.1 0.1 collective-permute-start
  18.1 1.0 %shard_map.77.rest_0_ = f32[384,256]{1,0:T(8,128)S(1)} custom-call(bf16[384,4096]{1,0:T(8,128)(2,1)S(1)} %copy-done.1, bf16[4096,1024]{1,0:T(8,128)(2,1)S(1)} %copy-done.3), custom_call_target="tpu_custom_call" | custom-call | flops 1000 | bytes 1000 | tf_op jit(solution)/shard_map/pallas_call | solution.py:26
  19.2 0.0 collective-permute-done.1.m_ref.rest_3_
  19.2 2.1 %collective-permute-start.3 = (bf16[64,4608]{1,0:T(8,128)(2,1)S(1)}, bf16[64,4608]{1,0:T(8,128)(2,1)S(1)}, u32[]{:S(2)}, u32[]{:S(2)}) collective-permute-start(bf16[64,4608]{1,0:T(8,128)(2,1)S(1)} %collective-permute-done.1.m_ref.rest_3_), channel_id=1, source_target_pairs={{0,4},{5,1},{4,8},{9,5},{8,12},{13,9},{12,14},{15,13},{14,10},{11,... | collective-permute-start | bytes 1769480 | tf_op jit(solution)/shard_map/ppermute | solution.py:172
  21.2 1.0 %shard_map.79.rest_1_ = f32[384,256]{1,0:T(8,128)S(1)} custom-call(bf16[384,4096]{1,0:T(8,128)(2,1)S(1)} %copy-done.1, bf16[4096,1024]{1,0:T(8,128)(2,1)S(1)} %copy-done.3), custom_call_target="tpu_custom_call" | custom-call | flops 1000 | bytes 1000 | tf_op jit(solution)/shard_map/pallas_call | solution.py:26
  22.3 1.0 %shard_map.78.rest_0_ = f32[384,64]{1,0:T(8,128)S(1)} custom-call(bf16[384,4096]{1,0:T(8,128)(2,1)S(1)} %copy-done.1, bf16[64,4608]{1,0:T(8,128)(2,1)S(1)} %collective-permute-done.1.m_ref.rest_3_, s32[384,128]{1,0:T(8,128)S(1)} %shard_map.73.far_ref, f32[384,64]{1,0:T(8,128)S(1)} %shard_map.76.rest_0_), custom_call_target="tpu_custom_call" | custom-call | flops 1000 | bytes 1000 | tf_op jit(solution)/shard_map/pallas_call | solution.py:26
  23.2 10.8 %collective-permute-done.m_ref.rest_4_ = bf16[64,4608]{1,0:T(8,128)(2,1)S(1)} collective-permute-done((bf16[64,4608]{1,0:T(8,128)(2,1)S(1)}, bf16[64,4608]{1,0:T(8,128)(2,1)S(1)}, u32[]{:S(2)}, u32[]{:S(2)}) %collective-permute-start) | collective-permute-done | bytes 589856 | tf_op jit(solution)/shard_map/ppermute | solution.py:173
  34.0 0.0 collective-permute-start.2
  34.0 1.0 %shard_map.80.rest_0_ = f32[384,64]{1,0:T(8,128)S(1)} custom-call(bf16[384,4096]{1,0:T(8,128)(2,1)S(1)} %copy-done.1, bf16[64,4608]{1,0:T(8,128)(2,1)S(1)} %collective-permute-done.m_ref.rest_4_, s32[384,128]{1,0:T(8,128)S(1)} %shard_map.73.far_ref, f32[384,64]{1,0:T(8,128)S(1)} %shard_map.78.rest_0_), custom_call_target="tpu_custom_call" | custom-call | flops 1000 | bytes 1000 | tf_op jit(solution)/shard_map/pallas_call | solution.py:26
  35.0 0.0 collective-permute-done.3.m_ref.rest_5_
  35.0 2.1 %collective-permute-start.5 = (bf16[64,4608]{1,0:T(8,128)(2,1)S(1)}, bf16[64,4608]{1,0:T(8,128)(2,1)S(1)}, u32[]{:S(2)}, u32[]{:S(2)}) collective-permute-start(bf16[64,4608]{1,0:T(8,128)(2,1)S(1)} %collective-permute-done.3.m_ref.rest_5_), channel_id=1, source_target_pairs={{0,4},{5,1},{4,8},{9,5},{8,12},{13,9},{12,14},{15,13},{14,10},{11,... | collective-permute-start | bytes 1769480 | tf_op jit(solution)/shard_map/ppermute | solution.py:172
  37.1 1.0 %shard_map.81.rest_0_ = f32[384,64]{1,0:T(8,128)S(1)} custom-call(bf16[384,4096]{1,0:T(8,128)(2,1)S(1)} %copy-done.1, bf16[64,4608]{1,0:T(8,128)(2,1)S(1)} %collective-permute-done.3.m_ref.rest_5_, s32[384,128]{1,0:T(8,128)S(1)} %shard_map.73.far_ref, f32[384,64]{1,0:T(8,128)S(1)} %shard_map.80.rest_0_), custom_call_target="tpu_custom_call" | custom-call | flops 1000 | bytes 1000 | tf_op jit(solution)/shard_map/pallas_call | solution.py:26
  38.0 11.1 %collective-permute-done.2.m_ref.rest_6_ = bf16[64,4608]{1,0:T(8,128)(2,1)S(1)} collective-permute-done((bf16[64,4608]{1,0:T(8,128)(2,1)S(1)}, bf16[64,4608]{1,0:T(8,128)(2,1)S(1)}, u32[]{:S(2)}, u32[]{:S(2)}) %collective-permute-start.2) | collective-permute-done | bytes 589856 | tf_op jit(solution)/shard_map/ppermute | solution.py:173
  49.2 0.5 collective-permute-start.4
  49.7 0.0 collective-permute-start.7
  49.7 1.0 %shard_map.82.rest_0_ = f32[384,64]{1,0:T(8,128)S(1)} custom-call(bf16[384,4096]{1,0:T(8,128)(2,1)S(1)} %copy-done.1, bf16[64,4608]{1,0:T(8,128)(2,1)S(1)} %collective-permute-done.2.m_ref.rest_6_, s32[384,128]{1,0:T(8,128)S(1)} %shard_map.73.far_ref, f32[384,64]{1,0:T(8,128)S(1)} %shard_map.81.rest_0_), custom_call_target="tpu_custom_call" | custom-call | flops 1000 | bytes 1000 | tf_op jit(solution)/shard_map/pallas_call | solution.py:26
  50.7 0.0 copy-start.2
  50.7 0.0 collective-permute-done.5.m_ref.rest_7_
  50.7 1.5 %collective-permute-start.8 = (bf16[32,4608]{1,0:T(8,128)(2,1)S(1)}, bf16[32,4608]{1,0:T(8,128)(2,1)S(1)}, u32[]{:S(2)}, u32[]{:S(2)}) collective-permute-start(bf16[32,4608]{1,0:T(8,128)(2,1)S(1)} %slice.6), channel_id=1, source_target_pairs={{0,4},{5,1},{4,8},{9,5},{8,12},{13,9},{12,14},{15,13},{14,10},{11,... | collective-permute-start | bytes 884744 | tf_op jit(solution)/shard_map/ppermute | solution.py:198
  52.3 1.0 %shard_map.83.rest_0_ = f32[384,64]{1,0:T(8,128)S(1)} custom-call(bf16[384,4096]{1,0:T(8,128)(2,1)S(1)} %copy-done.1, bf16[64,4608]{1,0:T(8,128)(2,1)S(1)} %collective-permute-done.5.m_ref.rest_7_, s32[384,128]{1,0:T(8,128)S(1)} %shard_map.73.far_ref, f32[384,64]{1,0:T(8,128)S(1)} %shard_map.82.rest_0_), custom_call_target="tpu_custom_call" | custom-call | flops 1000 | bytes 1000 | tf_op jit(solution)/shard_map/pallas_call | solution.py:26
  53.2 9.0 %collective-permute-done.4.m_ref.rest_8_ = bf16[64,4608]{1,0:T(8,128)(2,1)S(1)} collective-permute-done((bf16[64,4608]{1,0:T(8,128)(2,1)S(1)}, bf16[64,4608]{1,0:T(8,128)(2,1)S(1)}, u32[]{:S(2)}, u32[]{:S(2)}) %collective-permute-start.4) | collective-permute-done | bytes 589856 | tf_op jit(solution)/shard_map/ppermute | solution.py:173
  62.2 0.6 collective-permute-start.9
  62.8 1.0 %shard_map.84.own_ref = f32[384,64]{1,0:T(8,128)S(1)} custom-call(bf16[384,4096]{1,0:T(8,128)(2,1)S(1)} %copy-done.1, bf16[64,4608]{1,0:T(8,128)(2,1)S(1)} %collective-permute-done.4.m_ref.rest_8_, s32[384,128]{1,0:T(8,128)S(1)} %shard_map.73.far_ref, f32[384,64]{1,0:T(8,128)S(1)} %shard_map.83.rest_0_), custom_call_target="tpu_custom_call" | custom-call | flops 1000 | bytes 1000 | tf_op jit(solution)/shard_map/pallas_call | solution.py:26
  63.8 0.1 collective-permute-start.6
  63.9 0.0 collective-permute-done.7.there_ref
  63.9 1.4 %collective-permute-done.6.other_ref = f32[384,64]{1,0:T(8,128)S(1)} collective-permute-done((f32[384,64]{1,0:T(8,128)S(1)}, f32[384,64]{1,0:T(8,128)S(1)}, u32[]{:S(2)}, u32[]{:S(2)}) %collective-permute-start.6) | collective-permute-done | bytes 98336 | tf_op jit(solution)/shard_map/ppermute | solution.py:203
  65.3 0.6 shard_map.85.base_ref
  65.9 0.0 collective-permute-done.8.m_ref.rest_0_
  65.9 0.0 copy-done.2
  65.9 0.9 %shard_map.86.rest_0_ = f32[384,32]{1,0:T(8,128)S(1)} custom-call(bf16[384,4096]{1,0:T(8,128)(2,1)S(1)} %copy-done.2, bf16[32,4608]{1,0:T(8,128)(2,1)S(1)} %collective-permute-done.8.m_ref.rest_0_, s32[384,128]{1,0:T(8,128)S(1)} %shard_map.73.far_ref), custom_call_target="tpu_custom_call" | custom-call | flops 1000 | bytes 1000 | tf_op jit(solution)/shard_map/pallas_call | solution.py:26
  66.9 2.1 %collective-permute-done.9.m_ref.rest_1_ = bf16[32,4608]{1,0:T(8,128)(2,1)S(1)} collective-permute-done((bf16[32,4608]{1,0:T(8,128)(2,1)S(1)}, bf16[32,4608]{1,0:T(8,128)(2,1)S(1)}, u32[]{:S(2)}, u32[]{:S(2)}) %collective-permute-start.9) | collective-permute-done | bytes 294944 | tf_op jit(solution)/shard_map/ppermute | solution.py:199
  69.0 1.0 %shard_map.87.own_ref = f32[384,64]{1,0:T(8,128)S(1)} custom-call(bf16[384,4096]{1,0:T(8,128)(2,1)S(1)} %copy-done.2, bf16[32,4608]{1,0:T(8,128)(2,1)S(1)} %collective-permute-done.9.m_ref.rest_1_, s32[384,128]{1,0:T(8,128)S(1)} %shard_map.73.far_ref, f32[384,32]{1,0:T(8,128)S(1)} %shard_map.86.rest_0_), custom_call_target="tpu_custom_call" | custom-call | flops 1000 | bytes 1000 | tf_op jit(solution)/shard_map/pallas_call | solution.py:26
  70.0 0.1 collective-permute-start.10
  70.1 1.4 %collective-permute-done.10.other_ref = f32[384,64]{1,0:T(8,128)S(1)} collective-permute-done((f32[384,64]{1,0:T(8,128)S(1)}, f32[384,64]{1,0:T(8,128)S(1)}, u32[]{:S(2)}, u32[]{:S(2)}) %collective-permute-start.10) | collective-permute-done | bytes 98336 | tf_op jit(solution)/shard_map/ppermute | solution.py:224
  71.5 1.1 %shard_map.88 = bf16[384,512]{1,0:T(8,128)(2,1)} custom-call(s32[384,128]{1,0:T(8,128)S(1)} %shard_map.73.far_ref, f32[384,64]{1,0:T(8,128)S(1)} %shard_map.87.own_ref, f32[384,64]{1,0:T(8,128)S(1)} %collective-permute-done.10.other_ref, f32[384,512]{1,0:T(8,128)S(1)} %shard_map.85.base_ref, bf16[32,4608]{1,0:T(8,128)(2,1)S(1)} %collective-permute-done.8.m_ref.rest_0_, ...), custom_call_target="tpu_custom_call" | custom-call | flops 1000 | bytes 1000 | tf_op jit(solution)/shard_map/pallas_call | solution.py:26
  (2 shorter events, 0.0 us)
Async XLA Ops:
  0.0 1.0 %copy-start.4 = (bf16[1,4096,64]{1,2,0:T(8,128)(2,1)S(1)}, bf16[1,4096,64]{1,2,0:T(8,128)(2,1)}, u32[]{:S(2)}) copy-start(bf16[1,4096,64]{1,2,0:T(8,128)(2,1)} %param.11) | copy-start | bytes 1572868
  1.0 0.9 %copy-start.5 = (bf16[1,64,1024]{2,1,0:T(8,128)(2,1)S(1)}, bf16[1,64,1024]{2,1,0:T(8,128)(2,1)}, u32[]{:S(2)}) copy-start(bf16[1,64,1024]{2,1,0:T(8,128)(2,1)} %param.12) | copy-start | bytes 393220
  2.0 17.1 %collective-permute-start.1 = (bf16[64,4608]{1,0:T(8,128)(2,1)S(1)}, bf16[64,4608]{1,0:T(8,128)(2,1)S(1)}, u32[]{:S(2)}, u32[]{:S(2)}) collective-permute-start(bf16[64,4608]{1,0:T(8,128)(2,1)S(1)} %shard_map.75.m_ref.rest_2_), channel_id=1, source_target_pairs={{0,4},{5,1},{4,8},{9,5},{8,12},{13,9},{12,14},{15,13},{14,10},{11,... | collective-permute-start | bytes 1769480 | tf_op jit(solution)/shard_map/ppermute | solution.py:172
  5.9 0.7 copy-start.6
  6.6 0.7 copy-start.7
  8.1 1.9 %copy-start = (bf16[384,4096]{1,0:T(8,128)(2,1)S(1)}, bf16[384,4096]{1,0:T(8,128)(2,1)}, u32[]{:S(2)}) copy-start(bf16[384,4096]{1,0:T(8,128)(2,1)} %x_ref.16) | copy-start | bytes 9437188
  11.0 1.9 %copy-start.1 = (bf16[384,4096]{1,0:T(8,128)(2,1)S(1)}, bf16[384,4096]{1,0:T(8,128)(2,1)}, u32[]{:S(2)}) copy-start(bf16[384,4096]{1,0:T(8,128)(2,1)} %x_ref.16) | copy-start | bytes 9437188
  12.9 3.4 %copy-start.3 = (bf16[4096,1024]{1,0:T(8,128)(2,1)S(1)}, bf16[4096,1024]{1,0:T(8,128)(2,1)}, u32[]{:S(2)}) copy-start(bf16[4096,1024]{1,0:T(8,128)(2,1)} %w_ref.5) | copy-start | bytes 25165828
  18.1 15.9 %collective-permute-start = (bf16[64,4608]{1,0:T(8,128)(2,1)S(1)}, bf16[64,4608]{1,0:T(8,128)(2,1)S(1)}, u32[]{:S(2)}, u32[]{:S(2)}) collective-permute-start(bf16[64,4608]{1,0:T(8,128)(2,1)S(1)} %shard_map.75.m_ref.rest_2_), channel_id=1, source_target_pairs={{4,0},{1,5},{8,4},{5,9},{12,8},{9,13},{14,12},{13,15},{10,14},{15,... | collective-permute-start | bytes 1769480 | tf_op jit(solution)/shard_map/ppermute | solution.py:173
  19.2 15.8 %collective-permute-start.3 = (bf16[64,4608]{1,0:T(8,128)(2,1)S(1)}, bf16[64,4608]{1,0:T(8,128)(2,1)S(1)}, u32[]{:S(2)}, u32[]{:S(2)}) collective-permute-start(bf16[64,4608]{1,0:T(8,128)(2,1)S(1)} %collective-permute-done.1.m_ref.rest_3_), channel_id=1, source_target_pairs={{0,4},{5,1},{4,8},{9,5},{8,12},{13,9},{12,14},{15,13},{14,10},{11,... | collective-permute-start | bytes 1769480 | tf_op jit(solution)/shard_map/ppermute | solution.py:172
  34.0 15.2 %collective-permute-start.2 = (bf16[64,4608]{1,0:T(8,128)(2,1)S(1)}, bf16[64,4608]{1,0:T(8,128)(2,1)S(1)}, u32[]{:S(2)}, u32[]{:S(2)}) collective-permute-start(bf16[64,4608]{1,0:T(8,128)(2,1)S(1)} %collective-permute-done.m_ref.rest_4_), channel_id=1, source_target_pairs={{4,0},{1,5},{8,4},{5,9},{12,8},{9,13},{14,12},{13,15},{10,14},{15,... | collective-permute-start | bytes 1769480 | tf_op jit(solution)/shard_map/ppermute | solution.py:173
  35.0 15.7 %collective-permute-start.5 = (bf16[64,4608]{1,0:T(8,128)(2,1)S(1)}, bf16[64,4608]{1,0:T(8,128)(2,1)S(1)}, u32[]{:S(2)}, u32[]{:S(2)}) collective-permute-start(bf16[64,4608]{1,0:T(8,128)(2,1)S(1)} %collective-permute-done.3.m_ref.rest_5_), channel_id=1, source_target_pairs={{0,4},{5,1},{4,8},{9,5},{8,12},{13,9},{12,14},{15,13},{14,10},{11,... | collective-permute-start | bytes 1769480 | tf_op jit(solution)/shard_map/ppermute | solution.py:172
  49.2 13.0 %collective-permute-start.4 = (bf16[64,4608]{1,0:T(8,128)(2,1)S(1)}, bf16[64,4608]{1,0:T(8,128)(2,1)S(1)}, u32[]{:S(2)}, u32[]{:S(2)}) collective-permute-start(bf16[64,4608]{1,0:T(8,128)(2,1)S(1)} %collective-permute-done.2.m_ref.rest_6_), channel_id=1, source_target_pairs={{4,0},{1,5},{8,4},{5,9},{12,8},{9,13},{14,12},{13,15},{10,14},{15,... | collective-permute-start | bytes 1769480 | tf_op jit(solution)/shard_map/ppermute | solution.py:173
  49.7 14.2 %collective-permute-start.7 = (f32[384,512]{1,0:T(8,128)S(1)}, f32[384,512]{1,0:T(8,128)S(1)}, u32[]{:S(2)}, u32[]{:S(2)}) collective-permute-start(f32[384,512]{1,0:T(8,128)S(1)} %shard_map.74), channel_id=1, source_target_pairs={{0,1},{1,0},{2,3},{3,2},{4,5},{5,4},{6,7},{7,6},{8,9},{9,8},{10,11... | collective-permute-start | bytes 2359304 | tf_op jit(solution)/shard_map/ppermute | solution.py:161
  50.7 15.3 %copy-start.2 = (bf16[384,4096]{1,0:T(8,128)(2,1)S(1)}, bf16[384,4096]{1,0:T(8,128)(2,1)}, u32[]{:S(2)}) copy-start(bf16[384,4096]{1,0:T(8,128)(2,1)} %x_ref.16) | copy-start | bytes 9437188
  50.7 15.2 %collective-permute-start.8 = (bf16[32,4608]{1,0:T(8,128)(2,1)S(1)}, bf16[32,4608]{1,0:T(8,128)(2,1)S(1)}, u32[]{:S(2)}, u32[]{:S(2)}) collective-permute-start(bf16[32,4608]{1,0:T(8,128)(2,1)S(1)} %slice.6), channel_id=1, source_target_pairs={{0,4},{5,1},{4,8},{9,5},{8,12},{13,9},{12,14},{15,13},{14,10},{11,... | collective-permute-start | bytes 884744 | tf_op jit(solution)/shard_map/ppermute | solution.py:198
  62.2 6.8 %collective-permute-start.9 = (bf16[32,4608]{1,0:T(8,128)(2,1)S(1)}, bf16[32,4608]{1,0:T(8,128)(2,1)S(1)}, u32[]{:S(2)}, u32[]{:S(2)}) collective-permute-start(bf16[32,4608]{1,0:T(8,128)(2,1)S(1)} %slice.7), channel_id=1, source_target_pairs={{4,0},{1,5},{8,4},{5,9},{12,8},{9,13},{14,12},{13,15},{10,14},{15,... | collective-permute-start | bytes 884744 | tf_op jit(solution)/shard_map/ppermute | solution.py:199
  63.8 1.5 %collective-permute-start.6 = (f32[384,64]{1,0:T(8,128)S(1)}, f32[384,64]{1,0:T(8,128)S(1)}, u32[]{:S(2)}, u32[]{:S(2)}) collective-permute-start(f32[384,64]{1,0:T(8,128)S(1)} %shard_map.84.own_ref), channel_id=1, source_target_pairs={{0,1},{1,0},{2,3},{3,2},{4,5},{5,4},{6,7},{7,6},{8,9},{9,8},{10,11... | collective-permute-start | bytes 294920 | tf_op jit(solution)/shard_map/ppermute | solution.py:203
  70.0 1.5 %collective-permute-start.10 = (f32[384,64]{1,0:T(8,128)S(1)}, f32[384,64]{1,0:T(8,128)S(1)}, u32[]{:S(2)}, u32[]{:S(2)}) collective-permute-start(f32[384,64]{1,0:T(8,128)S(1)} %shard_map.87.own_ref), channel_id=1, source_target_pairs={{0,1},{1,0},{2,3},{3,2},{4,5},{5,4},{6,7},{7,6},{8,9},{9,8},{10,11... | collective-permute-start | bytes 294920 | tf_op jit(solution)/shard_map/ppermute | solution.py:224

commit v4 on v1

v4 whole, which is shorter than its diff:
```python
import functools

import jax
import jax.numpy as jnp
from jax import lax
from jax.experimental import pallas as pl
from jax.experimental.pallas import tpu as pltpu
from jax.sharding import PartitionSpec as P

LANES = 128
BASE_STEPS = 8
tie = lax.optimization_barrier
VMEM = pl.BlockSpec(memory_space=pltpu.VMEM)
SMEM = pl.BlockSpec(memory_space=pltpu.SMEM)
HBM = pl.BlockSpec(memory_space=pl.ANY)


def snakes(n):
    return n % 2 == 0 and n <= 16


def ring_of(n):
    if snakes(n):
        return list(range(0, n, 2)) + list(range(n - 1, 0, -2))
    return list(range(n))


def place_in(n, i):
    return jnp.where(i % 2 == 0, i // 2, n - 1 - i // 2) if snakes(n) else i


def call(kernel, outs, in_specs, *args, mib=16, scratch=(), moved=1000):
    shapes = [jax.ShapeDtypeStruct(shape, dtype) for shape, dtype in outs]
    got = pl.pallas_call(
        kernel,
        in_specs=in_specs,
        out_specs=[VMEM] * len(outs),
        out_shape=shapes,
        scratch_shapes=scratch,
        compiler_params=pltpu.CompilerParams(vmem_limit_bytes=mib << 20),
        cost_estimate=pl.CostEstimate(flops=1000, bytes_accessed=moved, transcendentals=0),
    )(*args)
    return got[0] if len(outs) == 1 else got


def pack_kernel(a_ref, b_ref, o_ref, sems):
    rank, half = a_ref.shape
    k_half, b_half = half // 2, o_ref.shape[1] - half // 2
    first = lax.axis_index("tensor") * (2 * b_half)
    copies = []
    for i in range(2):
        rows = pl.ds(i * rank, rank)
        b_first = pl.multiple_of(first + i * b_half, b_half)
        copies += [
            (a_ref.at[:, pl.ds(i * k_half, k_half)], o_ref.at[rows, pl.ds(0, k_half)]),
            (b_ref.at[:, pl.ds(b_first, b_half)], o_ref.at[rows, pl.ds(k_half, b_half)]),
        ]
    copies = [pltpu.make_async_copy(*c, sems.at[i]) for i, c in enumerate(copies)]
    for c in copies:
        c.start()
    for c in copies:
        c.wait()


def far_kernel(n, index_ref, storage_ref, o_ref):
    here = place_in(n, lax.axis_index("dp"))
    way = 1 - 2 * lax.axis_index("tensor")
    index = index_ref[...]

    def look(j, far):
        return jnp.where(index == j, lax.rem((here - place_in(n, storage_ref[j])) * way + n, n), far)

    far = lax.fori_loop(0, n, look, jnp.zeros_like(index))
    o_ref[...] = jnp.broadcast_to(far, o_ref.shape)


def base_kernel(x_hbm, w_hbm, x_ref, there_ref, here_ref, w_ref, x_sems, w_sems):
    depth = x_hbm.shape[1] // BASE_STEPS
    keys = here_ref.shape[1]
    core = lax.axis_index("tensor")
    copies = []
    for i in range(BASE_STEPS):
        k = pl.ds(i * depth, depth)
        copies.append(
            (
                pltpu.make_async_copy(x_hbm.at[:, k], x_ref.at[:, k], x_sems.at[i]),
                pltpu.make_async_copy(w_hbm.at[k, :], w_ref.at[k, :], w_sems.at[i]),
            )
        )
        for c in copies[-1]:
            c.start()
    for i in range(BASE_STEPS):
        k = pl.ds(i * depth, depth)
        for c in copies[i]:
            c.wait()
        for o_ref, side in ((there_ref, 1 - core), (here_ref, core)):
            columns = pl.ds(pl.multiple_of(side * keys, keys), keys)
            product = jnp.dot(x_ref[:, k], w_ref[k, columns], preferred_element_type=jnp.float32)
            o_ref[...] = product if i == 0 else o_ref[...] + product


def down_kernel(s, x_ref, m_ref, far_ref, *rest):
    o_ref = rest[-1]
    rank = o_ref.shape[1]
    k_half = x_ref.shape[1] // 2
    part = None
    for i in range(2):
        product = lax.dot_general(
            x_ref[:, i * k_half : (i + 1) * k_half],
            m_ref[i * rank : (i + 1) * rank, :k_half],
            (((1,), (1,)), ((), ())),
            preferred_element_type=jnp.float32,
        )
        part = product if part is None else part + product
    kept = rest[0][...] if len(rest) > 1 else 0.0
    o_ref[...] = jnp.where(far_ref[:, :rank] == s, part, kept)


def half_kernel(i, x_ref, m_ref, *rest):
    o_ref = rest[-1]
    k_half = x_ref.shape[1] // 2
    part = lax.dot_general(
        x_ref[:, i * k_half : (i + 1) * k_half],
        m_ref[:, :k_half],
        (((1,), (1,)), ((), ())),
        preferred_element_type=jnp.float32,
    )
    o_ref[...] = part + rest[0][...] if len(rest) > 1 else part


def lift(steps, far_ref, total, ups):
    high = total.astype(jnp.bfloat16)
    low = (total - high.astype(jnp.float32)).astype(jnp.bfloat16)
    rank = total.shape[1]
    far = far_ref[:, :rank]
    b_all = jnp.concatenate(ups, axis=0)
    out = None
    for part in (low, high):
        part = part.astype(jnp.float32)
        wide = jnp.concatenate([jnp.where(far == s, part, 0.0).astype(jnp.bfloat16) for s in steps], axis=1)
        product = jnp.dot(wide, b_all, preferred_element_type=jnp.float32)
        out = product if out is None else out + product
    return out


def up_kernel(steps, far_ref, own_ref, other_ref, here_ref, there_ref, *rest):
    o_ref = rest[-1]
    rank = own_ref.shape[1]
    b_half = o_ref.shape[1] // 2
    ups = []
    for m_ref in rest[:-1]:
        last = m_ref.shape[1]
        ups.append(jnp.concatenate([m_ref[:rank, last - b_half :], m_ref[rank:, last - b_half :]], axis=1))
    lifted = lift(steps, far_ref, own_ref[...] + other_ref[...], ups)
    o_ref[...] = here_ref[...] + there_ref[...] + lifted


def last_kernel(s, far_ref, own_ref, other_ref, base_ref, p_ref, q_ref, o_ref):
    first = p_ref.shape[1] - o_ref.shape[1] // 2
    ups = [jnp.concatenate([p_ref[:, first:], q_ref[:, first:]], axis=1)]
    lifted = lift([s], far_ref, own_ref[...] + other_ref[...], ups)
    o_ref[...] = (base_ref[...] + lifted).astype(jnp.bfloat16)


def shards(n, requests, adapter_index, storage_slot_index, key_base_weight, down_factor, up_factor):
    rows, half = requests.shape
    rank = down_factor.shape[2]
    keys = up_factor.shape[2]
    out_keys = keys // 2
    f32 = jnp.float32

    order = ring_of(n)
    forth, back = [], []
    for j in range(n):
        a, b = order[j], order[(j + 1) % n]
        forth += [(2 * a, 2 * b), (2 * b + 1, 2 * a + 1)]
        back += [(2 * b, 2 * a), (2 * a + 1, 2 * b + 1)]
    swap = [(0, 1), (1, 0)]
    both = ("dp", "tensor")

    own = call(
        pack_kernel,
        [((2 * rank, half // 2 + out_keys // 2), jnp.bfloat16)],
        [HBM, HBM],
        down_factor[0].T,
        up_factor[0],
        mib=16,
        scratch=[pltpu.SemaphoreType.DMA((4,))],
    )
    p = own
    opposite = n % 2 == 0 and n > 1
    rounds = (n - 1) // 2

    x, there, here = call(
        base_kernel,
        [((rows, half), jnp.bfloat16), ((rows, out_keys), f32), ((rows, out_keys), f32)],
        [HBM, HBM],
        *tie((own, requests, key_base_weight))[1:],
        mib=50,
        scratch=[
            pltpu.VMEM((half, keys), jnp.bfloat16),
            pltpu.SemaphoreType.DMA((BASE_STEPS,)),
            pltpu.SemaphoreType.DMA((BASE_STEPS,)),
        ],
    )
    there, q = tie((there, own))
    from_there = lax.ppermute(there, "tensor", swap)

    def far_of(index):
        kernel = functools.partial(far_kernel, n)
        return call(kernel, [((rows, LANES), jnp.int32)], [VMEM, SMEM], index, storage_slot_index)

    def down_of(message, s, *total, moved=1000):
        return call(
            functools.partial(down_kernel, s),
            [((rows, rank), f32)],
            [VMEM] * (3 + len(total)),
            tie((message, x))[1],
            message,
            far,
            *total,
            moved=moved,
        )

    total = None
    pieces = [(0, own)]
    for s in range(1, rounds + 1):
        p = lax.ppermute(p, both, forth)
        q = lax.ppermute(q, both, back)
        if s == 1:
            index = tie((p, adapter_index))[1]
            far = far_of(index)
            total = down_of(own, 0)
        else:
            total = down_of(pieces[-1][1], pieces[-1][0], total)
            total, p = tie((total, p))
        pieces.append((s, p))
        total = down_of(p, s, total)
        if s == min(2, rounds):
            from_there, q = tie((from_there, q))
        total, q = tie((total, q))
        pieces.append((n - s, q))
    if total is None:
        far = far_of(adapter_index)
        total = down_of(own, 0)
    else:
        total = down_of(pieces[-1][1], pieces[-1][0], total)

    if opposite:
        p = lax.ppermute(p[:rank], both, forth)
        q = lax.ppermute(q[rank:], both, back)
    other = lax.ppermute(total, "tensor", swap)
    messages = [m if n <= 16 else m[:, half // 2 :] for _, m in pieces]
    base = call(
        functools.partial(up_kernel, [s for s, _ in pieces]),
        [((rows, out_keys), f32)],
        [VMEM] * (5 + len(messages)),
        far,
        total,
        other,
        here,
        from_there,
        *messages,
        mib=32 if n > 16 else 16,
    )
    if not opposite:
        return base.astype(jnp.bfloat16)
    base, p = tie((base, p))
    total = call(functools.partial(half_kernel, 0), [((rows, rank), f32)], [VMEM] * 2, x, p)
    total, q = tie((total, q))
    total = call(functools.partial(half_kernel, 1), [((rows, rank), f32)], [VMEM] * 3, x, q, total)
    other = lax.ppermute(total, "tensor", swap)
    return call(
        functools.partial(last_kernel, n // 2),
        [((rows, out_keys), jnp.bfloat16)],
        [VMEM] * 6,
        far,
        total,
        other,
        base,
        p,
        q,
    )


def solution(mesh):
    placed = (
        P(("groups", "dp"), "tensor"),
        P(("groups", "dp"), None),
        P("groups"),
        P("tensor", None),
        P(("groups", "dp"), "tensor", None),
        P(("groups", "dp"), None, None),
    )
    n = mesh.shape["dp"]
    return jax.shard_map(
        functools.partial(shards, n),
        mesh=mesh,
        in_specs=placed,
        out_specs=P(("groups", "dp"), "tensor"),
        check_vma=False,
    )
```

time: 83.4 us -> 65 us (0.78)
  matrix products: 21.5 us -> 0 us
  Pallas kernels: 0 us -> 17.2 us
  starting transfers between devices: 22.6 us -> 10.7 us
  waiting for transfers between devices: 20.3 us -> 31.4 us
  other arithmetic: 7.54 us -> 0 us
  between operations: 5.15 us -> 0.22 us
    dot_general x13 -> x0, matrix products: 21.5 us -> none  [the longest x8 9.7 us: shards(): lax.dot_general(requests, block, (((1,), (1,)), ((), ())), preferred_elem...]
    pallas_call x0 -> x14, Pallas kernels: none -> 17.2 us  [call(): pl.pallas_call(kernel, in_specs=in_specs, out_specs=[VMEM] * len(outs), o...]
    ppermute x16 -> x11, starting transfers between devices: 22.6 us -> 10.7 us  [the longest x3 7.68 us: shards(): p = lax.ppermute(p, both, forth)]
    ppermute x16 -> x11, waiting for transfers between devices: 20.3 us -> 31.4 us  [the longest x3 26 us: shards(): q = lax.ppermute(q, both, back)]
    eq x1 -> x0, other arithmetic: 5.05 us -> none  [shards(): total = jnp.where(slot == origin, part, total)]
    unnamed x26 -> x12, local copies, waits for them, and re-layouts: 2.44 us -> 5.08 us
    concatenate x2 -> x0, other arithmetic: 1.91 us -> none  [the longest x1 1.89 us: shards(): own = jnp.concatenate([a_t, b_own], axis=1)]
    dynamic_slice x2 -> x0, local copies, waits for them, and re-layouts: 1.29 us -> none  [the longest x1 0.7 us: shards(): origin = jnp.array(order, jnp.int32)[(pos + way * s + n) % n]]
  transfers between devices with their start and end apart: 16 -> 11, of which waited for: 11 -> 7; matrix products, arithmetic and copies ran while one was open for 33% -> 0% of each run, Pallas kernels for 0% -> 24%
where the time goes in v4:
time: 65 us; the launch traced here: 64.7 us
  waiting for transfers between devices  31.4 us (48%)
  Pallas kernels  17.2 us (26%)
  starting transfers between devices  10.7 us (16%)
  local copies, waits for them, and re-layouts  5.25 us (8%)
    ppermute x3, waiting for transfers between devices, shards(): q = lax.ppermute(q, both, back)  26 us
    pallas_call x14, Pallas kernels, call(): pl.pallas_call(kernel, in_specs=in_specs, out_specs=[VMEM] * len(outs), o...  17.2 us
    ppermute x3, starting transfers between devices, shards(): p = lax.ppermute(p, both, forth)  7.68 us
    unnamed x12, local copies, waits for them, and re-layouts  5.08 us
    ppermute x2, waiting for transfers between devices, shards(): other = lax.ppermute(total, 'tensor', swap)  2.86 us
    ppermute x1, starting transfers between devices, shards(): p = lax.ppermute(p[:rank], both, forth)  1.8 us
  transfers between devices with their start and end apart: 11, of which 7 were waited for; matrix products, arithmetic and copies ran while one was open for 0% of the time, Pallas kernels for 24%

profile of v4, /device:TPU:0, one launch (start us, length us, event | category | flops | bytes accessed | tf_op | source)
XLA Modules:
  0.0 64.7 jit_solution(2878634640949294667)
XLA Ops:
  0.0 0.0 copy-start.2
  0.0 1.0 %copy-done.2 = bf16[1,4096,64]{1,2,0:T(8,128)(2,1)S(1)} copy-done((bf16[1,4096,64]{1,2,0:T(8,128)(2,1)S(1)}, bf16[1,4096,64]{1,2,0:T(8,128)(2,1)}, u32[]{:S(2)}) %copy-start.2) | copy-done | bytes 524312
  1.0 0.0 copy-start.3
  1.0 0.9 %copy-done.3 = bf16[1,64,1024]{2,1,0:T(8,128)(2,1)S(1)} copy-done((bf16[1,64,1024]{2,1,0:T(8,128)(2,1)S(1)}, bf16[1,64,1024]{2,1,0:T(8,128)(2,1)}, u32[]{:S(2)}) %copy-start.3) | copy-done | bytes 131096
  1.9 0.1 shard_map.64.m_ref.rest_0_
  2.0 0.0 copy-start.5
  2.1 0.0 copy-start.4
  2.1 3.1 %collective-permute-start = (bf16[128,2304]{1,0:T(8,128)(2,1)S(1)}, bf16[128,2304]{1,0:T(8,128)(2,1)S(1)}, u32[]{:S(2)}, u32[]{:S(2)}) collective-permute-start(bf16[128,2304]{1,0:T(8,128)(2,1)S(1)} %shard_map.64.m_ref.rest_0_), channel_id=1, source_target_pairs={{0,4},{5,1},{4,8},{9,5},{8,12},{13,9},{12,14},{15,13},{14,10},{11,... | collective-permute-start | bytes 1769480 | tf_op jit(solution)/shard_map/ppermute | solution.py:228
  5.1 6.6 %shard_map.66 = (bf16[384,4096]{1,0:T(8,128)(2,1)}, f32[384,512]{1,0:T(8,128)}, f32[384,512]{1,0:T(8,128)S(1)}) custom-call(bf16[384,4096]{1,0:T(8,128)(2,1)} %x_hbm, bf16[4096,1024]{1,0:T(8,128)(2,1)} %w_hbm), custom_call_target="tpu_custom_call" | custom-call | flops 1000 | bytes 1000 | tf_op jit(solution)/shard_map/pallas_call | solution.py:34
  11.8 0.1 collective-permute-start.1
  11.8 0.1 collective-permute-start.3
  11.9 1.3 %collective-permute-done.m_ref.rest_1_ = bf16[128,2304]{1,0:T(8,128)(2,1)S(1)} collective-permute-done((bf16[128,2304]{1,0:T(8,128)(2,1)S(1)}, bf16[128,2304]{1,0:T(8,128)(2,1)S(1)}, u32[]{:S(2)}, u32[]{:S(2)}) %collective-permute-start) | collective-permute-done | bytes 589856 | tf_op jit(solution)/shard_map/ppermute | solution.py:228
  13.2 0.0 copy-done.5
  13.2 0.1 copy.7.index_ref
  13.4 2.5 %collective-permute-start.2 = (bf16[128,2304]{1,0:T(8,128)(2,1)S(1)}, bf16[128,2304]{1,0:T(8,128)(2,1)S(1)}, u32[]{:S(2)}, u32[]{:S(2)}) collective-permute-start(bf16[128,2304]{1,0:T(8,128)(2,1)S(1)} %collective-permute-done.m_ref.rest_1_), channel_id=1, source_target_pairs={{0,4},{5,1},{4,8},{9,5},{8,12},{13,9},{12,14},{15,13},{14,10},{11,... | collective-permute-start | bytes 1769480 | tf_op jit(solution)/shard_map/ppermute | solution.py:228
  15.9 0.0 copy-done.4
  15.9 0.9 %shard_map.65.far_ref = s32[384,128]{1,0:T(8,128)S(1)} custom-call(s32[384,1]{1,0:T(8,128)S(1)} %copy.7.index_ref, s32[8]{0:T(128)S(1)} %copy-done.4), custom_call_target="tpu_custom_call" | custom-call | flops 1000 | bytes 1000 | tf_op jit(solution)/shard_map/pallas_call | solution.py:34
  16.8 0.0 copy-start
  16.9 1.9 %copy-done = bf16[384,4096]{1,0:T(8,128)(2,1)S(1)} copy-done((bf16[384,4096]{1,0:T(8,128)(2,1)S(1)}, bf16[384,4096]{1,0:T(8,128)(2,1)}, u32[]{:S(2)}) %copy-start) | copy-done | bytes 3145752
  18.7 1.0 %shard_map.67.rest_0_ = f32[384,64]{1,0:T(8,128)S(1)} custom-call(bf16[384,4096]{1,0:T(8,128)(2,1)S(1)} %copy-done, bf16[128,2304]{1,0:T(8,128)(2,1)S(1)} %shard_map.64.m_ref.rest_0_, s32[384,128]{1,0:T(8,128)S(1)} %shard_map.65.far_ref), custom_call_target="tpu_custom_call" | custom-call | flops 1000 | bytes 1000 | tf_op jit(solution)/shard_map/pallas_call | solution.py:34
  19.7 1.0 %shard_map.68.rest_0_ = f32[384,64]{1,0:T(8,128)S(1)} custom-call(bf16[384,4096]{1,0:T(8,128)(2,1)S(1)} %copy-done, bf16[128,2304]{1,0:T(8,128)(2,1)S(1)} %collective-permute-done.m_ref.rest_1_, s32[384,128]{1,0:T(8,128)S(1)} %shard_map.65.far_ref, f32[384,64]{1,0:T(8,128)S(1)} %shard_map.67.rest_0_), custom_call_target="tpu_custom_call" | custom-call | flops 1000 | bytes 1000 | tf_op jit(solution)/shard_map/pallas_call | solution.py:34
  20.7 7.3 %collective-permute-done.1.m_ref.rest_2_ = bf16[128,2304]{1,0:T(8,128)(2,1)S(1)} collective-permute-done((bf16[128,2304]{1,0:T(8,128)(2,1)S(1)}, bf16[128,2304]{1,0:T(8,128)(2,1)S(1)}, u32[]{:S(2)}, u32[]{:S(2)}) %collective-permute-start.1) | collective-permute-done | bytes 589856 | tf_op jit(solution)/shard_map/ppermute | solution.py:229
  28.0 0.0 collective-permute-start.4
  28.0 1.0 %shard_map.69.rest_0_ = f32[384,64]{1,0:T(8,128)S(1)} custom-call(bf16[384,4096]{1,0:T(8,128)(2,1)S(1)} %copy-done, bf16[128,2304]{1,0:T(8,128)(2,1)S(1)} %collective-permute-done.1.m_ref.rest_2_, s32[384,128]{1,0:T(8,128)S(1)} %shard_map.65.far_ref, f32[384,64]{1,0:T(8,128)S(1)} %shard_map.68.rest_0_), custom_call_target="tpu_custom_call" | custom-call | flops 1000 | bytes 1000 | tf_op jit(solution)/shard_map/pallas_call | solution.py:34
  29.0 0.0 collective-permute-done.2.m_ref.rest_3_
  29.0 2.1 %collective-permute-start.5 = (bf16[128,2304]{1,0:T(8,128)(2,1)S(1)}, bf16[128,2304]{1,0:T(8,128)(2,1)S(1)}, u32[]{:S(2)}, u32[]{:S(2)}) collective-permute-start(bf16[128,2304]{1,0:T(8,128)(2,1)S(1)} %collective-permute-done.2.m_ref.rest_3_), channel_id=1, source_target_pairs={{0,4},{5,1},{4,8},{9,5},{8,12},{13,9},{12,14},{15,13},{14,10},{11,... | collective-permute-start | bytes 1769480 | tf_op jit(solution)/shard_map/ppermute | solution.py:228
  31.1 1.0 %shard_map.70.rest_0_ = f32[384,64]{1,0:T(8,128)S(1)} custom-call(bf16[384,4096]{1,0:T(8,128)(2,1)S(1)} %copy-done, bf16[128,2304]{1,0:T(8,128)(2,1)S(1)} %collective-permute-done.2.m_ref.rest_3_, s32[384,128]{1,0:T(8,128)S(1)} %shard_map.65.far_ref, f32[384,64]{1,0:T(8,128)S(1)} %shard_map.69.rest_0_), custom_call_target="tpu_custom_call" | custom-call | flops 1000 | bytes 1000 | tf_op jit(solution)/shard_map/pallas_call | solution.py:34
  32.0 0.0 collective-permute-done.3.there_ref
  32.0 11.3 %collective-permute-done.4.m_ref.rest_4_ = bf16[128,2304]{1,0:T(8,128)(2,1)S(1)} collective-permute-done((bf16[128,2304]{1,0:T(8,128)(2,1)S(1)}, bf16[128,2304]{1,0:T(8,128)(2,1)S(1)}, u32[]{:S(2)}, u32[]{:S(2)}) %collective-permute-start.4) | collective-permute-done | bytes 589856 | tf_op jit(solution)/shard_map/ppermute | solution.py:229
  43.4 0.3 collective-permute-start.6
  43.6 1.0 %shard_map.71.rest_0_ = f32[384,64]{1,0:T(8,128)S(1)} custom-call(bf16[384,4096]{1,0:T(8,128)(2,1)S(1)} %copy-done, bf16[128,2304]{1,0:T(8,128)(2,1)S(1)} %collective-permute-done.4.m_ref.rest_4_, s32[384,128]{1,0:T(8,128)S(1)} %shard_map.65.far_ref, f32[384,64]{1,0:T(8,128)S(1)} %shard_map.70.rest_0_), custom_call_target="tpu_custom_call" | custom-call | flops 1000 | bytes 1000 | tf_op jit(solution)/shard_map/pallas_call | solution.py:34
  44.6 0.0 collective-permute-done.5.m_ref.rest_5_
  44.6 1.8 %collective-permute-start.8 = (bf16[64,2304]{1,0:T(8,128)(2,1)S(1)}, bf16[64,2304]{1,0:T(8,128)(2,1)S(1)}, u32[]{:S(2)}, u32[]{:S(2)}) collective-permute-start(bf16[64,2304]{1,0:T(8,128)(2,1)S(1)} %slice.6), channel_id=1, source_target_pairs={{0,4},{5,1},{4,8},{9,5},{8,12},{13,9},{12,14},{15,13},{14,10},{11,... | collective-permute-start | bytes 884744 | tf_op jit(solution)/shard_map/ppermute | solution.py:250
  46.4 1.0 %shard_map.72.rest_0_ = f32[384,64]{1,0:T(8,128)S(1)} custom-call(bf16[384,4096]{1,0:T(8,128)(2,1)S(1)} %copy-done, bf16[128,2304]{1,0:T(8,128)(2,1)S(1)} %collective-permute-done.5.m_ref.rest_5_, s32[384,128]{1,0:T(8,128)S(1)} %shard_map.65.far_ref, f32[384,64]{1,0:T(8,128)S(1)} %shard_map.71.rest_0_), custom_call_target="tpu_custom_call" | custom-call | flops 1000 | bytes 1000 | tf_op jit(solution)/shard_map/pallas_call | solution.py:34
  47.4 7.4 %collective-permute-done.6.m_ref.rest_6_ = bf16[128,2304]{1,0:T(8,128)(2,1)S(1)} collective-permute-done((bf16[128,2304]{1,0:T(8,128)(2,1)S(1)}, bf16[128,2304]{1,0:T(8,128)(2,1)S(1)}, u32[]{:S(2)}, u32[]{:S(2)}) %collective-permute-start.6) | collective-permute-done | bytes 589856 | tf_op jit(solution)/shard_map/ppermute | solution.py:229
  54.8 0.7 %collective-permute-start.9 = (bf16[64,2304]{1,0:T(8,128)(2,1)S(1)}, bf16[64,2304]{1,0:T(8,128)(2,1)S(1)}, u32[]{:S(2)}, u32[]{:S(2)}) collective-permute-start(bf16[64,2304]{1,0:T(8,128)(2,1)S(1)} %slice.7), channel_id=1, source_target_pairs={{4,0},{1,5},{8,4},{5,9},{12,8},{9,13},{14,12},{13,15},{10,14},{15,... | collective-permute-start | bytes 884744 | tf_op jit(solution)/shard_map/ppermute | solution.py:251
  55.5 1.0 %shard_map.73.own_ref = f32[384,64]{1,0:T(8,128)S(1)} custom-call(bf16[384,4096]{1,0:T(8,128)(2,1)S(1)} %copy-done, bf16[128,2304]{1,0:T(8,128)(2,1)S(1)} %collective-permute-done.6.m_ref.rest_6_, s32[384,128]{1,0:T(8,128)S(1)} %shard_map.65.far_ref, f32[384,64]{1,0:T(8,128)S(1)} %shard_map.72.rest_0_), custom_call_target="tpu_custom_call" | custom-call | flops 1000 | bytes 1000 | tf_op jit(solution)/shard_map/pallas_call | solution.py:34
  56.4 0.1 collective-permute-start.7
  56.5 1.4 %collective-permute-done.7.other_ref = f32[384,64]{1,0:T(8,128)S(1)} collective-permute-done((f32[384,64]{1,0:T(8,128)S(1)}, f32[384,64]{1,0:T(8,128)S(1)}, u32[]{:S(2)}, u32[]{:S(2)}) %collective-permute-start.7) | collective-permute-done | bytes 98336 | tf_op jit(solution)/shard_map/ppermute | solution.py:252
  57.9 0.0 copy-start.1
  57.9 0.6 shard_map.74.base_ref
  58.6 0.0 collective-permute-done.8.m_ref.p_ref
  58.6 1.2 %copy-done.1 = bf16[384,4096]{1,0:T(8,128)(2,1)S(1)} copy-done((bf16[384,4096]{1,0:T(8,128)(2,1)S(1)}, bf16[384,4096]{1,0:T(8,128)(2,1)}, u32[]{:S(2)}) %copy-start.1) | copy-done | bytes 3145752
  59.8 0.5 shard_map.75.rest_0_
  60.4 1.2 %collective-permute-done.9.m_ref.q_ref = bf16[64,2304]{1,0:T(8,128)(2,1)S(1)} collective-permute-done((bf16[64,2304]{1,0:T(8,128)(2,1)S(1)}, bf16[64,2304]{1,0:T(8,128)(2,1)S(1)}, u32[]{:S(2)}, u32[]{:S(2)}) %collective-permute-start.9) | collective-permute-done | bytes 294944 | tf_op jit(solution)/shard_map/ppermute | solution.py:251
  61.6 0.6 shard_map.76.own_ref
  62.1 0.1 collective-permute-start.10
  62.2 1.4 %collective-permute-done.10.other_ref = f32[384,64]{1,0:T(8,128)S(1)} collective-permute-done((f32[384,64]{1,0:T(8,128)S(1)}, f32[384,64]{1,0:T(8,128)S(1)}, u32[]{:S(2)}, u32[]{:S(2)}) %collective-permute-start.10) | collective-permute-done | bytes 98336 | tf_op jit(solution)/shard_map/ppermute | solution.py:272
  63.7 1.1 %shard_map.77 = bf16[384,512]{1,0:T(8,128)(2,1)} custom-call(s32[384,128]{1,0:T(8,128)S(1)} %shard_map.65.far_ref, f32[384,64]{1,0:T(8,128)S(1)} %shard_map.76.own_ref, f32[384,64]{1,0:T(8,128)S(1)} %collective-permute-done.10.other_ref, f32[384,512]{1,0:T(8,128)S(1)} %shard_map.74.base_ref, bf16[64,2304]{1,0:T(8,128)(2,1)S(1)} %collective-permute-done.8.m_ref.p_ref, ...), custom_call_target="tpu_custom_call" | custom-call | flops 1000 | bytes 1000 | tf_op jit(solution)/shard_map/pallas_call | solution.py:34
  (2 shorter events, 0.0 us)
Async XLA Ops:
  0.0 1.0 %copy-start.2 = (bf16[1,4096,64]{1,2,0:T(8,128)(2,1)S(1)}, bf16[1,4096,64]{1,2,0:T(8,128)(2,1)}, u32[]{:S(2)}) copy-start(bf16[1,4096,64]{1,2,0:T(8,128)(2,1)} %param.10) | copy-start | bytes 1572868
  1.0 0.9 %copy-start.3 = (bf16[1,64,1024]{2,1,0:T(8,128)(2,1)S(1)}, bf16[1,64,1024]{2,1,0:T(8,128)(2,1)}, u32[]{:S(2)}) copy-start(bf16[1,64,1024]{2,1,0:T(8,128)(2,1)} %param.11) | copy-start | bytes 393220
  2.0 11.2 %copy-start.5 = (s32[384,1]{0,1:T(1,128)S(1)}, s32[384,1]{0,1:T(1,128)}, u32[]{:S(2)}) copy-start(s32[384,1]{0,1:T(1,128)} %param.7) | copy-start | bytes 4612
  2.1 13.8 %copy-start.4 = (s32[8]{0:T(128)S(1)}, s32[8]{0:T(128)}, u32[]{:S(2)}) copy-start(s32[8]{0:T(128)} %storage_ref.1) | copy-start | bytes 100
  2.1 11.1 %collective-permute-start = (bf16[128,2304]{1,0:T(8,128)(2,1)S(1)}, bf16[128,2304]{1,0:T(8,128)(2,1)S(1)}, u32[]{:S(2)}, u32[]{:S(2)}) collective-permute-start(bf16[128,2304]{1,0:T(8,128)(2,1)S(1)} %shard_map.64.m_ref.rest_0_), channel_id=1, source_target_pairs={{0,4},{5,1},{4,8},{9,5},{8,12},{13,9},{12,14},{15,13},{14,10},{11,... | collective-permute-start | bytes 1769480 | tf_op jit(solution)/shard_map/ppermute | solution.py:228
  11.8 16.2 %collective-permute-start.1 = (bf16[128,2304]{1,0:T(8,128)(2,1)S(1)}, bf16[128,2304]{1,0:T(8,128)(2,1)S(1)}, u32[]{:S(2)}, u32[]{:S(2)}) collective-permute-start(bf16[128,2304]{1,0:T(8,128)(2,1)S(1)} %shard_map.64.m_ref.rest_0_), channel_id=1, source_target_pairs={{4,0},{1,5},{8,4},{5,9},{12,8},{9,13},{14,12},{13,15},{10,14},{15,... | collective-permute-start | bytes 1769480 | tf_op jit(solution)/shard_map/ppermute | solution.py:229
  11.8 20.2 %collective-permute-start.3 = (f32[384,512]{1,0:T(8,128)}, f32[384,512]{1,0:T(8,128)S(1)}, u32[]{:S(2)}, u32[]{:S(2)}) collective-permute-start(f32[384,512]{1,0:T(8,128)} %get-tuple-element.50), channel_id=1, source_target_pairs={{0,1},{1,0},{2,3},{3,2},{4,5},{5,4},{6,7},{7,6},{8,9},{9,8},{10,11... | collective-permute-start | bytes 2359304 | tf_op jit(solution)/shard_map/ppermute | solution.py:207
  13.4 15.6 %collective-permute-start.2 = (bf16[128,2304]{1,0:T(8,128)(2,1)S(1)}, bf16[128,2304]{1,0:T(8,128)(2,1)S(1)}, u32[]{:S(2)}, u32[]{:S(2)}) collective-permute-start(bf16[128,2304]{1,0:T(8,128)(2,1)S(1)} %collective-permute-done.m_ref.rest_1_), channel_id=1, source_target_pairs={{0,4},{5,1},{4,8},{9,5},{8,12},{13,9},{12,14},{15,13},{14,10},{11,... | collective-permute-start | bytes 1769480 | tf_op jit(solution)/shard_map/ppermute | solution.py:228
  16.8 1.9 %copy-start = (bf16[384,4096]{1,0:T(8,128)(2,1)S(1)}, bf16[384,4096]{1,0:T(8,128)(2,1)}, u32[]{:S(2)}) copy-start(bf16[384,4096]{1,0:T(8,128)(2,1)} %get-tuple-element.59.x_ref) | copy-start | bytes 9437188
  28.0 15.3 %collective-permute-start.4 = (bf16[128,2304]{1,0:T(8,128)(2,1)S(1)}, bf16[128,2304]{1,0:T(8,128)(2,1)S(1)}, u32[]{:S(2)}, u32[]{:S(2)}) collective-permute-start(bf16[128,2304]{1,0:T(8,128)(2,1)S(1)} %collective-permute-done.1.m_ref.rest_2_), channel_id=1, source_target_pairs={{4,0},{1,5},{8,4},{5,9},{12,8},{9,13},{14,12},{13,15},{10,14},{15,... | collective-permute-start | bytes 1769480 | tf_op jit(solution)/shard_map/ppermute | solution.py:229
  29.0 15.6 %collective-permute-start.5 = (bf16[128,2304]{1,0:T(8,128)(2,1)S(1)}, bf16[128,2304]{1,0:T(8,128)(2,1)S(1)}, u32[]{:S(2)}, u32[]{:S(2)}) collective-permute-start(bf16[128,2304]{1,0:T(8,128)(2,1)S(1)} %collective-permute-done.2.m_ref.rest_3_), channel_id=1, source_target_pairs={{0,4},{5,1},{4,8},{9,5},{8,12},{13,9},{12,14},{15,13},{14,10},{11,... | collective-permute-start | bytes 1769480 | tf_op jit(solution)/shard_map/ppermute | solution.py:228
  43.4 11.4 %collective-permute-start.6 = (bf16[128,2304]{1,0:T(8,128)(2,1)S(1)}, bf16[128,2304]{1,0:T(8,128)(2,1)S(1)}, u32[]{:S(2)}, u32[]{:S(2)}) collective-permute-start(bf16[128,2304]{1,0:T(8,128)(2,1)S(1)} %collective-permute-done.4.m_ref.rest_4_), channel_id=1, source_target_pairs={{4,0},{1,5},{8,4},{5,9},{12,8},{9,13},{14,12},{13,15},{10,14},{15,... | collective-permute-start | bytes 1769480 | tf_op jit(solution)/shard_map/ppermute | solution.py:229
  44.6 13.9 %collective-permute-start.8 = (bf16[64,2304]{1,0:T(8,128)(2,1)S(1)}, bf16[64,2304]{1,0:T(8,128)(2,1)S(1)}, u32[]{:S(2)}, u32[]{:S(2)}) collective-permute-start(bf16[64,2304]{1,0:T(8,128)(2,1)S(1)} %slice.6), channel_id=1, source_target_pairs={{0,4},{5,1},{4,8},{9,5},{8,12},{13,9},{12,14},{15,13},{14,10},{11,... | collective-permute-start | bytes 884744 | tf_op jit(solution)/shard_map/ppermute | solution.py:250
  54.8 6.8 %collective-permute-start.9 = (bf16[64,2304]{1,0:T(8,128)(2,1)S(1)}, bf16[64,2304]{1,0:T(8,128)(2,1)S(1)}, u32[]{:S(2)}, u32[]{:S(2)}) collective-permute-start(bf16[64,2304]{1,0:T(8,128)(2,1)S(1)} %slice.7), channel_id=1, source_target_pairs={{4,0},{1,5},{8,4},{5,9},{12,8},{9,13},{14,12},{13,15},{10,14},{15,... | collective-permute-start | bytes 884744 | tf_op jit(solution)/shard_map/ppermute | solution.py:251
  56.4 1.5 %collective-permute-start.7 = (f32[384,64]{1,0:T(8,128)S(1)}, f32[384,64]{1,0:T(8,128)S(1)}, u32[]{:S(2)}, u32[]{:S(2)}) collective-permute-start(f32[384,64]{1,0:T(8,128)S(1)} %shard_map.73.own_ref), channel_id=1, source_target_pairs={{0,1},{1,0},{2,3},{3,2},{4,5},{5,4},{6,7},{7,6},{8,9},{9,8},{10,11... | collective-permute-start | bytes 294920 | tf_op jit(solution)/shard_map/ppermute | solution.py:252
  57.9 1.9 %copy-start.1 = (bf16[384,4096]{1,0:T(8,128)(2,1)S(1)}, bf16[384,4096]{1,0:T(8,128)(2,1)}, u32[]{:S(2)}) copy-start(bf16[384,4096]{1,0:T(8,128)(2,1)} %get-tuple-element.59.x_ref) | copy-start | bytes 9437188
  62.1 1.5 %collective-permute-start.10 = (f32[384,64]{1,0:T(8,128)S(1)}, f32[384,64]{1,0:T(8,128)S(1)}, u32[]{:S(2)}, u32[]{:S(2)}) collective-permute-start(f32[384,64]{1,0:T(8,128)S(1)} %shard_map.76.own_ref), channel_id=1, source_target_pairs={{0,1},{1,0},{2,3},{3,2},{4,5},{5,4},{6,7},{7,6},{8,9},{9,8},{10,11... | collective-permute-start | bytes 294920 | tf_op jit(solution)/shard_map/ppermute | solution.py:272

commit v5 on v4

--- a/solution.py
+++ b/solution.py
@@ -228,9 +228,9 @@
         p = lax.ppermute(p, both, forth)
         q = lax.ppermute(q, both, back)
         if s == 1:
-            index = tie((p, adapter_index))[1]
-            far = far_of(index)
+            far = far_of(tie((there, adapter_index))[1])
             total = down_of(own, 0)
+            total, p = tie((total, p))
         else:
             total = down_of(pieces[-1][1], pieces[-1][0], total)
             total, p = tie((total, p))

time: 65 us -> 60.9 us (0.937)
  waiting for transfers between devices: 31.4 us -> 28.1 us
  starting transfers between devices: 10.7 us -> 9.88 us
    ppermute x3, waiting for transfers between devices: 26 us -> 14.4 us  [shards(): q = lax.ppermute(q, both, back)]
    ppermute x3, waiting for transfers between devices: 1.3 us -> 9.04 us  [shards(): p = lax.ppermute(p, both, forth)]
    ppermute x1, starting transfers between devices: 1.8 us -> 2.53 us  [shards(): p = lax.ppermute(p[:rank], both, forth)]
    ppermute x3, starting transfers between devices: 7.68 us -> 7.02 us  [shards(): p = lax.ppermute(p, both, forth)]
  transfers between devices with their start and end apart: 11 -> 11, of which waited for: 7 -> 8; matrix products, arithmetic and copies ran while one was open for 0% -> 0% of each run, Pallas kernels for 24% -> 26%
where the time goes in v5:
time: 60.9 us; the launch traced here: 60.6 us
  waiting for transfers between devices  28.1 us (46%)
  Pallas kernels  17.2 us (28%)
  starting transfers between devices  9.88 us (16%)
  local copies, waits for them, and re-layouts  5.26 us (9%)
    pallas_call x14, Pallas kernels, call(): pl.pallas_call(kernel, in_specs=in_specs, out_specs=[VMEM] * len(outs), o...  17.2 us
    ppermute x3, waiting for transfers between devices, shards(): q = lax.ppermute(q, both, back)  14.4 us
    ppermute x3, waiting for transfers between devices, shards(): p = lax.ppermute(p, both, forth)  9.04 us
    ppermute x3, starting transfers between devices, shards(): p = lax.ppermute(p, both, forth)  7.02 us
    unnamed x12, local copies, waits for them, and re-layouts  5.08 us
    ppermute x2, waiting for transfers between devices, shards(): other = lax.ppermute(total, 'tensor', swap)  2.86 us
    ppermute x1, starting transfers between devices, shards(): p = lax.ppermute(p[:rank], both, forth)  2.53 us
    ppermute x1, waiting for transfers between devices, shards(): q = lax.ppermute(q[rank:], both, back)  1.79 us
  transfers between devices with their start and end apart: 11, of which 8 were waited for; matrix products, arithmetic and copies ran while one was open for 0% of the time, Pallas kernels for 26%

profile of v5, /device:TPU:0, one launch (start us, length us, event | category | flops | bytes accessed | tf_op | source)
XLA Modules:
  0.0 60.6 jit_solution(7645861787377562729)
XLA Ops:
  0.0 0.0 copy-start.2
  0.0 1.0 %copy-done.2 = bf16[1,4096,64]{1,2,0:T(8,128)(2,1)S(1)} copy-done((bf16[1,4096,64]{1,2,0:T(8,128)(2,1)S(1)}, bf16[1,4096,64]{1,2,0:T(8,128)(2,1)}, u32[]{:S(2)}) %copy-start.2) | copy-done | bytes 524312
  1.0 0.0 copy-start.3
  1.0 0.9 %copy-done.3 = bf16[1,64,1024]{2,1,0:T(8,128)(2,1)S(1)} copy-done((bf16[1,64,1024]{2,1,0:T(8,128)(2,1)S(1)}, bf16[1,64,1024]{2,1,0:T(8,128)(2,1)}, u32[]{:S(2)}) %copy-start.3) | copy-done | bytes 131096
  1.9 0.1 shard_map.64.m_ref.rest_0_
  2.0 0.0 copy-start.5
  2.1 0.0 copy-start.4
  2.1 3.1 %collective-permute-start = (bf16[128,2304]{1,0:T(8,128)(2,1)S(1)}, bf16[128,2304]{1,0:T(8,128)(2,1)S(1)}, u32[]{:S(2)}, u32[]{:S(2)}) collective-permute-start(bf16[128,2304]{1,0:T(8,128)(2,1)S(1)} %shard_map.64.m_ref.rest_0_), channel_id=1, source_target_pairs={{0,4},{5,1},{4,8},{9,5},{8,12},{13,9},{12,14},{15,13},{14,10},{11,... | collective-permute-start | bytes 1769480 | tf_op jit(solution)/shard_map/ppermute | solution.py:228
  5.1 6.6 %shard_map.65 = (bf16[384,4096]{1,0:T(8,128)(2,1)}, f32[384,512]{1,0:T(8,128)}, f32[384,512]{1,0:T(8,128)S(1)}) custom-call(bf16[384,4096]{1,0:T(8,128)(2,1)} %x_hbm, bf16[4096,1024]{1,0:T(8,128)(2,1)} %w_hbm), custom_call_target="tpu_custom_call" | custom-call | flops 1000 | bytes 1000 | tf_op jit(solution)/shard_map/pallas_call | solution.py:34
  11.8 0.1 collective-permute-start.1
  11.8 0.1 collective-permute-start.3
  11.9 0.0 copy-done.5
  11.9 0.1 copy.7.index_ref
  12.1 0.0 copy-done.4
  12.1 0.9 %shard_map.66.far_ref = s32[384,128]{1,0:T(8,128)S(1)} custom-call(s32[384,1]{1,0:T(8,128)S(1)} %copy.7.index_ref, s32[8]{0:T(128)S(1)} %copy-done.4), custom_call_target="tpu_custom_call" | custom-call | flops 1000 | bytes 1000 | tf_op jit(solution)/shard_map/pallas_call | solution.py:34
  13.0 0.0 copy-start
  13.0 1.9 %copy-done = bf16[384,4096]{1,0:T(8,128)(2,1)S(1)} copy-done((bf16[384,4096]{1,0:T(8,128)(2,1)S(1)}, bf16[384,4096]{1,0:T(8,128)(2,1)}, u32[]{:S(2)}) %copy-start) | copy-done | bytes 3145752
  14.9 1.0 %shard_map.67.rest_0_ = f32[384,64]{1,0:T(8,128)S(1)} custom-call(bf16[384,4096]{1,0:T(8,128)(2,1)S(1)} %copy-done, bf16[128,2304]{1,0:T(8,128)(2,1)S(1)} %shard_map.64.m_ref.rest_0_, s32[384,128]{1,0:T(8,128)S(1)} %shard_map.66.far_ref), custom_call_target="tpu_custom_call" | custom-call | flops 1000 | bytes 1000 | tf_op jit(solution)/shard_map/pallas_call | solution.py:34
  15.9 0.0 collective-permute-done.m_ref.rest_1_
  15.9 2.0 %collective-permute-start.2 = (bf16[128,2304]{1,0:T(8,128)(2,1)S(1)}, bf16[128,2304]{1,0:T(8,128)(2,1)S(1)}, u32[]{:S(2)}, u32[]{:S(2)}) collective-permute-start(bf16[128,2304]{1,0:T(8,128)(2,1)S(1)} %collective-permute-done.m_ref.rest_1_), channel_id=1, source_target_pairs={{0,4},{5,1},{4,8},{9,5},{8,12},{13,9},{12,14},{15,13},{14,10},{11,... | collective-permute-start | bytes 1769480 | tf_op jit(solution)/shard_map/ppermute | solution.py:228
  17.9 1.0 %shard_map.68.rest_0_ = f32[384,64]{1,0:T(8,128)S(1)} custom-call(bf16[384,4096]{1,0:T(8,128)(2,1)S(1)} %copy-done, bf16[128,2304]{1,0:T(8,128)(2,1)S(1)} %collective-permute-done.m_ref.rest_1_, s32[384,128]{1,0:T(8,128)S(1)} %shard_map.66.far_ref, f32[384,64]{1,0:T(8,128)S(1)} %shard_map.67.rest_0_), custom_call_target="tpu_custom_call" | custom-call | flops 1000 | bytes 1000 | tf_op jit(solution)/shard_map/pallas_call | solution.py:34
  18.9 5.3 %collective-permute-done.1.m_ref.rest_2_ = bf16[128,2304]{1,0:T(8,128)(2,1)S(1)} collective-permute-done((bf16[128,2304]{1,0:T(8,128)(2,1)S(1)}, bf16[128,2304]{1,0:T(8,128)(2,1)S(1)}, u32[]{:S(2)}, u32[]{:S(2)}) %collective-permute-start.1) | collective-permute-done | bytes 589856 | tf_op jit(solution)/shard_map/ppermute | solution.py:229
  24.1 0.0 collective-permute-start.4
  24.1 1.0 %shard_map.69.rest_0_ = f32[384,64]{1,0:T(8,128)S(1)} custom-call(bf16[384,4096]{1,0:T(8,128)(2,1)S(1)} %copy-done, bf16[128,2304]{1,0:T(8,128)(2,1)S(1)} %collective-permute-done.1.m_ref.rest_2_, s32[384,128]{1,0:T(8,128)S(1)} %shard_map.66.far_ref, f32[384,64]{1,0:T(8,128)S(1)} %shard_map.68.rest_0_), custom_call_target="tpu_custom_call" | custom-call | flops 1000 | bytes 1000 | tf_op jit(solution)/shard_map/pallas_call | solution.py:34
  25.1 4.4 %collective-permute-done.2.m_ref.rest_3_ = bf16[128,2304]{1,0:T(8,128)(2,1)S(1)} collective-permute-done((bf16[128,2304]{1,0:T(8,128)(2,1)S(1)}, bf16[128,2304]{1,0:T(8,128)(2,1)S(1)}, u32[]{:S(2)}, u32[]{:S(2)}) %collective-permute-start.2) | collective-permute-done | bytes 589856 | tf_op jit(solution)/shard_map/ppermute | solution.py:228
  29.5 2.0 %collective-permute-start.5 = (bf16[128,2304]{1,0:T(8,128)(2,1)S(1)}, bf16[128,2304]{1,0:T(8,128)(2,1)S(1)}, u32[]{:S(2)}, u32[]{:S(2)}) collective-permute-start(bf16[128,2304]{1,0:T(8,128)(2,1)S(1)} %collective-permute-done.2.m_ref.rest_3_), channel_id=1, source_target_pairs={{0,4},{5,1},{4,8},{9,5},{8,12},{13,9},{12,14},{15,13},{14,10},{11,... | collective-permute-start | bytes 1769480 | tf_op jit(solution)/shard_map/ppermute | solution.py:228
  31.4 1.0 %shard_map.70.rest_0_ = f32[384,64]{1,0:T(8,128)S(1)} custom-call(bf16[384,4096]{1,0:T(8,128)(2,1)S(1)} %copy-done, bf16[128,2304]{1,0:T(8,128)(2,1)S(1)} %collective-permute-done.2.m_ref.rest_3_, s32[384,128]{1,0:T(8,128)S(1)} %shard_map.66.far_ref, f32[384,64]{1,0:T(8,128)S(1)} %shard_map.69.rest_0_), custom_call_target="tpu_custom_call" | custom-call | flops 1000 | bytes 1000 | tf_op jit(solution)/shard_map/pallas_call | solution.py:34
  32.4 0.0 collective-permute-done.3.there_ref
  32.4 5.2 %collective-permute-done.4.m_ref.rest_4_ = bf16[128,2304]{1,0:T(8,128)(2,1)S(1)} collective-permute-done((bf16[128,2304]{1,0:T(8,128)(2,1)S(1)}, bf16[128,2304]{1,0:T(8,128)(2,1)S(1)}, u32[]{:S(2)}, u32[]{:S(2)}) %collective-permute-start.4) | collective-permute-done | bytes 589856 | tf_op jit(solution)/shard_map/ppermute | solution.py:229
  37.6 0.0 collective-permute-start.6
  37.6 1.0 %shard_map.71.rest_0_ = f32[384,64]{1,0:T(8,128)S(1)} custom-call(bf16[384,4096]{1,0:T(8,128)(2,1)S(1)} %copy-done, bf16[128,2304]{1,0:T(8,128)(2,1)S(1)} %collective-permute-done.4.m_ref.rest_4_, s32[384,128]{1,0:T(8,128)S(1)} %shard_map.66.far_ref, f32[384,64]{1,0:T(8,128)S(1)} %shard_map.70.rest_0_), custom_call_target="tpu_custom_call" | custom-call | flops 1000 | bytes 1000 | tf_op jit(solution)/shard_map/pallas_call | solution.py:34
  38.6 4.7 %collective-permute-done.5.m_ref.rest_5_ = bf16[128,2304]{1,0:T(8,128)(2,1)S(1)} collective-permute-done((bf16[128,2304]{1,0:T(8,128)(2,1)S(1)}, bf16[128,2304]{1,0:T(8,128)(2,1)S(1)}, u32[]{:S(2)}, u32[]{:S(2)}) %collective-permute-start.5) | collective-permute-done | bytes 589856 | tf_op jit(solution)/shard_map/ppermute | solution.py:228
  43.3 2.5 %collective-permute-start.8 = (bf16[64,2304]{1,0:T(8,128)(2,1)S(1)}, bf16[64,2304]{1,0:T(8,128)(2,1)S(1)}, u32[]{:S(2)}, u32[]{:S(2)}) collective-permute-start(bf16[64,2304]{1,0:T(8,128)(2,1)S(1)} %slice.6), channel_id=1, source_target_pairs={{0,4},{5,1},{4,8},{9,5},{8,12},{13,9},{12,14},{15,13},{14,10},{11,... | collective-permute-start | bytes 884744 | tf_op jit(solution)/shard_map/ppermute | solution.py:250
  45.8 1.0 %shard_map.72.rest_0_ = f32[384,64]{1,0:T(8,128)S(1)} custom-call(bf16[384,4096]{1,0:T(8,128)(2,1)S(1)} %copy-done, bf16[128,2304]{1,0:T(8,128)(2,1)S(1)} %collective-permute-done.5.m_ref.rest_5_, s32[384,128]{1,0:T(8,128)S(1)} %shard_map.66.far_ref, f32[384,64]{1,0:T(8,128)S(1)} %shard_map.71.rest_0_), custom_call_target="tpu_custom_call" | custom-call | flops 1000 | bytes 1000 | tf_op jit(solution)/shard_map/pallas_call | solution.py:34
  46.8 3.9 %collective-permute-done.6.m_ref.rest_6_ = bf16[128,2304]{1,0:T(8,128)(2,1)S(1)} collective-permute-done((bf16[128,2304]{1,0:T(8,128)(2,1)S(1)}, bf16[128,2304]{1,0:T(8,128)(2,1)S(1)}, u32[]{:S(2)}, u32[]{:S(2)}) %collective-permute-start.6) | collective-permute-done | bytes 589856 | tf_op jit(solution)/shard_map/ppermute | solution.py:229
  50.7 0.1 collective-permute-start.9
  50.7 1.0 %shard_map.73.own_ref = f32[384,64]{1,0:T(8,128)S(1)} custom-call(bf16[384,4096]{1,0:T(8,128)(2,1)S(1)} %copy-done, bf16[128,2304]{1,0:T(8,128)(2,1)S(1)} %collective-permute-done.6.m_ref.rest_6_, s32[384,128]{1,0:T(8,128)S(1)} %shard_map.66.far_ref, f32[384,64]{1,0:T(8,128)S(1)} %shard_map.72.rest_0_), custom_call_target="tpu_custom_call" | custom-call | flops 1000 | bytes 1000 | tf_op jit(solution)/shard_map/pallas_call | solution.py:34
  51.7 0.1 collective-permute-start.7
  51.8 1.4 %collective-permute-done.7.other_ref = f32[384,64]{1,0:T(8,128)S(1)} collective-permute-done((f32[384,64]{1,0:T(8,128)S(1)}, f32[384,64]{1,0:T(8,128)S(1)}, u32[]{:S(2)}, u32[]{:S(2)}) %collective-permute-start.7) | collective-permute-done | bytes 98336 | tf_op jit(solution)/shard_map/ppermute | solution.py:252
  53.2 0.0 copy-start.1
  53.2 0.6 %shard_map.74.base_ref = f32[384,512]{1,0:T(8,128)S(1)} custom-call(s32[384,128]{1,0:T(8,128)S(1)} %shard_map.66.far_ref, f32[384,64]{1,0:T(8,128)S(1)} %shard_map.73.own_ref, f32[384,64]{1,0:T(8,128)S(1)} %collective-permute-done.7.other_ref, f32[384,512]{1,0:T(8,128)S(1)} %get-tuple-element.65.here_ref, f32[384,512]{1,0:T(8,128)S(1)} %collective-permute-done.3.there_ref, ...), custom_call_target="tpu_custom_call" | custom-call | flops 1000 | bytes 1000 | tf_op jit(solution)/shard_map/pallas_call | solution.py:34
  53.9 0.0 collective-permute-done.8.m_ref.p_ref
  53.9 1.2 %copy-done.1 = bf16[384,4096]{1,0:T(8,128)(2,1)S(1)} copy-done((bf16[384,4096]{1,0:T(8,128)(2,1)S(1)}, bf16[384,4096]{1,0:T(8,128)(2,1)}, u32[]{:S(2)}) %copy-start.1) | copy-done | bytes 3145752
  55.1 0.5 shard_map.75.rest_0_
  55.7 1.8 %collective-permute-done.9.m_ref.q_ref = bf16[64,2304]{1,0:T(8,128)(2,1)S(1)} collective-permute-done((bf16[64,2304]{1,0:T(8,128)(2,1)S(1)}, bf16[64,2304]{1,0:T(8,128)(2,1)S(1)}, u32[]{:S(2)}, u32[]{:S(2)}) %collective-permute-start.9) | collective-permute-done | bytes 294944 | tf_op jit(solution)/shard_map/ppermute | solution.py:251
  57.5 0.6 shard_map.76.own_ref
  58.0 0.1 collective-permute-start.10
  58.1 1.4 %collective-permute-done.10.other_ref = f32[384,64]{1,0:T(8,128)S(1)} collective-permute-done((f32[384,64]{1,0:T(8,128)S(1)}, f32[384,64]{1,0:T(8,128)S(1)}, u32[]{:S(2)}, u32[]{:S(2)}) %collective-permute-start.10) | collective-permute-done | bytes 98336 | tf_op jit(solution)/shard_map/ppermute | solution.py:272
  59.5 1.1 %shard_map.77 = bf16[384,512]{1,0:T(8,128)(2,1)} custom-call(s32[384,128]{1,0:T(8,128)S(1)} %shard_map.66.far_ref, f32[384,64]{1,0:T(8,128)S(1)} %shard_map.76.own_ref, f32[384,64]{1,0:T(8,128)S(1)} %collective-permute-done.10.other_ref, f32[384,512]{1,0:T(8,128)S(1)} %shard_map.74.base_ref, bf16[64,2304]{1,0:T(8,128)(2,1)S(1)} %collective-permute-done.8.m_ref.p_ref, ...), custom_call_target="tpu_custom_call" | custom-call | flops 1000 | bytes 1000 | tf_op jit(solution)/shard_map/pallas_call | solution.py:34
  (2 shorter events, 0.0 us)
Async XLA Ops:
  0.0 1.0 %copy-start.2 = (bf16[1,4096,64]{1,2,0:T(8,128)(2,1)S(1)}, bf16[1,4096,64]{1,2,0:T(8,128)(2,1)}, u32[]{:S(2)}) copy-start(bf16[1,4096,64]{1,2,0:T(8,128)(2,1)} %param.10) | copy-start | bytes 1572868
  1.0 0.9 %copy-start.3 = (bf16[1,64,1024]{2,1,0:T(8,128)(2,1)S(1)}, bf16[1,64,1024]{2,1,0:T(8,128)(2,1)}, u32[]{:S(2)}) copy-start(bf16[1,64,1024]{2,1,0:T(8,128)(2,1)} %param.11) | copy-start | bytes 393220
  2.0 9.9 %copy-start.5 = (s32[384,1]{0,1:T(1,128)S(1)}, s32[384,1]{0,1:T(1,128)}, u32[]{:S(2)}) copy-start(s32[384,1]{0,1:T(1,128)} %param.7) | copy-start | bytes 4612
  2.1 10.0 %copy-start.4 = (s32[8]{0:T(128)S(1)}, s32[8]{0:T(128)}, u32[]{:S(2)}) copy-start(s32[8]{0:T(128)} %storage_ref.1) | copy-start | bytes 100
  2.1 13.8 %collective-permute-start = (bf16[128,2304]{1,0:T(8,128)(2,1)S(1)}, bf16[128,2304]{1,0:T(8,128)(2,1)S(1)}, u32[]{:S(2)}, u32[]{:S(2)}) collective-permute-start(bf16[128,2304]{1,0:T(8,128)(2,1)S(1)} %shard_map.64.m_ref.rest_0_), channel_id=1, source_target_pairs={{0,4},{5,1},{4,8},{9,5},{8,12},{13,9},{12,14},{15,13},{14,10},{11,... | collective-permute-start | bytes 1769480 | tf_op jit(solution)/shard_map/ppermute | solution.py:228
  11.8 12.3 %collective-permute-start.1 = (bf16[128,2304]{1,0:T(8,128)(2,1)S(1)}, bf16[128,2304]{1,0:T(8,128)(2,1)S(1)}, u32[]{:S(2)}, u32[]{:S(2)}) collective-permute-start(bf16[128,2304]{1,0:T(8,128)(2,1)S(1)} %shard_map.64.m_ref.rest_0_), channel_id=1, source_target_pairs={{4,0},{1,5},{8,4},{5,9},{12,8},{9,13},{14,12},{13,15},{10,14},{15,... | collective-permute-start | bytes 1769480 | tf_op jit(solution)/shard_map/ppermute | solution.py:229
  11.8 20.5 %collective-permute-start.3 = (f32[384,512]{1,0:T(8,128)}, f32[384,512]{1,0:T(8,128)S(1)}, u32[]{:S(2)}, u32[]{:S(2)}) collective-permute-start(f32[384,512]{1,0:T(8,128)} %get-tuple-element.41), channel_id=1, source_target_pairs={{0,1},{1,0},{2,3},{3,2},{4,5},{5,4},{6,7},{7,6},{8,9},{9,8},{10,11... | collective-permute-start | bytes 2359304 | tf_op jit(solution)/shard_map/ppermute | solution.py:207
  13.0 1.9 %copy-start = (bf16[384,4096]{1,0:T(8,128)(2,1)S(1)}, bf16[384,4096]{1,0:T(8,128)(2,1)}, u32[]{:S(2)}) copy-start(bf16[384,4096]{1,0:T(8,128)(2,1)} %get-tuple-element.63.x_ref) | copy-start | bytes 9437188
  15.9 13.5 %collective-permute-start.2 = (bf16[128,2304]{1,0:T(8,128)(2,1)S(1)}, bf16[128,2304]{1,0:T(8,128)(2,1)S(1)}, u32[]{:S(2)}, u32[]{:S(2)}) collective-permute-start(bf16[128,2304]{1,0:T(8,128)(2,1)S(1)} %collective-permute-done.m_ref.rest_1_), channel_id=1, source_target_pairs={{0,4},{5,1},{4,8},{9,5},{8,12},{13,9},{12,14},{15,13},{14,10},{11,... | collective-permute-start | bytes 1769480 | tf_op jit(solution)/shard_map/ppermute | solution.py:228
  24.1 13.5 %collective-permute-start.4 = (bf16[128,2304]{1,0:T(8,128)(2,1)S(1)}, bf16[128,2304]{1,0:T(8,128)(2,1)S(1)}, u32[]{:S(2)}, u32[]{:S(2)}) collective-permute-start(bf16[128,2304]{1,0:T(8,128)(2,1)S(1)} %collective-permute-done.1.m_ref.rest_2_), channel_id=1, source_target_pairs={{4,0},{1,5},{8,4},{5,9},{12,8},{9,13},{14,12},{13,15},{10,14},{15,... | collective-permute-start | bytes 1769480 | tf_op jit(solution)/shard_map/ppermute | solution.py:229
  29.5 13.8 %collective-permute-start.5 = (bf16[128,2304]{1,0:T(8,128)(2,1)S(1)}, bf16[128,2304]{1,0:T(8,128)(2,1)S(1)}, u32[]{:S(2)}, u32[]{:S(2)}) collective-permute-start(bf16[128,2304]{1,0:T(8,128)(2,1)S(1)} %collective-permute-done.2.m_ref.rest_3_), channel_id=1, source_target_pairs={{0,4},{5,1},{4,8},{9,5},{8,12},{13,9},{12,14},{15,13},{14,10},{11,... | collective-permute-start | bytes 1769480 | tf_op jit(solution)/shard_map/ppermute | solution.py:228
  37.6 13.0 %collective-permute-start.6 = (bf16[128,2304]{1,0:T(8,128)(2,1)S(1)}, bf16[128,2304]{1,0:T(8,128)(2,1)S(1)}, u32[]{:S(2)}, u32[]{:S(2)}) collective-permute-start(bf16[128,2304]{1,0:T(8,128)(2,1)S(1)} %collective-permute-done.4.m_ref.rest_4_), channel_id=1, source_target_pairs={{4,0},{1,5},{8,4},{5,9},{12,8},{9,13},{14,12},{13,15},{10,14},{15,... | collective-permute-start | bytes 1769480 | tf_op jit(solution)/shard_map/ppermute | solution.py:229
  43.3 10.6 %collective-permute-start.8 = (bf16[64,2304]{1,0:T(8,128)(2,1)S(1)}, bf16[64,2304]{1,0:T(8,128)(2,1)S(1)}, u32[]{:S(2)}, u32[]{:S(2)}) collective-permute-start(bf16[64,2304]{1,0:T(8,128)(2,1)S(1)} %slice.6), channel_id=1, source_target_pairs={{0,4},{5,1},{4,8},{9,5},{8,12},{13,9},{12,14},{15,13},{14,10},{11,... | collective-permute-start | bytes 884744 | tf_op jit(solution)/shard_map/ppermute | solution.py:250
  50.7 6.8 %collective-permute-start.9 = (bf16[64,2304]{1,0:T(8,128)(2,1)S(1)}, bf16[64,2304]{1,0:T(8,128)(2,1)S(1)}, u32[]{:S(2)}, u32[]{:S(2)}) collective-permute-start(bf16[64,2304]{1,0:T(8,128)(2,1)S(1)} %slice.7), channel_id=1, source_target_pairs={{4,0},{1,5},{8,4},{5,9},{12,8},{9,13},{14,12},{13,15},{10,14},{15,... | collective-permute-start | bytes 884744 | tf_op jit(solution)/shard_map/ppermute | solution.py:251
  51.7 1.5 %collective-permute-start.7 = (f32[384,64]{1,0:T(8,128)S(1)}, f32[384,64]{1,0:T(8,128)S(1)}, u32[]{:S(2)}, u32[]{:S(2)}) collective-permute-start(f32[384,64]{1,0:T(8,128)S(1)} %shard_map.73.own_ref), channel_id=1, source_target_pairs={{0,1},{1,0},{2,3},{3,2},{4,5},{5,4},{6,7},{7,6},{8,9},{9,8},{10,11... | collective-permute-start | bytes 294920 | tf_op jit(solution)/shard_map/ppermute | solution.py:252
  53.2 1.9 %copy-start.1 = (bf16[384,4096]{1,0:T(8,128)(2,1)S(1)}, bf16[384,4096]{1,0:T(8,128)(2,1)}, u32[]{:S(2)}) copy-start(bf16[384,4096]{1,0:T(8,128)(2,1)} %get-tuple-element.63.x_ref) | copy-start | bytes 9437188
  58.0 1.5 %collective-permute-start.10 = (f32[384,64]{1,0:T(8,128)S(1)}, f32[384,64]{1,0:T(8,128)S(1)}, u32[]{:S(2)}, u32[]{:S(2)}) collective-permute-start(f32[384,64]{1,0:T(8,128)S(1)} %shard_map.76.own_ref), channel_id=1, source_target_pairs={{0,1},{1,0},{2,3},{3,2},{4,5},{5,4},{6,7},{7,6},{8,9},{9,8},{10,11... | collective-permute-start | bytes 294920 | tf_op jit(solution)/shard_map/ppermute | solution.py:272

commit v6 on v5

--- a/solution.py
+++ b/solution.py
@@ -9,6 +9,8 @@
 
 LANES = 128
 BASE_STEPS = 8
+BASE_MIB = 48
+PACK_MIB = 60
 tie = lax.optimization_barrier
 VMEM = pl.BlockSpec(memory_space=pltpu.VMEM)
 SMEM = pl.BlockSpec(memory_space=pltpu.SMEM)
@@ -29,12 +31,12 @@
     return jnp.where(i % 2 == 0, i // 2, n - 1 - i // 2) if snakes(n) else i
 
 
-def call(kernel, outs, in_specs, *args, mib=16, scratch=(), moved=1000):
+def call(kernel, outs, in_specs, *args, mib=16, scratch=(), moved=1000, out_space=VMEM):
     shapes = [jax.ShapeDtypeStruct(shape, dtype) for shape, dtype in outs]
     got = pl.pallas_call(
         kernel,
         in_specs=in_specs,
-        out_specs=[VMEM] * len(outs),
+        out_specs=[out_space] * len(outs),
         out_shape=shapes,
         scratch_shapes=scratch,
         compiler_params=pltpu.CompilerParams(vmem_limit_bytes=mib << 20),
@@ -74,17 +76,17 @@
     o_ref[...] = jnp.broadcast_to(far, o_ref.shape)
 
 
-def base_kernel(x_hbm, w_hbm, x_ref, there_ref, here_ref, w_ref, x_sems, w_sems):
+def base_kernel(x_hbm, w_hbm, x_ref, o_ref, w_ref, x_sems, w_sems):
     depth = x_hbm.shape[1] // BASE_STEPS
-    keys = here_ref.shape[1]
-    core = lax.axis_index("tensor")
+    keys = o_ref.shape[1]
+    columns = pl.ds(pl.multiple_of((1 - lax.axis_index("tensor")) * keys, keys), keys)
     copies = []
     for i in range(BASE_STEPS):
         k = pl.ds(i * depth, depth)
         copies.append(
             (
                 pltpu.make_async_copy(x_hbm.at[:, k], x_ref.at[:, k], x_sems.at[i]),
-                pltpu.make_async_copy(w_hbm.at[k, :], w_ref.at[k, :], w_sems.at[i]),
+                pltpu.make_async_copy(w_hbm.at[k, columns], w_ref.at[k, :], w_sems.at[i]),
             )
         )
         for c in copies[-1]:
@@ -93,21 +95,43 @@
         k = pl.ds(i * depth, depth)
         for c in copies[i]:
             c.wait()
-        for o_ref, side in ((there_ref, 1 - core), (here_ref, core)):
-            columns = pl.ds(pl.multiple_of(side * keys, keys), keys)
-            product = jnp.dot(x_ref[:, k], w_ref[k, columns], preferred_element_type=jnp.float32)
-            o_ref[...] = product if i == 0 else o_ref[...] + product
-
-
-def down_kernel(s, x_ref, m_ref, far_ref, *rest):
+        product = jnp.dot(x_ref[:, k], w_ref[k, :], preferred_element_type=jnp.float32)
+        o_ref[...] = product if i == 0 else o_ref[...] + product
+
+
+def here_kernel(x_ref, w_hbm, o_ref, w_ref, w_sems):
+    depth = x_ref.shape[1] // BASE_STEPS
+    keys = o_ref.shape[1]
+    columns = pl.ds(pl.multiple_of(lax.axis_index("tensor") * keys, keys), keys)
+    copies = []
+    for i in range(BASE_STEPS):
+        k = pl.ds(i * depth, depth)
+        copies.append(pltpu.make_async_copy(w_hbm.at[k, columns], w_ref.at[k, :], w_sems.at[i]))
+        copies[-1].start()
+    for i in range(BASE_STEPS):
+        k = pl.ds(i * depth, depth)
+        copies[i].wait()
+        product = jnp.dot(x_ref[:, k], w_ref[k, :], preferred_element_type=jnp.float32)
+        o_ref[...] = product if i == 0 else o_ref[...] + product
+
+
+def halves_of(m_refs, rank):
+    if len(m_refs) == 2:
+        return m_refs
+    return [m_refs[0].at[pl.ds(i * rank, rank), :] for i in range(2)]
+
+
+def down_kernel(s, split, x_ref, far_ref, *rest):
     o_ref = rest[-1]
     rank = o_ref.shape[1]
     k_half = x_ref.shape[1] // 2
+    m_refs = rest[: 1 + split]
+    rest = rest[1 + split :]
     part = None
-    for i in range(2):
+    for i, m_ref in enumerate(halves_of(m_refs, rank)):
         product = lax.dot_general(
             x_ref[:, i * k_half : (i + 1) * k_half],
-            m_ref[i * rank : (i + 1) * rank, :k_half],
+            m_ref[:, :k_half],
             (((1,), (1,)), ((), ())),
             preferred_element_type=jnp.float32,
         )
@@ -143,14 +167,15 @@
     return out
 
 
-def up_kernel(steps, far_ref, own_ref, other_ref, here_ref, there_ref, *rest):
+def up_kernel(steps, counts, far_ref, own_ref, other_ref, here_ref, there_ref, *rest):
     o_ref = rest[-1]
     rank = own_ref.shape[1]
     b_half = o_ref.shape[1] // 2
     ups = []
-    for m_ref in rest[:-1]:
-        last = m_ref.shape[1]
-        ups.append(jnp.concatenate([m_ref[:rank, last - b_half :], m_ref[rank:, last - b_half :]], axis=1))
+    for count in counts:
+        parts = halves_of(rest[:count], rank)
+        rest = rest[count:]
+        ups.append(jnp.concatenate([m[:, m.shape[1] - b_half :] for m in parts], axis=1))
     lifted = lift(steps, far_ref, own_ref[...] + other_ref[...], ups)
     o_ref[...] = here_ref[...] + there_ref[...] + lifted
 
@@ -184,75 +209,95 @@
         [HBM, HBM],
         down_factor[0].T,
         up_factor[0],
-        mib=16,
+        mib=PACK_MIB,
         scratch=[pltpu.SemaphoreType.DMA((4,))],
     )
     p = own
     opposite = n % 2 == 0 and n > 1
     rounds = (n - 1) // 2
 
-    x, there, here = call(
+    _, x_hbm, w_hbm = tie((own, requests, key_base_weight))
+    x, there = call(
         base_kernel,
-        [((rows, half), jnp.bfloat16), ((rows, out_keys), f32), ((rows, out_keys), f32)],
+        [((rows, half), jnp.bfloat16), ((rows, out_keys), f32)],
         [HBM, HBM],
-        *tie((own, requests, key_base_weight))[1:],
-        mib=50,
+        x_hbm,
+        w_hbm,
+        mib=BASE_MIB,
         scratch=[
-            pltpu.VMEM((half, keys), jnp.bfloat16),
+            pltpu.VMEM((half, out_keys), jnp.bfloat16),
             pltpu.SemaphoreType.DMA((BASE_STEPS,)),
             pltpu.SemaphoreType.DMA((BASE_STEPS,)),
         ],
     )
     there, q = tie((there, own))
     from_there = lax.ppermute(there, "tensor", swap)
+    here = call(
+        here_kernel,
+        [((rows, out_keys), f32)],
+        [VMEM, HBM],
+        tie((there, x))[1],
+        key_base_weight,
+        mib=BASE_MIB,
+        scratch=[pltpu.VMEM((half, out_keys), jnp.bfloat16), pltpu.SemaphoreType.DMA((BASE_STEPS,))],
+    )
 
     def far_of(index):
         kernel = functools.partial(far_kernel, n)
         return call(kernel, [((rows, LANES), jnp.int32)], [VMEM, SMEM], index, storage_slot_index)
 
-    def down_of(message, s, *total, moved=1000):
+    def down_of(message, s, *total):
         return call(
-            functools.partial(down_kernel, s),
+            functools.partial(down_kernel, s, len(message) - 1),
             [((rows, rank), f32)],
-            [VMEM] * (3 + len(total)),
-            tie((message, x))[1],
-            message,
+            [VMEM] * (2 + len(message) + len(total)),
+            tie((*message, x))[-1],
             far,
+            *message,
             *total,
-            moved=moved,
         )
 
     total = None
-    pieces = [(0, own)]
+    pieces = [(0, (own,))]
     for s in range(1, rounds + 1):
+        halved = False
+        if halved:
+            p = tuple(lax.ppermute(h, both, forth) for h in (p[:rank], p[rank:]))
+            q = tuple(lax.ppermute(h, both, back) for h in (q[rank:], q[:rank]))[::-1]
+        else:
+            p = (lax.ppermute(p, both, forth),)
+            q = (lax.ppermute(q, both, back),)
+        if s == 1:
+            far = far_of(tie((there, adapter_index))[1])
+            here, far, *p = tie((here, far, *p))
+            total = down_of((own,), 0)
+        else:
+            total = down_of(pieces[-1][1], pieces[-1][0], total)
+            total, *p = tie((total, *p))
+        pieces.append((s, tuple(p)))
+        if halved:
+            pieces.append((n - s, tuple(q)))
+            break
+        total = down_of(pieces[-1][1], s, total)
+        if s == min(2, rounds):
+            from_there, *q = tie((from_there, *q))
+        total, *q = tie((total, *q))
+        pieces.append((n - s, tuple(q)))
+        p, q = p[0], q[0]
+    if opposite:
+        p, q = tie((p, q)) if rounds else (p, q)
+        p, q = p[:rank], q[rank:]
         p = lax.ppermute(p, both, forth)
         q = lax.ppermute(q, both, back)
-        if s == 1:
-            far = far_of(tie((there, adapter_index))[1])
-            total = down_of(own, 0)
-            total, p = tie((total, p))
-        else:
-            total = down_of(pieces[-1][1], pieces[-1][0], total)
-            total, p = tie((total, p))
-        pieces.append((s, p))
-        total = down_of(p, s, total)
-        if s == min(2, rounds):
-            from_there, q = tie((from_there, q))
-        total, q = tie((total, q))
-        pieces.append((n - s, q))
     if total is None:
         far = far_of(adapter_index)
-        total = down_of(own, 0)
+        total = down_of((own,), 0)
     else:
         total = down_of(pieces[-1][1], pieces[-1][0], total)
-
-    if opposite:
-        p = lax.ppermute(p[:rank], both, forth)
-        q = lax.ppermute(q[rank:], both, back)
     other = lax.ppermute(total, "tensor", swap)
-    messages = [m if n <= 16 else m[:, half // 2 :] for _, m in pieces]
+    messages = [m if n <= 16 else m[:, half // 2 :] for _, ms in pieces for m in ms]
     base = call(
-        functools.partial(up_kernel, [s for s, _ in pieces]),
+        functools.partial(up_kernel, [s for s, _ in pieces], [len(ms) for _, ms in pieces]),
         [((rows, out_keys), f32)],
         [VMEM] * (5 + len(messages)),
         far,

time: 60.9 us -> 59.2 us (0.972)
  Pallas kernels: 17.2 us -> 25.1 us
  waiting for transfers between devices: 28.1 us -> 22.2 us
  local copies, waits for them, and re-layouts: 5.26 us -> 1.07 us
    ppermute x2 -> x6, waiting for transfers between devices: 1.79 us -> 16.7 us  [the longest x3 12.2 us: shards(): p = (lax.ppermute(p, both, forth),)]
    ppermute x3 -> x1, waiting for transfers between devices: 14.4 us -> 0.01 us  [shards(): q = lax.ppermute(q, both, back)]
    pallas_call x14 -> x15, Pallas kernels: 17.2 us -> 25.1 us  [call(): pl.pallas_call(kernel, in_specs=in_specs, out_specs=[out_space] * len(out...]
    ppermute x3 -> x1, waiting for transfers between devices: 9.04 us -> 2.59 us  [shards(): p = lax.ppermute(p, both, forth)]
    ppermute x3 -> x1, starting transfers between devices: 7.02 us -> 1.49 us  [shards(): p = lax.ppermute(p, both, forth)]
    ppermute x2 -> x6, starting transfers between devices: 2.59 us -> 8.06 us  [the longest x3 7.93 us: shards(): p = (lax.ppermute(p, both, forth),)]
    unnamed x12 -> x8, local copies, waits for them, and re-layouts: 5.08 us -> 0.89 us
  transfers between devices with their start and end apart: 11 -> 11, of which waited for: 8 -> 8; matrix products, arithmetic and copies ran while one was open for 0% -> 0% of each run, Pallas kernels for 26% -> 37%
where the time goes in v6:
time: 59.2 us; the launch traced here: 58.9 us
  Pallas kernels  25.1 us (42%)
  waiting for transfers between devices  22.2 us (38%)
  starting transfers between devices  10.4 us (18%)
  local copies, waits for them, and re-layouts  1.07 us (2%)
    pallas_call x15, Pallas kernels, call(): pl.pallas_call(kernel, in_specs=in_specs, out_specs=[out_space] * len(out...  25.1 us
    ppermute x3, waiting for transfers between devices, shards(): p = (lax.ppermute(p, both, forth),)  12.2 us
    ppermute x3, starting transfers between devices, shards(): p = (lax.ppermute(p, both, forth),)  7.93 us
    ppermute x3, waiting for transfers between devices, shards(): q = (lax.ppermute(q, both, back),)  4.55 us
    ppermute x2, waiting for transfers between devices, shards(): other = lax.ppermute(total, 'tensor', swap)  2.86 us
    ppermute x1, waiting for transfers between devices, shards(): p = lax.ppermute(p, both, forth)  2.59 us
    ppermute x1, starting transfers between devices, shards(): p = lax.ppermute(p, both, forth)  1.49 us
  transfers between devices with their start and end apart: 11, of which 8 were waited for; matrix products, arithmetic and copies ran while one was open for 0% of the time, Pallas kernels for 37%

profile of v6, /device:TPU:0, one launch (start us, length us, event | category | flops | bytes accessed | tf_op | source)
XLA Modules:
  0.0 58.9 jit_solution(14323119995058056547)
XLA Ops:
  0.0 1.9 %shard_map.64.rest_0_ = bf16[128,2304]{1,0:T(8,128)(2,1)} custom-call(bf16[64,4096]{1,0:T(8,128)(2,1)} %bitcast.4, bf16[64,1024]{1,0:T(8,128)(2,1)} %bitcast.5), custom_call_target="tpu_custom_call" | custom-call | flops 1000 | bytes 1000 | tf_op jit(solution)/shard_map/pallas_call | solution.py:36
  1.9 3.1 %collective-permute-start = (bf16[128,2304]{1,0:T(8,128)(2,1)}, bf16[128,2304]{1,0:T(8,128)(2,1)}, u32[]{:S(2)}, u32[]{:S(2)}) collective-permute-start(bf16[128,2304]{1,0:T(8,128)(2,1)} %shard_map.64.rest_0_), channel_id=1, source_target_pairs={{0,4},{5,1},{4,8},{9,5},{8,12},{13,9},{12,14},{15,13},{14,10},{11,... | collective-permute-start | bytes 1769480 | tf_op jit(solution)/shard_map/ppermute | solution.py:268
  5.0 4.5 %shard_map.65 = (bf16[384,4096]{1,0:T(8,128)(2,1)S(1)}, f32[384,512]{1,0:T(8,128)}) custom-call(bf16[384,4096]{1,0:T(8,128)(2,1)} %x_hbm, bf16[4096,1024]{1,0:T(8,128)(2,1)} %w_hbm.2), custom_call_target="tpu_custom_call" | custom-call | flops 1000 | bytes 1000 | tf_op jit(solution)/shard_map/pallas_call | solution.py:36
  9.5 0.1 collective-permute-start.1
  9.6 0.1 collective-permute-start.3
  9.7 0.0 copy-start.3
  9.7 0.0 copy-start.2
  9.7 3.3 %shard_map.66.here_ref = f32[384,512]{1,0:T(8,128)S(1)} custom-call(bf16[384,4096]{1,0:T(8,128)(2,1)S(1)} %get-tuple-element.67.x_ref, bf16[4096,1024]{1,0:T(8,128)(2,1)} %w_hbm.2), custom_call_target="tpu_custom_call" | custom-call | flops 1000 | bytes 1000 | tf_op jit(solution)/shard_map/pallas_call | solution.py:36
  13.0 0.0 copy-start
  13.0 0.9 %copy-done = f32[384,512]{1,0:T(8,128)} copy-done((f32[384,512]{1,0:T(8,128)}, f32[384,512]{1,0:T(8,128)S(1)}, u32[]{:S(2)}) %copy-start) | copy-done | bytes 786456
  13.9 0.0 copy-done.3
  13.9 0.1 copy.7.index_ref
  14.0 0.0 copy-done.2
  14.0 0.9 %shard_map.67.far_ref = s32[384,128]{1,0:T(8,128)S(1)} custom-call(s32[384,1]{1,0:T(8,128)S(1)} %copy.7.index_ref, s32[8]{0:T(128)S(1)} %copy-done.2), custom_call_target="tpu_custom_call" | custom-call | flops 1000 | bytes 1000 | tf_op jit(solution)/shard_map/pallas_call | solution.py:36
  15.0 0.5 collective-permute-done.rest_0_.rest_1_
  15.5 2.5 %collective-permute-start.2 = (bf16[128,2304]{1,0:T(8,128)(2,1)}, bf16[128,2304]{1,0:T(8,128)(2,1)S(1)}, u32[]{:S(2)}, u32[]{:S(2)}) collective-permute-start(bf16[128,2304]{1,0:T(8,128)(2,1)} %collective-permute-done.rest_0_.rest_1_), channel_id=1, source_target_pairs={{0,4},{5,1},{4,8},{9,5},{8,12},{13,9},{12,14},{15,13},{14,10},{11,... | collective-permute-start | bytes 1769480 | tf_op jit(solution)/shard_map/ppermute | solution.py:268
  18.0 2.0 %shard_map.68.rest_1_ = f32[384,64]{1,0:T(8,128)S(1)} custom-call(bf16[384,4096]{1,0:T(8,128)(2,1)S(1)} %get-tuple-element.67.x_ref, s32[384,128]{1,0:T(8,128)S(1)} %shard_map.67.far_ref, bf16[128,2304]{1,0:T(8,128)(2,1)} %shard_map.64.rest_0_), custom_call_target="tpu_custom_call" | custom-call | flops 1000 | bytes 1000 | tf_op jit(solution)/shard_map/pallas_call | solution.py:36
  20.0 2.0 %shard_map.69.rest_1_ = f32[384,64]{1,0:T(8,128)S(1)} custom-call(bf16[384,4096]{1,0:T(8,128)(2,1)S(1)} %get-tuple-element.67.x_ref, s32[384,128]{1,0:T(8,128)S(1)} %shard_map.67.far_ref, bf16[128,2304]{1,0:T(8,128)(2,1)} %collective-permute-done.rest_0_.rest_1_, f32[384,64]{1,0:T(8,128)S(1)} %shard_map.68.rest_1_), custom_call_target="tpu_custom_call" | custom-call | flops 1000 | bytes 1000 | tf_op jit(solution)/shard_map/pallas_call | solution.py:36
  22.0 0.0 collective-permute-done.1.rest_0_.rest_2_
  22.0 0.1 collective-permute-start.4
  22.1 2.0 %shard_map.70.rest_1_ = f32[384,64]{1,0:T(8,128)S(1)} custom-call(bf16[384,4096]{1,0:T(8,128)(2,1)S(1)} %get-tuple-element.67.x_ref, s32[384,128]{1,0:T(8,128)S(1)} %shard_map.67.far_ref, bf16[128,2304]{1,0:T(8,128)(2,1)} %collective-permute-done.1.rest_0_.rest_2_, f32[384,64]{1,0:T(8,128)S(1)} %shard_map.69.rest_1_), custom_call_target="tpu_custom_call" | custom-call | flops 1000 | bytes 1000 | tf_op jit(solution)/shard_map/pallas_call | solution.py:36
  24.2 5.1 %collective-permute-done.2.rest_0_.rest_3_ = bf16[128,2304]{1,0:T(8,128)(2,1)S(1)} collective-permute-done((bf16[128,2304]{1,0:T(8,128)(2,1)}, bf16[128,2304]{1,0:T(8,128)(2,1)S(1)}, u32[]{:S(2)}, u32[]{:S(2)}) %collective-permute-start.2) | collective-permute-done | bytes 589856 | tf_op jit(solution)/shard_map/ppermute | solution.py:268
  29.2 2.4 %collective-permute-start.5 = (bf16[128,2304]{1,0:T(8,128)(2,1)S(1)}, bf16[128,2304]{1,0:T(8,128)(2,1)S(1)}, u32[]{:S(2)}, u32[]{:S(2)}) collective-permute-start(bf16[128,2304]{1,0:T(8,128)(2,1)S(1)} %collective-permute-done.2.rest_0_.rest_3_), channel_id=1, source_target_pairs={{0,4},{5,1},{4,8},{9,5},{8,12},{13,9},{12,14},{15,13},{14,10},{11,... | collective-permute-start | bytes 1769480 | tf_op jit(solution)/shard_map/ppermute | solution.py:268
  31.6 1.0 %shard_map.71.rest_1_ = f32[384,64]{1,0:T(8,128)S(1)} custom-call(bf16[384,4096]{1,0:T(8,128)(2,1)S(1)} %get-tuple-element.67.x_ref, s32[384,128]{1,0:T(8,128)S(1)} %shard_map.67.far_ref, bf16[128,2304]{1,0:T(8,128)(2,1)S(1)} %collective-permute-done.2.rest_0_.rest_3_, f32[384,64]{1,0:T(8,128)S(1)} %shard_map.70.rest_1_), custom_call_target="tpu_custom_call" | custom-call | flops 1000 | bytes 1000 | tf_op jit(solution)/shard_map/pallas_call | solution.py:36
  32.6 0.0 collective-permute-done.3.there_ref
  32.6 3.2 %collective-permute-done.4.rest_0_.rest_4_ = bf16[128,2304]{1,0:T(8,128)(2,1)S(1)} collective-permute-done((bf16[128,2304]{1,0:T(8,128)(2,1)}, bf16[128,2304]{1,0:T(8,128)(2,1)S(1)}, u32[]{:S(2)}, u32[]{:S(2)}) %collective-permute-start.4) | collective-permute-done | bytes 589856 | tf_op jit(solution)/shard_map/ppermute | solution.py:269
  35.8 0.0 collective-permute-start.6
  35.8 1.0 %shard_map.72.rest_1_ = f32[384,64]{1,0:T(8,128)S(1)} custom-call(bf16[384,4096]{1,0:T(8,128)(2,1)S(1)} %get-tuple-element.67.x_ref, s32[384,128]{1,0:T(8,128)S(1)} %shard_map.67.far_ref, bf16[128,2304]{1,0:T(8,128)(2,1)S(1)} %collective-permute-done.4.rest_0_.rest_4_, f32[384,64]{1,0:T(8,128)S(1)} %shard_map.71.rest_1_), custom_call_target="tpu_custom_call" | custom-call | flops 1000 | bytes 1000 | tf_op jit(solution)/shard_map/pallas_call | solution.py:36
  36.8 6.6 %collective-permute-done.5.rest_0_.rest_5_ = bf16[128,2304]{1,0:T(8,128)(2,1)S(1)} collective-permute-done((bf16[128,2304]{1,0:T(8,128)(2,1)S(1)}, bf16[128,2304]{1,0:T(8,128)(2,1)S(1)}, u32[]{:S(2)}, u32[]{:S(2)}) %collective-permute-start.5) | collective-permute-done | bytes 589856 | tf_op jit(solution)/shard_map/ppermute | solution.py:268
  43.4 1.0 %shard_map.73.rest_1_ = f32[384,64]{1,0:T(8,128)S(1)} custom-call(bf16[384,4096]{1,0:T(8,128)(2,1)S(1)} %get-tuple-element.67.x_ref, s32[384,128]{1,0:T(8,128)S(1)} %shard_map.67.far_ref, bf16[128,2304]{1,0:T(8,128)(2,1)S(1)} %collective-permute-done.5.rest_0_.rest_5_, f32[384,64]{1,0:T(8,128)S(1)} %shard_map.72.rest_1_), custom_call_target="tpu_custom_call" | custom-call | flops 1000 | bytes 1000 | tf_op jit(solution)/shard_map/pallas_call | solution.py:36
  44.3 0.0 copy-start.1
  44.3 1.3 %collective-permute-done.6.rest_0_.rest_6_ = bf16[128,2304]{1,0:T(8,128)(2,1)S(1)} collective-permute-done((bf16[128,2304]{1,0:T(8,128)(2,1)S(1)}, bf16[128,2304]{1,0:T(8,128)(2,1)S(1)}, u32[]{:S(2)}, u32[]{:S(2)}) %collective-permute-start.6) | collective-permute-done | bytes 589856 | tf_op jit(solution)/shard_map/ppermute | solution.py:269
  45.7 1.5 %collective-permute-start.8 = (bf16[64,2304]{1,0:T(8,128)(2,1)S(1)}, bf16[64,2304]{1,0:T(8,128)(2,1)S(1)}, u32[]{:S(2)}, u32[]{:S(2)}) collective-permute-start(bf16[64,2304]{1,0:T(8,128)(2,1)S(1)} %slice.6), channel_id=1, source_target_pairs={{0,4},{5,1},{4,8},{9,5},{8,12},{13,9},{12,14},{15,13},{14,10},{11,... | collective-permute-start | bytes 884744 | tf_op jit(solution)/shard_map/ppermute | solution.py:290
  47.2 0.6 %collective-permute-start.9 = (bf16[64,2304]{1,0:T(8,128)(2,1)S(1)}, bf16[64,2304]{1,0:T(8,128)(2,1)S(1)}, u32[]{:S(2)}, u32[]{:S(2)}) collective-permute-start(bf16[64,2304]{1,0:T(8,128)(2,1)S(1)} %slice.7), channel_id=1, source_target_pairs={{4,0},{1,5},{8,4},{5,9},{12,8},{9,13},{14,12},{13,15},{10,14},{15,... | collective-permute-start | bytes 884744 | tf_op jit(solution)/shard_map/ppermute | solution.py:291
  47.9 1.0 %shard_map.74.own_ref = f32[384,64]{1,0:T(8,128)S(1)} custom-call(bf16[384,4096]{1,0:T(8,128)(2,1)S(1)} %get-tuple-element.67.x_ref, s32[384,128]{1,0:T(8,128)S(1)} %shard_map.67.far_ref, bf16[128,2304]{1,0:T(8,128)(2,1)S(1)} %collective-permute-done.6.rest_0_.rest_6_, f32[384,64]{1,0:T(8,128)S(1)} %shard_map.73.rest_1_), custom_call_target="tpu_custom_call" | custom-call | flops 1000 | bytes 1000 | tf_op jit(solution)/shard_map/pallas_call | solution.py:36
  48.8 0.1 collective-permute-start.7
  48.9 1.4 %collective-permute-done.7.other_ref = f32[384,64]{1,0:T(8,128)S(1)} collective-permute-done((f32[384,64]{1,0:T(8,128)S(1)}, f32[384,64]{1,0:T(8,128)S(1)}, u32[]{:S(2)}, u32[]{:S(2)}) %collective-permute-start.7) | collective-permute-done | bytes 98336 | tf_op jit(solution)/shard_map/ppermute | solution.py:297
  50.3 0.0 copy-done.1
  50.3 2.3 %shard_map.75.base_ref = f32[384,512]{1,0:T(8,128)S(1)} custom-call(s32[384,128]{1,0:T(8,128)S(1)} %shard_map.67.far_ref, f32[384,64]{1,0:T(8,128)S(1)} %shard_map.74.own_ref, f32[384,64]{1,0:T(8,128)S(1)} %collective-permute-done.7.other_ref, f32[384,512]{1,0:T(8,128)S(1)} %copy-done.1, f32[384,512]{1,0:T(8,128)} %collective-permute-done.3.there_ref, ...), custom_call_target="tpu_custom_call" | custom-call | flops 1000 | bytes 1000 | tf_op jit(solution)/shard_map/pallas_call | solution.py:36
  52.6 2.6 %collective-permute-done.8.m_ref.p_ref = bf16[64,2304]{1,0:T(8,128)(2,1)S(1)} collective-permute-done((bf16[64,2304]{1,0:T(8,128)(2,1)S(1)}, bf16[64,2304]{1,0:T(8,128)(2,1)S(1)}, u32[]{:S(2)}, u32[]{:S(2)}) %collective-permute-start.8) | collective-permute-done | bytes 294944 | tf_op jit(solution)/shard_map/ppermute | solution.py:290
  55.2 0.6 shard_map.76.rest_0_
  55.8 0.0 collective-permute-done.9.m_ref.q_ref
  55.8 0.6 shard_map.77.own_ref
  56.3 0.1 collective-permute-start.10
  56.4 1.4 %collective-permute-done.10.other_ref = f32[384,64]{1,0:T(8,128)S(1)} collective-permute-done((f32[384,64]{1,0:T(8,128)S(1)}, f32[384,64]{1,0:T(8,128)S(1)}, u32[]{:S(2)}, u32[]{:S(2)}) %collective-permute-start.10) | collective-permute-done | bytes 98336 | tf_op jit(solution)/shard_map/ppermute | solution.py:317
  57.8 1.1 %shard_map.78 = bf16[384,512]{1,0:T(8,128)(2,1)} custom-call(s32[384,128]{1,0:T(8,128)S(1)} %shard_map.67.far_ref, f32[384,64]{1,0:T(8,128)S(1)} %shard_map.77.own_ref, f32[384,64]{1,0:T(8,128)S(1)} %collective-permute-done.10.other_ref, f32[384,512]{1,0:T(8,128)S(1)} %shard_map.75.base_ref, bf16[64,2304]{1,0:T(8,128)(2,1)S(1)} %collective-permute-done.8.m_ref.p_ref, ...), custom_call_target="tpu_custom_call" | custom-call | flops 1000 | bytes 1000 | tf_op jit(solution)/shard_map/pallas_call | solution.py:36
  (2 shorter events, 0.0 us)
Async XLA Ops:
  1.9 13.6 %collective-permute-start = (bf16[128,2304]{1,0:T(8,128)(2,1)}, bf16[128,2304]{1,0:T(8,128)(2,1)}, u32[]{:S(2)}, u32[]{:S(2)}) collective-permute-start(bf16[128,2304]{1,0:T(8,128)(2,1)} %shard_map.64.rest_0_), channel_id=1, source_target_pairs={{0,4},{5,1},{4,8},{9,5},{8,12},{13,9},{12,14},{15,13},{14,10},{11,... | collective-permute-start | bytes 1769480 | tf_op jit(solution)/shard_map/ppermute | solution.py:268
  9.5 12.5 %collective-permute-start.1 = (bf16[128,2304]{1,0:T(8,128)(2,1)}, bf16[128,2304]{1,0:T(8,128)(2,1)}, u32[]{:S(2)}, u32[]{:S(2)}) collective-permute-start(bf16[128,2304]{1,0:T(8,128)(2,1)} %shard_map.64.rest_0_), channel_id=1, source_target_pairs={{4,0},{1,5},{8,4},{5,9},{12,8},{9,13},{14,12},{13,15},{10,14},{15,... | collective-permute-start | bytes 1769480 | tf_op jit(solution)/shard_map/ppermute | solution.py:269
  9.6 23.0 %collective-permute-start.3 = (f32[384,512]{1,0:T(8,128)}, f32[384,512]{1,0:T(8,128)}, u32[]{:S(2)}, u32[]{:S(2)}) collective-permute-start(f32[384,512]{1,0:T(8,128)} %get-tuple-element.44), channel_id=1, source_target_pairs={{0,1},{1,0},{2,3},{3,2},{4,5},{5,4},{6,7},{7,6},{8,9},{9,8},{10,11... | collective-permute-start | bytes 2359304 | tf_op jit(solution)/shard_map/ppermute | solution.py:234
  9.7 4.2 %copy-start.3 = (s32[384,1]{0,1:T(1,128)S(1)}, s32[384,1]{0,1:T(1,128)}, u32[]{:S(2)}) copy-start(s32[384,1]{0,1:T(1,128)} %param.7) | copy-start | bytes 4612
  9.7 4.3 %copy-start.2 = (s32[8]{0:T(128)S(1)}, s32[8]{0:T(128)}, u32[]{:S(2)}) copy-start(s32[8]{0:T(128)} %storage_ref.1) | copy-start | bytes 100
  13.0 0.9 %copy-start = (f32[384,512]{1,0:T(8,128)}, f32[384,512]{1,0:T(8,128)S(1)}, u32[]{:S(2)}) copy-start(f32[384,512]{1,0:T(8,128)S(1)} %shard_map.66.here_ref) | copy-start | bytes 2359300
  15.5 13.8 %collective-permute-start.2 = (bf16[128,2304]{1,0:T(8,128)(2,1)}, bf16[128,2304]{1,0:T(8,128)(2,1)S(1)}, u32[]{:S(2)}, u32[]{:S(2)}) collective-permute-start(bf16[128,2304]{1,0:T(8,128)(2,1)} %collective-permute-done.rest_0_.rest_1_), channel_id=1, source_target_pairs={{0,4},{5,1},{4,8},{9,5},{8,12},{13,9},{12,14},{15,13},{14,10},{11,... | collective-permute-start | bytes 1769480 | tf_op jit(solution)/shard_map/ppermute | solution.py:268
  22.0 13.8 %collective-permute-start.4 = (bf16[128,2304]{1,0:T(8,128)(2,1)}, bf16[128,2304]{1,0:T(8,128)(2,1)S(1)}, u32[]{:S(2)}, u32[]{:S(2)}) collective-permute-start(bf16[128,2304]{1,0:T(8,128)(2,1)} %collective-permute-done.1.rest_0_.rest_2_), channel_id=1, source_target_pairs={{4,0},{1,5},{8,4},{5,9},{12,8},{9,13},{14,12},{13,15},{10,14},{15,... | collective-permute-start | bytes 1769480 | tf_op jit(solution)/shard_map/ppermute | solution.py:269
  29.2 14.1 %collective-permute-start.5 = (bf16[128,2304]{1,0:T(8,128)(2,1)S(1)}, bf16[128,2304]{1,0:T(8,128)(2,1)S(1)}, u32[]{:S(2)}, u32[]{:S(2)}) collective-permute-start(bf16[128,2304]{1,0:T(8,128)(2,1)S(1)} %collective-permute-done.2.rest_0_.rest_3_), channel_id=1, source_target_pairs={{0,4},{5,1},{4,8},{9,5},{8,12},{13,9},{12,14},{15,13},{14,10},{11,... | collective-permute-start | bytes 1769480 | tf_op jit(solution)/shard_map/ppermute | solution.py:268
  35.8 9.9 %collective-permute-start.6 = (bf16[128,2304]{1,0:T(8,128)(2,1)S(1)}, bf16[128,2304]{1,0:T(8,128)(2,1)S(1)}, u32[]{:S(2)}, u32[]{:S(2)}) collective-permute-start(bf16[128,2304]{1,0:T(8,128)(2,1)S(1)} %collective-permute-done.4.rest_0_.rest_4_), channel_id=1, source_target_pairs={{4,0},{1,5},{8,4},{5,9},{12,8},{9,13},{14,12},{13,15},{10,14},{15,... | collective-permute-start | bytes 1769480 | tf_op jit(solution)/shard_map/ppermute | solution.py:269
  44.3 6.0 %copy-start.1 = (f32[384,512]{1,0:T(8,128)S(1)}, f32[384,512]{1,0:T(8,128)}, u32[]{:S(2)}) copy-start(f32[384,512]{1,0:T(8,128)} %copy-done) | copy-start | bytes 2359300
  45.7 9.5 %collective-permute-start.8 = (bf16[64,2304]{1,0:T(8,128)(2,1)S(1)}, bf16[64,2304]{1,0:T(8,128)(2,1)S(1)}, u32[]{:S(2)}, u32[]{:S(2)}) collective-permute-start(bf16[64,2304]{1,0:T(8,128)(2,1)S(1)} %slice.6), channel_id=1, source_target_pairs={{0,4},{5,1},{4,8},{9,5},{8,12},{13,9},{12,14},{15,13},{14,10},{11,... | collective-permute-start | bytes 884744 | tf_op jit(solution)/shard_map/ppermute | solution.py:290
  47.2 8.6 %collective-permute-start.9 = (bf16[64,2304]{1,0:T(8,128)(2,1)S(1)}, bf16[64,2304]{1,0:T(8,128)(2,1)S(1)}, u32[]{:S(2)}, u32[]{:S(2)}) collective-permute-start(bf16[64,2304]{1,0:T(8,128)(2,1)S(1)} %slice.7), channel_id=1, source_target_pairs={{4,0},{1,5},{8,4},{5,9},{12,8},{9,13},{14,12},{13,15},{10,14},{15,... | collective-permute-start | bytes 884744 | tf_op jit(solution)/shard_map/ppermute | solution.py:291
  48.8 1.5 %collective-permute-start.7 = (f32[384,64]{1,0:T(8,128)S(1)}, f32[384,64]{1,0:T(8,128)S(1)}, u32[]{:S(2)}, u32[]{:S(2)}) collective-permute-start(f32[384,64]{1,0:T(8,128)S(1)} %shard_map.74.own_ref), channel_id=1, source_target_pairs={{0,1},{1,0},{2,3},{3,2},{4,5},{5,4},{6,7},{7,6},{8,9},{9,8},{10,11... | collective-permute-start | bytes 294920 | tf_op jit(solution)/shard_map/ppermute | solution.py:297
  56.3 1.5 %collective-permute-start.10 = (f32[384,64]{1,0:T(8,128)S(1)}, f32[384,64]{1,0:T(8,128)S(1)}, u32[]{:S(2)}, u32[]{:S(2)}) collective-permute-start(f32[384,64]{1,0:T(8,128)S(1)} %shard_map.77.own_ref), channel_id=1, source_target_pairs={{0,1},{1,0},{2,3},{3,2},{4,5},{5,4},{6,7},{7,6},{8,9},{9,8},{10,11... | collective-permute-start | bytes 294920 | tf_op jit(solution)/shard_map/ppermute | solution.py:317

commit v7 on v6

--- a/solution.py
+++ b/solution.py
@@ -140,7 +140,7 @@
     o_ref[...] = jnp.where(far_ref[:, :rank] == s, part, kept)
 
 
-def half_kernel(i, x_ref, m_ref, *rest):
+def half_kernel(i, s, x_ref, far_ref, m_ref, *rest):
     o_ref = rest[-1]
     k_half = x_ref.shape[1] // 2
     part = lax.dot_general(
@@ -149,7 +149,10 @@
         (((1,), (1,)), ((), ())),
         preferred_element_type=jnp.float32,
     )
-    o_ref[...] = part + rest[0][...] if len(rest) > 1 else part
+    if i == 1:
+        kept = rest[1][...] if len(rest) > 2 else 0.0
+        part = jnp.where(far_ref[:, : part.shape[1]] == s, part + rest[0][...], kept)
+    o_ref[...] = part
 
 
 def lift(steps, far_ref, total, ups):
@@ -167,23 +170,26 @@
     return out
 
 
+def ups_of(counts, refs, rank, keys):
+    ups = []
+    for count in counts:
+        parts = halves_of(refs[:count], rank)
+        refs = refs[count:]
+        ups.append(jnp.concatenate([m[:, m.shape[1] - keys // 2 :] for m in parts], axis=1))
+    return ups
+
+
 def up_kernel(steps, counts, far_ref, own_ref, other_ref, here_ref, there_ref, *rest):
     o_ref = rest[-1]
-    rank = own_ref.shape[1]
-    b_half = o_ref.shape[1] // 2
-    ups = []
-    for count in counts:
-        parts = halves_of(rest[:count], rank)
-        rest = rest[count:]
-        ups.append(jnp.concatenate([m[:, m.shape[1] - b_half :] for m in parts], axis=1))
+    ups = ups_of(counts, rest[:-1], own_ref.shape[1], o_ref.shape[1])
     lifted = lift(steps, far_ref, own_ref[...] + other_ref[...], ups)
     o_ref[...] = here_ref[...] + there_ref[...] + lifted
 
 
-def last_kernel(s, far_ref, own_ref, other_ref, base_ref, p_ref, q_ref, o_ref):
-    first = p_ref.shape[1] - o_ref.shape[1] // 2
-    ups = [jnp.concatenate([p_ref[:, first:], q_ref[:, first:]], axis=1)]
-    lifted = lift([s], far_ref, own_ref[...] + other_ref[...], ups)
+def last_kernel(steps, counts, far_ref, own_ref, other_ref, base_ref, *rest):
+    o_ref = rest[-1]
+    ups = ups_of(counts, rest[:-1], own_ref.shape[1], o_ref.shape[1])
+    lifted = lift(steps, far_ref, own_ref[...] + other_ref[...], ups)
     o_ref[...] = (base_ref[...] + lifted).astype(jnp.bfloat16)
 
 
@@ -260,9 +266,9 @@
     total = None
     pieces = [(0, (own,))]
     for s in range(1, rounds + 1):
-        halved = False
+        halved = opposite and s == rounds and s > 1
         if halved:
-            p = tuple(lax.ppermute(h, both, forth) for h in (p[:rank], p[rank:]))
+            p = (lax.ppermute(p, both, forth),)
             q = tuple(lax.ppermute(h, both, back) for h in (q[rank:], q[:rank]))[::-1]
         else:
             p = (lax.ppermute(p, both, forth),)
@@ -284,15 +290,19 @@
         total, *q = tie((total, *q))
         pieces.append((n - s, tuple(q)))
         p, q = p[0], q[0]
+    late = pieces[-2:] if opposite and rounds > 1 else []
+    if late:
+        pieces = pieces[:-2]
     if opposite:
-        p, q = tie((p, q)) if rounds else (p, q)
-        p, q = p[:rank], q[rank:]
+        p = (p[0] if late else p)[:rank]
+        q = q[1] if late else q[rank:]
+        total, q = tie((total, q)) if late else (total, q)
         p = lax.ppermute(p, both, forth)
         q = lax.ppermute(q, both, back)
     if total is None:
         far = far_of(adapter_index)
         total = down_of((own,), 0)
-    else:
+    elif not late:
         total = down_of(pieces[-1][1], pieces[-1][0], total)
     other = lax.ppermute(total, "tensor", swap)
     messages = [m if n <= 16 else m[:, half // 2 :] for _, ms in pieces for m in ms]
@@ -310,21 +320,36 @@
     )
     if not opposite:
         return base.astype(jnp.bfloat16)
-    base, p = tie((base, p))
-    total = call(functools.partial(half_kernel, 0), [((rows, rank), f32)], [VMEM] * 2, x, p)
-    total, q = tie((total, q))
-    total = call(functools.partial(half_kernel, 1), [((rows, rank), f32)], [VMEM] * 3, x, q, total)
+    kept = []
+    for i, (s, message) in enumerate(late):
+        if i:
+            base, *message = tie((base, *message))
+        kept = [down_of(tuple(message), s, *kept)]
+    base, p, *kept = tie((base, p, *kept))
+    first = call(functools.partial(half_kernel, 0, n // 2), [((rows, rank), f32)], [VMEM] * 3, x, far, p)
+    first, q = tie((first, q))
+    total = call(
+        functools.partial(half_kernel, 1, n // 2),
+        [((rows, rank), f32)],
+        [VMEM] * (4 + len(kept)),
+        x,
+        far,
+        q,
+        first,
+        *kept,
+    )
     other = lax.ppermute(total, "tensor", swap)
+    late = late + [(n // 2, (p, q))]
+    messages = [m for _, ms in late for m in ms]
     return call(
-        functools.partial(last_kernel, n // 2),
+        functools.partial(last_kernel, [s for s, _ in late], [len(ms) for _, ms in late]),
         [((rows, out_keys), jnp.bfloat16)],
-        [VMEM] * 6,
+        [VMEM] * (4 + len(messages)),
         far,
         total,
         other,
         base,
-        p,
-        q,
+        *messages,
     )
 
 

time: 59.2 us -> 56.6 us (0.956)
  waiting for transfers between devices: 22.2 us -> 18.2 us
  starting transfers between devices: 10.4 us -> 11.7 us
    ppermute x3, waiting for transfers between devices: 12.2 us -> 9.15 us  [shards(): p = (lax.ppermute(p, both, forth),)]
    ppermute x1, waiting for transfers between devices: 2.59 us -> 0.9 us  [shards(): p = lax.ppermute(p, both, forth)]
    ppermute x0 -> x2, waiting for transfers between devices: none -> 1.3 us  [shards(): q = tuple((lax.ppermute(h, both, back) for h in (q[rank:], q[:rank])))[::-1]]
    ppermute x1, starting transfers between devices: 1.49 us -> 2.53 us  [shards(): p = lax.ppermute(p, both, forth)]
    ppermute x0 -> x2, starting transfers between devices: none -> 0.98 us  [shards(): q = tuple((lax.ppermute(h, both, back) for h in (q[rank:], q[:rank])))[::-1]]
    ppermute x2, waiting for transfers between devices: 2.86 us -> 1.9 us  [shards(): other = lax.ppermute(total, 'tensor', swap)]
    ppermute x1, waiting for transfers between devices: 0.01 us -> 0.73 us  [shards(): q = lax.ppermute(q, both, back)]
    ppermute x1, starting transfers between devices: 0.64 us -> 0.01 us  [shards(): q = lax.ppermute(q, both, back)]
  transfers between devices with their start and end apart: 11 -> 12, of which waited for: 8 -> 10; matrix products, arithmetic and copies ran while one was open for 0% -> 0% of each run, Pallas kernels for 37% -> 38%
where the time goes in v7:
time: 56.6 us; the launch traced here: 56.3 us
  Pallas kernels  25.1 us (44%)
  waiting for transfers between devices  18.2 us (32%)
  starting transfers between devices  11.7 us (21%)
  local copies, waits for them, and re-layouts  1.09 us (2%)
    pallas_call x15, Pallas kernels, call(): pl.pallas_call(kernel, in_specs=in_specs, out_specs=[out_space] * len(out...  25.1 us
    ppermute x3, waiting for transfers between devices, shards(): p = (lax.ppermute(p, both, forth),)  9.15 us
    ppermute x3, starting transfers between devices, shards(): p = (lax.ppermute(p, both, forth),)  7.93 us
    ppermute x2, waiting for transfers between devices, shards(): q = (lax.ppermute(q, both, back),)  4.17 us
    ppermute x1, starting transfers between devices, shards(): p = lax.ppermute(p, both, forth)  2.53 us
    ppermute x2, waiting for transfers between devices, shards(): other = lax.ppermute(total, 'tensor', swap)  1.9 us
    ppermute x2, waiting for transfers between devices, shards(): q = tuple((lax.ppermute(h, both, back) for h in (q[rank:], q[:rank])))[::-1]  1.3 us
  transfers between devices with their start and end apart: 12, of which 10 were waited for; matrix products, arithmetic and copies ran while one was open for 0% of the time, Pallas kernels for 38%

profile of v7, /device:TPU:0, one launch (start us, length us, event | category | flops | bytes accessed | tf_op | source)
XLA Modules:
  0.0 56.3 jit_solution(9202738102842549463)
XLA Ops:
  0.0 1.9 %shard_map.64.rest_0_ = bf16[128,2304]{1,0:T(8,128)(2,1)} custom-call(bf16[64,4096]{1,0:T(8,128)(2,1)} %bitcast.4, bf16[64,1024]{1,0:T(8,128)(2,1)} %bitcast.5), custom_call_target="tpu_custom_call" | custom-call | flops 1000 | bytes 1000 | tf_op jit(solution)/shard_map/pallas_call | solution.py:36
  1.9 3.1 %collective-permute-start = (bf16[128,2304]{1,0:T(8,128)(2,1)}, bf16[128,2304]{1,0:T(8,128)(2,1)}, u32[]{:S(2)}, u32[]{:S(2)}) collective-permute-start(bf16[128,2304]{1,0:T(8,128)(2,1)} %shard_map.64.rest_0_), channel_id=1, source_target_pairs={{0,4},{5,1},{4,8},{9,5},{8,12},{13,9},{12,14},{15,13},{14,10},{11,... | collective-permute-start | bytes 1769480 | tf_op jit(solution)/shard_map/ppermute | solution.py:274
  5.0 4.5 %shard_map.65 = (bf16[384,4096]{1,0:T(8,128)(2,1)S(1)}, f32[384,512]{1,0:T(8,128)}) custom-call(bf16[384,4096]{1,0:T(8,128)(2,1)} %x_hbm, bf16[4096,1024]{1,0:T(8,128)(2,1)} %w_hbm.2), custom_call_target="tpu_custom_call" | custom-call | flops 1000 | bytes 1000 | tf_op jit(solution)/shard_map/pallas_call | solution.py:36
  9.5 0.1 collective-permute-start.1
  9.6 0.1 collective-permute-start.3
  9.7 0.0 copy-start.3
  9.7 0.0 copy-start.2
  9.7 3.3 %shard_map.66.here_ref = f32[384,512]{1,0:T(8,128)S(1)} custom-call(bf16[384,4096]{1,0:T(8,128)(2,1)S(1)} %get-tuple-element.74.x_ref, bf16[4096,1024]{1,0:T(8,128)(2,1)} %w_hbm.2), custom_call_target="tpu_custom_call" | custom-call | flops 1000 | bytes 1000 | tf_op jit(solution)/shard_map/pallas_call | solution.py:36
  13.0 0.0 copy-start
  13.0 0.9 %copy-done = f32[384,512]{1,0:T(8,128)} copy-done((f32[384,512]{1,0:T(8,128)}, f32[384,512]{1,0:T(8,128)S(1)}, u32[]{:S(2)}) %copy-start) | copy-done | bytes 786456
  13.9 0.0 copy-done.3
  13.9 0.1 copy.7.index_ref
  14.0 0.0 copy-done.2
  14.0 0.9 %shard_map.67.far_ref = s32[384,128]{1,0:T(8,128)S(1)} custom-call(s32[384,1]{1,0:T(8,128)S(1)} %copy.7.index_ref, s32[8]{0:T(128)S(1)} %copy-done.2), custom_call_target="tpu_custom_call" | custom-call | flops 1000 | bytes 1000 | tf_op jit(solution)/shard_map/pallas_call | solution.py:36
  15.0 0.5 collective-permute-done.rest_0_.rest_1_
  15.5 2.5 %collective-permute-start.2 = (bf16[128,2304]{1,0:T(8,128)(2,1)}, bf16[128,2304]{1,0:T(8,128)(2,1)S(1)}, u32[]{:S(2)}, u32[]{:S(2)}) collective-permute-start(bf16[128,2304]{1,0:T(8,128)(2,1)} %collective-permute-done.rest_0_.rest_1_), channel_id=1, source_target_pairs={{0,4},{5,1},{4,8},{9,5},{8,12},{13,9},{12,14},{15,13},{14,10},{11,... | collective-permute-start | bytes 1769480 | tf_op jit(solution)/shard_map/ppermute | solution.py:274
  18.0 2.0 %shard_map.68.rest_1_ = f32[384,64]{1,0:T(8,128)S(1)} custom-call(bf16[384,4096]{1,0:T(8,128)(2,1)S(1)} %get-tuple-element.74.x_ref, s32[384,128]{1,0:T(8,128)S(1)} %shard_map.67.far_ref, bf16[128,2304]{1,0:T(8,128)(2,1)} %shard_map.64.rest_0_), custom_call_target="tpu_custom_call" | custom-call | flops 1000 | bytes 1000 | tf_op jit(solution)/shard_map/pallas_call | solution.py:36
  20.0 2.0 %shard_map.69.rest_1_ = f32[384,64]{1,0:T(8,128)S(1)} custom-call(bf16[384,4096]{1,0:T(8,128)(2,1)S(1)} %get-tuple-element.74.x_ref, s32[384,128]{1,0:T(8,128)S(1)} %shard_map.67.far_ref, bf16[128,2304]{1,0:T(8,128)(2,1)} %collective-permute-done.rest_0_.rest_1_, f32[384,64]{1,0:T(8,128)S(1)} %shard_map.68.rest_1_), custom_call_target="tpu_custom_call" | custom-call | flops 1000 | bytes 1000 | tf_op jit(solution)/shard_map/pallas_call | solution.py:36
  22.0 0.0 collective-permute-done.1.rest_0_.rest_2_
  22.0 0.1 collective-permute-start.4
  22.1 2.0 %shard_map.70.rest_1_ = f32[384,64]{1,0:T(8,128)S(1)} custom-call(bf16[384,4096]{1,0:T(8,128)(2,1)S(1)} %get-tuple-element.74.x_ref, s32[384,128]{1,0:T(8,128)S(1)} %shard_map.67.far_ref, bf16[128,2304]{1,0:T(8,128)(2,1)} %collective-permute-done.1.rest_0_.rest_2_, f32[384,64]{1,0:T(8,128)S(1)} %shard_map.69.rest_1_), custom_call_target="tpu_custom_call" | custom-call | flops 1000 | bytes 1000 | tf_op jit(solution)/shard_map/pallas_call | solution.py:36
  24.2 5.1 %collective-permute-done.2.rest_0_.rest_3_ = bf16[128,2304]{1,0:T(8,128)(2,1)S(1)} collective-permute-done((bf16[128,2304]{1,0:T(8,128)(2,1)}, bf16[128,2304]{1,0:T(8,128)(2,1)S(1)}, u32[]{:S(2)}, u32[]{:S(2)}) %collective-permute-start.2) | collective-permute-done | bytes 589856 | tf_op jit(solution)/shard_map/ppermute | solution.py:274
  29.3 2.4 %collective-permute-start.5 = (bf16[128,2304]{1,0:T(8,128)(2,1)S(1)}, bf16[128,2304]{1,0:T(8,128)(2,1)S(1)}, u32[]{:S(2)}, u32[]{:S(2)}) collective-permute-start(bf16[128,2304]{1,0:T(8,128)(2,1)S(1)} %collective-permute-done.2.rest_0_.rest_3_), channel_id=1, source_target_pairs={{0,4},{5,1},{4,8},{9,5},{8,12},{13,9},{12,14},{15,13},{14,10},{11,... | collective-permute-start | bytes 1769480 | tf_op jit(solution)/shard_map/ppermute | solution.py:271
  31.6 0.0 collective-permute-done.3.there_ref
  31.6 4.2 %collective-permute-done.4.rest_0_.rest_4_ = bf16[128,2304]{1,0:T(8,128)(2,1)S(1)} collective-permute-done((bf16[128,2304]{1,0:T(8,128)(2,1)}, bf16[128,2304]{1,0:T(8,128)(2,1)S(1)}, u32[]{:S(2)}, u32[]{:S(2)}) %collective-permute-start.4) | collective-permute-done | bytes 589856 | tf_op jit(solution)/shard_map/ppermute | solution.py:275
  35.8 1.0 %shard_map.71.rest_1_ = f32[384,64]{1,0:T(8,128)S(1)} custom-call(bf16[384,4096]{1,0:T(8,128)(2,1)S(1)} %get-tuple-element.74.x_ref, s32[384,128]{1,0:T(8,128)S(1)} %shard_map.67.far_ref, bf16[128,2304]{1,0:T(8,128)(2,1)S(1)} %collective-permute-done.2.rest_0_.rest_3_, f32[384,64]{1,0:T(8,128)S(1)} %shard_map.70.rest_1_), custom_call_target="tpu_custom_call" | custom-call | flops 1000 | bytes 1000 | tf_op jit(solution)/shard_map/pallas_call | solution.py:36
  36.8 0.1 collective-permute-start.6
  36.9 0.9 %collective-permute-start.8 = (bf16[64,2304]{1,0:T(8,128)(2,1)S(1)}, bf16[64,2304]{1,0:T(8,128)(2,1)S(1)}, u32[]{:S(2)}, u32[]{:S(2)}) collective-permute-start(bf16[64,2304]{1,0:T(8,128)(2,1)S(1)} %get-tuple-element.81), channel_id=1, source_target_pairs={{4,0},{1,5},{8,4},{5,9},{12,8},{9,13},{14,12},{13,15},{10,14},{15,... | collective-permute-start | bytes 884744 | tf_op jit(solution)/shard_map/ppermute | solution.py:272
  37.8 1.0 %shard_map.72.own_ref = f32[384,64]{1,0:T(8,128)S(1)} custom-call(bf16[384,4096]{1,0:T(8,128)(2,1)S(1)} %get-tuple-element.74.x_ref, s32[384,128]{1,0:T(8,128)S(1)} %shard_map.67.far_ref, bf16[128,2304]{1,0:T(8,128)(2,1)S(1)} %collective-permute-done.4.rest_0_.rest_4_, f32[384,64]{1,0:T(8,128)S(1)} %shard_map.71.rest_1_), custom_call_target="tpu_custom_call" | custom-call | flops 1000 | bytes 1000 | tf_op jit(solution)/shard_map/pallas_call | solution.py:36
  38.8 0.0 copy-start.1
  38.8 3.5 %collective-permute-done.5.rest_0_ = bf16[128,2304]{1,0:T(8,128)(2,1)S(1)} collective-permute-done((bf16[128,2304]{1,0:T(8,128)(2,1)S(1)}, bf16[128,2304]{1,0:T(8,128)(2,1)S(1)}, u32[]{:S(2)}, u32[]{:S(2)}) %collective-permute-start.5) | collective-permute-done | bytes 589856 | tf_op jit(solution)/shard_map/ppermute | solution.py:271
  42.3 2.5 %collective-permute-start.9 = (bf16[64,2304]{1,0:T(8,128)(2,1)S(1)}, bf16[64,2304]{1,0:T(8,128)(2,1)S(1)}, u32[]{:S(2)}, u32[]{:S(2)}) collective-permute-start(bf16[64,2304]{1,0:T(8,128)(2,1)S(1)} %slice.11), channel_id=1, source_target_pairs={{0,4},{5,1},{4,8},{9,5},{8,12},{13,9},{12,14},{15,13},{14,10},{11,... | collective-permute-start | bytes 884744 | tf_op jit(solution)/shard_map/ppermute | solution.py:300
  44.9 0.9 %collective-permute-done.6.rest_1_.rest_2_ = bf16[64,2304]{1,0:T(8,128)(2,1)S(1)} collective-permute-done((bf16[64,2304]{1,0:T(8,128)(2,1)S(1)}, bf16[64,2304]{1,0:T(8,128)(2,1)S(1)}, u32[]{:S(2)}, u32[]{:S(2)}) %collective-permute-start.6) | collective-permute-done | bytes 294944 | tf_op jit(solution)/shard_map/ppermute | solution.py:272
  45.8 0.0 collective-permute-start.10
  45.8 0.0 collective-permute-start.7
  45.8 1.0 %shard_map.74.rest_2_ = f32[384,64]{1,0:T(8,128)S(1)} custom-call(bf16[384,4096]{1,0:T(8,128)(2,1)S(1)} %get-tuple-element.74.x_ref, s32[384,128]{1,0:T(8,128)S(1)} %shard_map.67.far_ref, bf16[128,2304]{1,0:T(8,128)(2,1)S(1)} %collective-permute-done.5.rest_0_), custom_call_target="tpu_custom_call" | custom-call | flops 1000 | bytes 1000 | tf_op jit(solution)/shard_map/pallas_call | solution.py:36
  46.7 0.5 collective-permute-done.7.other_ref
  47.2 0.0 copy-done.1
  47.2 2.3 %shard_map.73.base_ref = f32[384,512]{1,0:T(8,128)S(1)} custom-call(s32[384,128]{1,0:T(8,128)S(1)} %shard_map.67.far_ref, f32[384,64]{1,0:T(8,128)S(1)} %shard_map.72.own_ref, f32[384,64]{1,0:T(8,128)S(1)} %collective-permute-done.7.other_ref, f32[384,512]{1,0:T(8,128)S(1)} %copy-done.1, f32[384,512]{1,0:T(8,128)} %collective-permute-done.3.there_ref, ...), custom_call_target="tpu_custom_call" | custom-call | flops 1000 | bytes 1000 | tf_op jit(solution)/shard_map/pallas_call | solution.py:36
  49.5 0.4 collective-permute-done.8.rest_0_.rest_1_
  49.9 1.0 %shard_map.75.rest_1_ = f32[384,64]{1,0:T(8,128)S(1)} custom-call(bf16[384,4096]{1,0:T(8,128)(2,1)S(1)} %get-tuple-element.74.x_ref, s32[384,128]{1,0:T(8,128)S(1)} %shard_map.67.far_ref, bf16[64,2304]{1,0:T(8,128)(2,1)S(1)} %collective-permute-done.8.rest_0_.rest_1_, bf16[64,2304]{1,0:T(8,128)(2,1)S(1)} %collective-permute-done.6.rest_1_.rest_2_, ...), custom_call_target="tpu_custom_call" | custom-call | flops 1000 | bytes 1000 | tf_op jit(solution)/shard_map/pallas_call | solution.py:36
  50.9 0.9 %collective-permute-done.9.m_ref.rest_3_ = bf16[64,2304]{1,0:T(8,128)(2,1)S(1)} collective-permute-done((bf16[64,2304]{1,0:T(8,128)(2,1)S(1)}, bf16[64,2304]{1,0:T(8,128)(2,1)S(1)}, u32[]{:S(2)}, u32[]{:S(2)}) %collective-permute-start.9) | collective-permute-done | bytes 294944 | tf_op jit(solution)/shard_map/ppermute | solution.py:300
  51.8 0.5 shard_map.76.rest_0_
  52.3 0.7 %collective-permute-done.10.m_ref.rest_4_ = bf16[64,2304]{1,0:T(8,128)(2,1)S(1)} collective-permute-done((bf16[64,2304]{1,0:T(8,128)(2,1)S(1)}, bf16[64,2304]{1,0:T(8,128)(2,1)S(1)}, u32[]{:S(2)}, u32[]{:S(2)}) %collective-permute-start.10) | collective-permute-done | bytes 294944 | tf_op jit(solution)/shard_map/ppermute | solution.py:301
  53.1 0.6 shard_map.77.own_ref
  53.6 0.1 collective-permute-start.11
  53.7 1.4 %collective-permute-done.11.other_ref = f32[384,64]{1,0:T(8,128)S(1)} collective-permute-done((f32[384,64]{1,0:T(8,128)S(1)}, f32[384,64]{1,0:T(8,128)S(1)}, u32[]{:S(2)}, u32[]{:S(2)}) %collective-permute-start.11) | collective-permute-done | bytes 98336 | tf_op jit(solution)/shard_map/ppermute | solution.py:341
  55.1 1.2 %shard_map.78 = bf16[384,512]{1,0:T(8,128)(2,1)} custom-call(s32[384,128]{1,0:T(8,128)S(1)} %shard_map.67.far_ref, f32[384,64]{1,0:T(8,128)S(1)} %shard_map.77.own_ref, f32[384,64]{1,0:T(8,128)S(1)} %collective-permute-done.11.other_ref, f32[384,512]{1,0:T(8,128)S(1)} %shard_map.73.base_ref, bf16[128,2304]{1,0:T(8,128)(2,1)S(1)} %collective-permute-done.5.rest_0_, ...), custom_call_target="tpu_custom_call" | custom-call | flops 1000 | bytes 1000 | tf_op jit(solution)/shard_map/pallas_call | solution.py:36
  (2 shorter events, 0.1 us)
Async XLA Ops:
  1.9 13.6 %collective-permute-start = (bf16[128,2304]{1,0:T(8,128)(2,1)}, bf16[128,2304]{1,0:T(8,128)(2,1)}, u32[]{:S(2)}, u32[]{:S(2)}) collective-permute-start(bf16[128,2304]{1,0:T(8,128)(2,1)} %shard_map.64.rest_0_), channel_id=1, source_target_pairs={{0,4},{5,1},{4,8},{9,5},{8,12},{13,9},{12,14},{15,13},{14,10},{11,... | collective-permute-start | bytes 1769480 | tf_op jit(solution)/shard_map/ppermute | solution.py:274
  9.5 12.5 %collective-permute-start.1 = (bf16[128,2304]{1,0:T(8,128)(2,1)}, bf16[128,2304]{1,0:T(8,128)(2,1)}, u32[]{:S(2)}, u32[]{:S(2)}) collective-permute-start(bf16[128,2304]{1,0:T(8,128)(2,1)} %shard_map.64.rest_0_), channel_id=1, source_target_pairs={{4,0},{1,5},{8,4},{5,9},{12,8},{9,13},{14,12},{13,15},{10,14},{15,... | collective-permute-start | bytes 1769480 | tf_op jit(solution)/shard_map/ppermute | solution.py:275
  9.6 22.0 %collective-permute-start.3 = (f32[384,512]{1,0:T(8,128)}, f32[384,512]{1,0:T(8,128)}, u32[]{:S(2)}, u32[]{:S(2)}) collective-permute-start(f32[384,512]{1,0:T(8,128)} %get-tuple-element.46), channel_id=1, source_target_pairs={{0,1},{1,0},{2,3},{3,2},{4,5},{5,4},{6,7},{7,6},{8,9},{9,8},{10,11... | collective-permute-start | bytes 2359304 | tf_op jit(solution)/shard_map/ppermute | solution.py:240
  9.7 4.2 %copy-start.3 = (s32[384,1]{0,1:T(1,128)S(1)}, s32[384,1]{0,1:T(1,128)}, u32[]{:S(2)}) copy-start(s32[384,1]{0,1:T(1,128)} %param.7) | copy-start | bytes 4612
  9.7 4.3 %copy-start.2 = (s32[8]{0:T(128)S(1)}, s32[8]{0:T(128)}, u32[]{:S(2)}) copy-start(s32[8]{0:T(128)} %storage_ref.1) | copy-start | bytes 100
  13.0 0.9 %copy-start = (f32[384,512]{1,0:T(8,128)}, f32[384,512]{1,0:T(8,128)S(1)}, u32[]{:S(2)}) copy-start(f32[384,512]{1,0:T(8,128)S(1)} %shard_map.66.here_ref) | copy-start | bytes 2359300
  15.5 13.8 %collective-permute-start.2 = (bf16[128,2304]{1,0:T(8,128)(2,1)}, bf16[128,2304]{1,0:T(8,128)(2,1)S(1)}, u32[]{:S(2)}, u32[]{:S(2)}) collective-permute-start(bf16[128,2304]{1,0:T(8,128)(2,1)} %collective-permute-done.rest_0_.rest_1_), channel_id=1, source_target_pairs={{0,4},{5,1},{4,8},{9,5},{8,12},{13,9},{12,14},{15,13},{14,10},{11,... | collective-permute-start | bytes 1769480 | tf_op jit(solution)/shard_map/ppermute | solution.py:274
  22.0 13.8 %collective-permute-start.4 = (bf16[128,2304]{1,0:T(8,128)(2,1)}, bf16[128,2304]{1,0:T(8,128)(2,1)S(1)}, u32[]{:S(2)}, u32[]{:S(2)}) collective-permute-start(bf16[128,2304]{1,0:T(8,128)(2,1)} %collective-permute-done.1.rest_0_.rest_2_), channel_id=1, source_target_pairs={{4,0},{1,5},{8,4},{5,9},{12,8},{9,13},{14,12},{13,15},{10,14},{15,... | collective-permute-start | bytes 1769480 | tf_op jit(solution)/shard_map/ppermute | solution.py:275
  29.3 13.1 %collective-permute-start.5 = (bf16[128,2304]{1,0:T(8,128)(2,1)S(1)}, bf16[128,2304]{1,0:T(8,128)(2,1)S(1)}, u32[]{:S(2)}, u32[]{:S(2)}) collective-permute-start(bf16[128,2304]{1,0:T(8,128)(2,1)S(1)} %collective-permute-done.2.rest_0_.rest_3_), channel_id=1, source_target_pairs={{0,4},{5,1},{4,8},{9,5},{8,12},{13,9},{12,14},{15,13},{14,10},{11,... | collective-permute-start | bytes 1769480 | tf_op jit(solution)/shard_map/ppermute | solution.py:271
  36.8 9.0 %collective-permute-start.6 = (bf16[64,2304]{1,0:T(8,128)(2,1)S(1)}, bf16[64,2304]{1,0:T(8,128)(2,1)S(1)}, u32[]{:S(2)}, u32[]{:S(2)}) collective-permute-start(bf16[64,2304]{1,0:T(8,128)(2,1)S(1)} %get-tuple-element.82), channel_id=1, source_target_pairs={{4,0},{1,5},{8,4},{5,9},{12,8},{9,13},{14,12},{13,15},{10,14},{15,... | collective-permute-start | bytes 884744 | tf_op jit(solution)/shard_map/ppermute | solution.py:272
  36.9 13.0 %collective-permute-start.8 = (bf16[64,2304]{1,0:T(8,128)(2,1)S(1)}, bf16[64,2304]{1,0:T(8,128)(2,1)S(1)}, u32[]{:S(2)}, u32[]{:S(2)}) collective-permute-start(bf16[64,2304]{1,0:T(8,128)(2,1)S(1)} %get-tuple-element.81), channel_id=1, source_target_pairs={{4,0},{1,5},{8,4},{5,9},{12,8},{9,13},{14,12},{13,15},{10,14},{15,... | collective-permute-start | bytes 884744 | tf_op jit(solution)/shard_map/ppermute | solution.py:272
  38.8 8.5 %copy-start.1 = (f32[384,512]{1,0:T(8,128)S(1)}, f32[384,512]{1,0:T(8,128)}, u32[]{:S(2)}) copy-start(f32[384,512]{1,0:T(8,128)} %copy-done) | copy-start | bytes 2359300
  42.3 9.4 %collective-permute-start.9 = (bf16[64,2304]{1,0:T(8,128)(2,1)S(1)}, bf16[64,2304]{1,0:T(8,128)(2,1)S(1)}, u32[]{:S(2)}, u32[]{:S(2)}) collective-permute-start(bf16[64,2304]{1,0:T(8,128)(2,1)S(1)} %slice.11), channel_id=1, source_target_pairs={{0,4},{5,1},{4,8},{9,5},{8,12},{13,9},{12,14},{15,13},{14,10},{11,... | collective-permute-start | bytes 884744 | tf_op jit(solution)/shard_map/ppermute | solution.py:300
  45.8 7.3 %collective-permute-start.10 = (bf16[64,2304]{1,0:T(8,128)(2,1)S(1)}, bf16[64,2304]{1,0:T(8,128)(2,1)S(1)}, u32[]{:S(2)}, u32[]{:S(2)}) collective-permute-start(bf16[64,2304]{1,0:T(8,128)(2,1)S(1)} %collective-permute-done.6.rest_1_.rest_2_), channel_id=1, source_target_pairs={{4,0},{1,5},{8,4},{5,9},{12,8},{9,13},{14,12},{13,15},{10,14},{15,... | collective-permute-start | bytes 884744 | tf_op jit(solution)/shard_map/ppermute | solution.py:301
  45.8 1.4 %collective-permute-start.7 = (f32[384,64]{1,0:T(8,128)S(1)}, f32[384,64]{1,0:T(8,128)S(1)}, u32[]{:S(2)}, u32[]{:S(2)}) collective-permute-start(f32[384,64]{1,0:T(8,128)S(1)} %shard_map.72.own_ref), channel_id=1, source_target_pairs={{0,1},{1,0},{2,3},{3,2},{4,5},{5,4},{6,7},{7,6},{8,9},{9,8},{10,11... | collective-permute-start | bytes 294920 | tf_op jit(solution)/shard_map/ppermute | solution.py:307
  53.6 1.5 %collective-permute-start.11 = (f32[384,64]{1,0:T(8,128)S(1)}, f32[384,64]{1,0:T(8,128)S(1)}, u32[]{:S(2)}, u32[]{:S(2)}) collective-permute-start(f32[384,64]{1,0:T(8,128)S(1)} %shard_map.77.own_ref), channel_id=1, source_target_pairs={{0,1},{1,0},{2,3},{3,2},{4,5},{5,4},{6,7},{7,6},{8,9},{9,8},{10,11... | collective-permute-start | bytes 294920 | tf_op jit(solution)/shard_map/ppermute | solution.py:341

commit v8 on v7

--- a/solution.py
+++ b/solution.py
@@ -45,22 +45,28 @@
     return got[0] if len(outs) == 1 else got
 
 
-def pack_kernel(a_ref, b_ref, o_ref, sems):
+def pack_kernel(a_ref, b_ref, o_ref, held, in_sems, out_sems):
     rank, half = a_ref.shape
     k_half, b_half = half // 2, o_ref.shape[1] - half // 2
     first = lax.axis_index("tensor") * (2 * b_half)
-    copies = []
+    arriving, leaving = [], []
     for i in range(2):
         rows = pl.ds(i * rank, rank)
         b_first = pl.multiple_of(first + i * b_half, b_half)
-        copies += [
-            (a_ref.at[:, pl.ds(i * k_half, k_half)], o_ref.at[rows, pl.ds(0, k_half)]),
-            (b_ref.at[:, pl.ds(b_first, b_half)], o_ref.at[rows, pl.ds(k_half, b_half)]),
+        pairs = [
+            (a_ref.at[:, pl.ds(i * k_half, k_half)], held.at[rows, pl.ds(0, k_half)]),
+            (b_ref.at[:, pl.ds(b_first, b_half)], held.at[rows, pl.ds(k_half, b_half)]),
         ]
-    copies = [pltpu.make_async_copy(*c, sems.at[i]) for i, c in enumerate(copies)]
-    for c in copies:
-        c.start()
-    for c in copies:
+        arriving.append([pltpu.make_async_copy(*pair, in_sems.at[2 * i + j]) for j, pair in enumerate(pairs)])
+        leaving.append(pltpu.make_async_copy(held.at[rows, :], o_ref.at[rows, :], out_sems.at[i]))
+    for copies in arriving:
+        for c in copies:
+            c.start()
+    for i in range(2):
+        for c in arriving[i]:
+            c.wait()
+        leaving[i].start()
+    for c in leaving:
         c.wait()
 
 
@@ -152,6 +158,8 @@
     if i == 1:
         kept = rest[1][...] if len(rest) > 2 else 0.0
         part = jnp.where(far_ref[:, : part.shape[1]] == s, part + rest[0][...], kept)
+        middle = part.shape[0] // 2
+        part = jnp.concatenate([part[:middle], part[middle:]], axis=1)
     o_ref[...] = part
 
 
@@ -187,10 +195,20 @@
 
 
 def last_kernel(steps, counts, far_ref, own_ref, other_ref, base_ref, *rest):
-    o_ref = rest[-1]
-    ups = ups_of(counts, rest[:-1], own_ref.shape[1], o_ref.shape[1])
-    lifted = lift(steps, far_ref, own_ref[...] + other_ref[...], ups)
-    o_ref[...] = (base_ref[...] + lifted).astype(jnp.bfloat16)
+    o_ref, held, sems = rest[-3:]
+    rows, keys = held.shape
+    rank = own_ref.shape[1] // 2
+    ups = ups_of(counts, rest[:-3], rank, keys)
+    total = own_ref[...] + other_ref[...]
+    copies = []
+    for i in range(2):
+        part = pl.ds(i * (rows // 2), rows // 2)
+        lifted = lift(steps, far_ref.at[part, :], total[:, i * rank : (i + 1) * rank], ups)
+        held[part, :] = (base_ref[part, :] + lifted).astype(jnp.bfloat16)
+        copies.append(pltpu.make_async_copy(held.at[part, :], o_ref.at[part, :], sems.at[i]))
+        copies[-1].start()
+    for c in copies:
+        c.wait()
 
 
 def shards(n, requests, adapter_index, storage_slot_index, key_base_weight, down_factor, up_factor):
@@ -216,7 +234,12 @@
         down_factor[0].T,
         up_factor[0],
         mib=PACK_MIB,
-        scratch=[pltpu.SemaphoreType.DMA((4,))],
+        scratch=[
+            pltpu.VMEM((2 * rank, half // 2 + out_keys // 2), jnp.bfloat16),
+            pltpu.SemaphoreType.DMA((4,)),
+            pltpu.SemaphoreType.DMA((2,)),
+        ],
+        out_space=HBM,
     )
     p = own
     opposite = n % 2 == 0 and n > 1
@@ -330,7 +353,7 @@
     first, q = tie((first, q))
     total = call(
         functools.partial(half_kernel, 1, n // 2),
-        [((rows, rank), f32)],
+        [((rows // 2, 2 * rank), f32)],
         [VMEM] * (4 + len(kept)),
         x,
         far,
@@ -350,6 +373,8 @@
         other,
         base,
         *messages,
+        scratch=[pltpu.VMEM((rows, out_keys), jnp.bfloat16), pltpu.SemaphoreType.DMA((2,))],
+        out_space=HBM,
     )
 
 

time: 56.6 us -> 56.4 us (level)
  no operation moved by 1% of the time
where the time goes in v8:
time: 56.4 us; the launch traced here: 56.1 us
  Pallas kernels  25.1 us (45%)
  waiting for transfers between devices  18 us (32%)
  starting transfers between devices  11.7 us (21%)
  local copies, waits for them, and re-layouts  1.09 us (2%)
    pallas_call x15, Pallas kernels, call(): pl.pallas_call(kernel, in_specs=in_specs, out_specs=[out_space] * len(out...  25.1 us
    ppermute x3, waiting for transfers between devices, shards(): p = (lax.ppermute(p, both, forth),)  9.16 us
    ppermute x3, starting transfers between devices, shards(): p = (lax.ppermute(p, both, forth),)  7.93 us
    ppermute x2, waiting for transfers between devices, shards(): q = (lax.ppermute(q, both, back),)  4.17 us
    ppermute x1, starting transfers between devices, shards(): p = lax.ppermute(p, both, forth)  2.53 us
    ppermute x2, waiting for transfers between devices, shards(): other = lax.ppermute(total, 'tensor', swap)  1.76 us
    ppermute x2, waiting for transfers between devices, shards(): q = tuple((lax.ppermute(h, both, back) for h in (q[rank:], q[:rank])))[::-1]  1.3 us
  transfers between devices with their start and end apart: 12, of which 10 were waited for; matrix products, arithmetic and copies ran while one was open for 0% of the time, Pallas kernels for 38%

profile of v8, /device:TPU:0, one launch (start us, length us, event | category | flops | bytes accessed | tf_op | source)
XLA Modules:
  0.0 56.1 jit_solution(16074304956782603162)
XLA Ops:
  0.0 1.8 %shard_map.64.rest_0_ = bf16[128,2304]{1,0:T(8,128)(2,1)} custom-call(bf16[64,4096]{1,0:T(8,128)(2,1)} %bitcast.4, bf16[64,1024]{1,0:T(8,128)(2,1)} %bitcast.5), custom_call_target="tpu_custom_call" | custom-call | flops 1000 | bytes 1000 | tf_op jit(solution)/shard_map/pallas_call | solution.py:36
  1.8 3.1 %collective-permute-start = (bf16[128,2304]{1,0:T(8,128)(2,1)}, bf16[128,2304]{1,0:T(8,128)(2,1)}, u32[]{:S(2)}, u32[]{:S(2)}) collective-permute-start(bf16[128,2304]{1,0:T(8,128)(2,1)} %shard_map.64.rest_0_), channel_id=1, source_target_pairs={{0,4},{5,1},{4,8},{9,5},{8,12},{13,9},{12,14},{15,13},{14,10},{11,... | collective-permute-start | bytes 1769480 | tf_op jit(solution)/shard_map/ppermute | solution.py:297
  4.9 4.5 %shard_map.65 = (bf16[384,4096]{1,0:T(8,128)(2,1)S(1)}, f32[384,512]{1,0:T(8,128)}) custom-call(bf16[384,4096]{1,0:T(8,128)(2,1)} %x_hbm, bf16[4096,1024]{1,0:T(8,128)(2,1)} %w_hbm.2), custom_call_target="tpu_custom_call" | custom-call | flops 1000 | bytes 1000 | tf_op jit(solution)/shard_map/pallas_call | solution.py:36
  9.4 0.1 collective-permute-start.1
  9.5 0.1 collective-permute-start.3
  9.6 0.0 copy-start.3
  9.6 0.0 copy-start.2
  9.6 3.3 %shard_map.66.here_ref = f32[384,512]{1,0:T(8,128)S(1)} custom-call(bf16[384,4096]{1,0:T(8,128)(2,1)S(1)} %get-tuple-element.74.x_ref, bf16[4096,1024]{1,0:T(8,128)(2,1)} %w_hbm.2), custom_call_target="tpu_custom_call" | custom-call | flops 1000 | bytes 1000 | tf_op jit(solution)/shard_map/pallas_call | solution.py:36
  12.9 0.0 copy-start
  12.9 0.9 %copy-done = f32[384,512]{1,0:T(8,128)} copy-done((f32[384,512]{1,0:T(8,128)}, f32[384,512]{1,0:T(8,128)S(1)}, u32[]{:S(2)}) %copy-start) | copy-done | bytes 786456
  13.8 0.0 copy-done.3
  13.8 0.1 copy.7.index_ref
  13.9 0.0 copy-done.2
  13.9 0.9 %shard_map.67.far_ref = s32[384,128]{1,0:T(8,128)S(1)} custom-call(s32[384,1]{1,0:T(8,128)S(1)} %copy.7.index_ref, s32[8]{0:T(128)S(1)} %copy-done.2), custom_call_target="tpu_custom_call" | custom-call | flops 1000 | bytes 1000 | tf_op jit(solution)/shard_map/pallas_call | solution.py:36
  14.9 0.5 collective-permute-done.rest_0_.rest_1_
  15.4 2.5 %collective-permute-start.2 = (bf16[128,2304]{1,0:T(8,128)(2,1)}, bf16[128,2304]{1,0:T(8,128)(2,1)S(1)}, u32[]{:S(2)}, u32[]{:S(2)}) collective-permute-start(bf16[128,2304]{1,0:T(8,128)(2,1)} %collective-permute-done.rest_0_.rest_1_), channel_id=1, source_target_pairs={{0,4},{5,1},{4,8},{9,5},{8,12},{13,9},{12,14},{15,13},{14,10},{11,... | collective-permute-start | bytes 1769480 | tf_op jit(solution)/shard_map/ppermute | solution.py:297
  17.9 2.0 %shard_map.68.rest_1_ = f32[384,64]{1,0:T(8,128)S(1)} custom-call(bf16[384,4096]{1,0:T(8,128)(2,1)S(1)} %get-tuple-element.74.x_ref, s32[384,128]{1,0:T(8,128)S(1)} %shard_map.67.far_ref, bf16[128,2304]{1,0:T(8,128)(2,1)} %shard_map.64.rest_0_), custom_call_target="tpu_custom_call" | custom-call | flops 1000 | bytes 1000 | tf_op jit(solution)/shard_map/pallas_call | solution.py:36
  19.9 2.0 %shard_map.69.rest_1_ = f32[384,64]{1,0:T(8,128)S(1)} custom-call(bf16[384,4096]{1,0:T(8,128)(2,1)S(1)} %get-tuple-element.74.x_ref, s32[384,128]{1,0:T(8,128)S(1)} %shard_map.67.far_ref, bf16[128,2304]{1,0:T(8,128)(2,1)} %collective-permute-done.rest_0_.rest_1_, f32[384,64]{1,0:T(8,128)S(1)} %shard_map.68.rest_1_), custom_call_target="tpu_custom_call" | custom-call | flops 1000 | bytes 1000 | tf_op jit(solution)/shard_map/pallas_call | solution.py:36
  21.9 0.0 collective-permute-done.1.rest_0_.rest_2_
  22.0 0.1 collective-permute-start.4
  22.0 2.0 %shard_map.70.rest_1_ = f32[384,64]{1,0:T(8,128)S(1)} custom-call(bf16[384,4096]{1,0:T(8,128)(2,1)S(1)} %get-tuple-element.74.x_ref, s32[384,128]{1,0:T(8,128)S(1)} %shard_map.67.far_ref, bf16[128,2304]{1,0:T(8,128)(2,1)} %collective-permute-done.1.rest_0_.rest_2_, f32[384,64]{1,0:T(8,128)S(1)} %shard_map.69.rest_1_), custom_call_target="tpu_custom_call" | custom-call | flops 1000 | bytes 1000 | tf_op jit(solution)/shard_map/pallas_call | solution.py:36
  24.1 5.1 %collective-permute-done.2.rest_0_.rest_3_ = bf16[128,2304]{1,0:T(8,128)(2,1)S(1)} collective-permute-done((bf16[128,2304]{1,0:T(8,128)(2,1)}, bf16[128,2304]{1,0:T(8,128)(2,1)S(1)}, u32[]{:S(2)}, u32[]{:S(2)}) %collective-permute-start.2) | collective-permute-done | bytes 589856 | tf_op jit(solution)/shard_map/ppermute | solution.py:297
  29.2 2.4 %collective-permute-start.5 = (bf16[128,2304]{1,0:T(8,128)(2,1)S(1)}, bf16[128,2304]{1,0:T(8,128)(2,1)S(1)}, u32[]{:S(2)}, u32[]{:S(2)}) collective-permute-start(bf16[128,2304]{1,0:T(8,128)(2,1)S(1)} %collective-permute-done.2.rest_0_.rest_3_), channel_id=1, source_target_pairs={{0,4},{5,1},{4,8},{9,5},{8,12},{13,9},{12,14},{15,13},{14,10},{11,... | collective-permute-start | bytes 1769480 | tf_op jit(solution)/shard_map/ppermute | solution.py:294
  31.6 0.0 collective-permute-done.3.there_ref
  31.6 4.2 %collective-permute-done.4.rest_0_.rest_4_ = bf16[128,2304]{1,0:T(8,128)(2,1)S(1)} collective-permute-done((bf16[128,2304]{1,0:T(8,128)(2,1)}, bf16[128,2304]{1,0:T(8,128)(2,1)S(1)}, u32[]{:S(2)}, u32[]{:S(2)}) %collective-permute-start.4) | collective-permute-done | bytes 589856 | tf_op jit(solution)/shard_map/ppermute | solution.py:298
  35.7 1.0 %shard_map.71.rest_1_ = f32[384,64]{1,0:T(8,128)S(1)} custom-call(bf16[384,4096]{1,0:T(8,128)(2,1)S(1)} %get-tuple-element.74.x_ref, s32[384,128]{1,0:T(8,128)S(1)} %shard_map.67.far_ref, bf16[128,2304]{1,0:T(8,128)(2,1)S(1)} %collective-permute-done.2.rest_0_.rest_3_, f32[384,64]{1,0:T(8,128)S(1)} %shard_map.70.rest_1_), custom_call_target="tpu_custom_call" | custom-call | flops 1000 | bytes 1000 | tf_op jit(solution)/shard_map/pallas_call | solution.py:36
  36.7 0.1 collective-permute-start.6
  36.8 0.9 %collective-permute-start.8 = (bf16[64,2304]{1,0:T(8,128)(2,1)S(1)}, bf16[64,2304]{1,0:T(8,128)(2,1)S(1)}, u32[]{:S(2)}, u32[]{:S(2)}) collective-permute-start(bf16[64,2304]{1,0:T(8,128)(2,1)S(1)} %get-tuple-element.81), channel_id=1, source_target_pairs={{4,0},{1,5},{8,4},{5,9},{12,8},{9,13},{14,12},{13,15},{10,14},{15,... | collective-permute-start | bytes 884744 | tf_op jit(solution)/shard_map/ppermute | solution.py:295
  37.7 1.0 %shard_map.72.own_ref = f32[384,64]{1,0:T(8,128)S(1)} custom-call(bf16[384,4096]{1,0:T(8,128)(2,1)S(1)} %get-tuple-element.74.x_ref, s32[384,128]{1,0:T(8,128)S(1)} %shard_map.67.far_ref, bf16[128,2304]{1,0:T(8,128)(2,1)S(1)} %collective-permute-done.4.rest_0_.rest_4_, f32[384,64]{1,0:T(8,128)S(1)} %shard_map.71.rest_1_), custom_call_target="tpu_custom_call" | custom-call | flops 1000 | bytes 1000 | tf_op jit(solution)/shard_map/pallas_call | solution.py:36
  38.7 0.0 copy-start.1
  38.7 3.5 %collective-permute-done.5.rest_0_ = bf16[128,2304]{1,0:T(8,128)(2,1)S(1)} collective-permute-done((bf16[128,2304]{1,0:T(8,128)(2,1)S(1)}, bf16[128,2304]{1,0:T(8,128)(2,1)S(1)}, u32[]{:S(2)}, u32[]{:S(2)}) %collective-permute-start.5) | collective-permute-done | bytes 589856 | tf_op jit(solution)/shard_map/ppermute | solution.py:294
  42.3 2.5 %collective-permute-start.9 = (bf16[64,2304]{1,0:T(8,128)(2,1)S(1)}, bf16[64,2304]{1,0:T(8,128)(2,1)S(1)}, u32[]{:S(2)}, u32[]{:S(2)}) collective-permute-start(bf16[64,2304]{1,0:T(8,128)(2,1)S(1)} %slice.11), channel_id=1, source_target_pairs={{0,4},{5,1},{4,8},{9,5},{8,12},{13,9},{12,14},{15,13},{14,10},{11,... | collective-permute-start | bytes 884744 | tf_op jit(solution)/shard_map/ppermute | solution.py:323
  44.8 0.9 %collective-permute-done.6.rest_1_.rest_2_ = bf16[64,2304]{1,0:T(8,128)(2,1)S(1)} collective-permute-done((bf16[64,2304]{1,0:T(8,128)(2,1)S(1)}, bf16[64,2304]{1,0:T(8,128)(2,1)S(1)}, u32[]{:S(2)}, u32[]{:S(2)}) %collective-permute-start.6) | collective-permute-done | bytes 294944 | tf_op jit(solution)/shard_map/ppermute | solution.py:295
  45.7 0.0 collective-permute-start.10
  45.7 0.0 collective-permute-start.7
  45.7 1.0 %shard_map.74.rest_2_ = f32[384,64]{1,0:T(8,128)S(1)} custom-call(bf16[384,4096]{1,0:T(8,128)(2,1)S(1)} %get-tuple-element.74.x_ref, s32[384,128]{1,0:T(8,128)S(1)} %shard_map.67.far_ref, bf16[128,2304]{1,0:T(8,128)(2,1)S(1)} %collective-permute-done.5.rest_0_), custom_call_target="tpu_custom_call" | custom-call | flops 1000 | bytes 1000 | tf_op jit(solution)/shard_map/pallas_call | solution.py:36
  46.7 0.5 collective-permute-done.7.other_ref
  47.1 0.0 copy-done.1
  47.1 2.3 %shard_map.73.base_ref = f32[384,512]{1,0:T(8,128)S(1)} custom-call(s32[384,128]{1,0:T(8,128)S(1)} %shard_map.67.far_ref, f32[384,64]{1,0:T(8,128)S(1)} %shard_map.72.own_ref, f32[384,64]{1,0:T(8,128)S(1)} %collective-permute-done.7.other_ref, f32[384,512]{1,0:T(8,128)S(1)} %copy-done.1, f32[384,512]{1,0:T(8,128)} %collective-permute-done.3.there_ref, ...), custom_call_target="tpu_custom_call" | custom-call | flops 1000 | bytes 1000 | tf_op jit(solution)/shard_map/pallas_call | solution.py:36
  49.4 0.4 collective-permute-done.8.rest_0_.rest_1_
  49.8 1.0 %shard_map.75.rest_1_ = f32[384,64]{1,0:T(8,128)S(1)} custom-call(bf16[384,4096]{1,0:T(8,128)(2,1)S(1)} %get-tuple-element.74.x_ref, s32[384,128]{1,0:T(8,128)S(1)} %shard_map.67.far_ref, bf16[64,2304]{1,0:T(8,128)(2,1)S(1)} %collective-permute-done.8.rest_0_.rest_1_, bf16[64,2304]{1,0:T(8,128)(2,1)S(1)} %collective-permute-done.6.rest_1_.rest_2_, ...), custom_call_target="tpu_custom_call" | custom-call | flops 1000 | bytes 1000 | tf_op jit(solution)/shard_map/pallas_call | solution.py:36
  50.8 0.9 %collective-permute-done.9.m_ref.rest_3_ = bf16[64,2304]{1,0:T(8,128)(2,1)S(1)} collective-permute-done((bf16[64,2304]{1,0:T(8,128)(2,1)S(1)}, bf16[64,2304]{1,0:T(8,128)(2,1)S(1)}, u32[]{:S(2)}, u32[]{:S(2)}) %collective-permute-start.9) | collective-permute-done | bytes 294944 | tf_op jit(solution)/shard_map/ppermute | solution.py:323
  51.7 0.6 shard_map.76.rest_0_
  52.3 0.7 %collective-permute-done.10.m_ref.rest_4_ = bf16[64,2304]{1,0:T(8,128)(2,1)S(1)} collective-permute-done((bf16[64,2304]{1,0:T(8,128)(2,1)S(1)}, bf16[64,2304]{1,0:T(8,128)(2,1)S(1)}, u32[]{:S(2)}, u32[]{:S(2)}) %collective-permute-start.10) | collective-permute-done | bytes 294944 | tf_op jit(solution)/shard_map/ppermute | solution.py:324
  53.0 0.6 %shard_map.77.own_ref = f32[192,128]{1,0:T(8,128)S(1)} custom-call(bf16[384,4096]{1,0:T(8,128)(2,1)S(1)} %get-tuple-element.74.x_ref, s32[384,128]{1,0:T(8,128)S(1)} %shard_map.67.far_ref, bf16[64,2304]{1,0:T(8,128)(2,1)S(1)} %collective-permute-done.10.m_ref.rest_4_, f32[384,64]{1,0:T(8,128)S(1)} %shard_map.76.rest_0_, f32[384,64]{1,0:T(8,128)S(1)} %shard_map.75.rest_1_), custom_call_target="tpu_custom_call" | custom-call | flops 1000 | bytes 1000 | tf_op jit(solution)/shard_map/pallas_call | solution.py:36
  53.6 0.1 collective-permute-start.11
  53.7 1.3 %collective-permute-done.11.other_ref = f32[192,128]{1,0:T(8,128)S(1)} collective-permute-done((f32[192,128]{1,0:T(8,128)S(1)}, f32[192,128]{1,0:T(8,128)S(1)}, u32[]{:S(2)}, u32[]{:S(2)}) %collective-permute-start.11) | collective-permute-done | bytes 98336 | tf_op jit(solution)/shard_map/ppermute | solution.py:364
  55.0 1.1 %shard_map.78 = bf16[384,512]{1,0:T(8,128)(2,1)} custom-call(s32[384,128]{1,0:T(8,128)S(1)} %shard_map.67.far_ref, f32[192,128]{1,0:T(8,128)S(1)} %shard_map.77.own_ref, f32[192,128]{1,0:T(8,128)S(1)} %collective-permute-done.11.other_ref, f32[384,512]{1,0:T(8,128)S(1)} %shard_map.73.base_ref, bf16[128,2304]{1,0:T(8,128)(2,1)S(1)} %collective-permute-done.5.rest_0_, ...), custom_call_target="tpu_custom_call" | custom-call | flops 1000 | bytes 1000 | tf_op jit(solution)/shard_map/pallas_call | solution.py:36
  (2 shorter events, 0.1 us)
Async XLA Ops:
  1.8 13.6 %collective-permute-start = (bf16[128,2304]{1,0:T(8,128)(2,1)}, bf16[128,2304]{1,0:T(8,128)(2,1)}, u32[]{:S(2)}, u32[]{:S(2)}) collective-permute-start(bf16[128,2304]{1,0:T(8,128)(2,1)} %shard_map.64.rest_0_), channel_id=1, source_target_pairs={{0,4},{5,1},{4,8},{9,5},{8,12},{13,9},{12,14},{15,13},{14,10},{11,... | collective-permute-start | bytes 1769480 | tf_op jit(solution)/shard_map/ppermute | solution.py:297
  9.4 12.5 %collective-permute-start.1 = (bf16[128,2304]{1,0:T(8,128)(2,1)}, bf16[128,2304]{1,0:T(8,128)(2,1)}, u32[]{:S(2)}, u32[]{:S(2)}) collective-permute-start(bf16[128,2304]{1,0:T(8,128)(2,1)} %shard_map.64.rest_0_), channel_id=1, source_target_pairs={{4,0},{1,5},{8,4},{5,9},{12,8},{9,13},{14,12},{13,15},{10,14},{15,... | collective-permute-start | bytes 1769480 | tf_op jit(solution)/shard_map/ppermute | solution.py:298
  9.5 22.0 %collective-permute-start.3 = (f32[384,512]{1,0:T(8,128)}, f32[384,512]{1,0:T(8,128)}, u32[]{:S(2)}, u32[]{:S(2)}) collective-permute-start(f32[384,512]{1,0:T(8,128)} %get-tuple-element.46), channel_id=1, source_target_pairs={{0,1},{1,0},{2,3},{3,2},{4,5},{5,4},{6,7},{7,6},{8,9},{9,8},{10,11... | collective-permute-start | bytes 2359304 | tf_op jit(solution)/shard_map/ppermute | solution.py:263
  9.6 4.2 %copy-start.3 = (s32[384,1]{0,1:T(1,128)S(1)}, s32[384,1]{0,1:T(1,128)}, u32[]{:S(2)}) copy-start(s32[384,1]{0,1:T(1,128)} %param.7) | copy-start | bytes 4612
  9.6 4.3 %copy-start.2 = (s32[8]{0:T(128)S(1)}, s32[8]{0:T(128)}, u32[]{:S(2)}) copy-start(s32[8]{0:T(128)} %storage_ref.1) | copy-start | bytes 100
  12.9 0.9 %copy-start = (f32[384,512]{1,0:T(8,128)}, f32[384,512]{1,0:T(8,128)S(1)}, u32[]{:S(2)}) copy-start(f32[384,512]{1,0:T(8,128)S(1)} %shard_map.66.here_ref) | copy-start | bytes 2359300
  15.4 13.8 %collective-permute-start.2 = (bf16[128,2304]{1,0:T(8,128)(2,1)}, bf16[128,2304]{1,0:T(8,128)(2,1)S(1)}, u32[]{:S(2)}, u32[]{:S(2)}) collective-permute-start(bf16[128,2304]{1,0:T(8,128)(2,1)} %collective-permute-done.rest_0_.rest_1_), channel_id=1, source_target_pairs={{0,4},{5,1},{4,8},{9,5},{8,12},{13,9},{12,14},{15,13},{14,10},{11,... | collective-permute-start | bytes 1769480 | tf_op jit(solution)/shard_map/ppermute | solution.py:297
  22.0 13.8 %collective-permute-start.4 = (bf16[128,2304]{1,0:T(8,128)(2,1)}, bf16[128,2304]{1,0:T(8,128)(2,1)S(1)}, u32[]{:S(2)}, u32[]{:S(2)}) collective-permute-start(bf16[128,2304]{1,0:T(8,128)(2,1)} %collective-permute-done.1.rest_0_.rest_2_), channel_id=1, source_target_pairs={{4,0},{1,5},{8,4},{5,9},{12,8},{9,13},{14,12},{13,15},{10,14},{15,... | collective-permute-start | bytes 1769480 | tf_op jit(solution)/shard_map/ppermute | solution.py:298
  29.2 13.1 %collective-permute-start.5 = (bf16[128,2304]{1,0:T(8,128)(2,1)S(1)}, bf16[128,2304]{1,0:T(8,128)(2,1)S(1)}, u32[]{:S(2)}, u32[]{:S(2)}) collective-permute-start(bf16[128,2304]{1,0:T(8,128)(2,1)S(1)} %collective-permute-done.2.rest_0_.rest_3_), channel_id=1, source_target_pairs={{0,4},{5,1},{4,8},{9,5},{8,12},{13,9},{12,14},{15,13},{14,10},{11,... | collective-permute-start | bytes 1769480 | tf_op jit(solution)/shard_map/ppermute | solution.py:294
  36.7 9.0 %collective-permute-start.6 = (bf16[64,2304]{1,0:T(8,128)(2,1)S(1)}, bf16[64,2304]{1,0:T(8,128)(2,1)S(1)}, u32[]{:S(2)}, u32[]{:S(2)}) collective-permute-start(bf16[64,2304]{1,0:T(8,128)(2,1)S(1)} %get-tuple-element.82), channel_id=1, source_target_pairs={{4,0},{1,5},{8,4},{5,9},{12,8},{9,13},{14,12},{13,15},{10,14},{15,... | collective-permute-start | bytes 884744 | tf_op jit(solution)/shard_map/ppermute | solution.py:295
  36.8 13.0 %collective-permute-start.8 = (bf16[64,2304]{1,0:T(8,128)(2,1)S(1)}, bf16[64,2304]{1,0:T(8,128)(2,1)S(1)}, u32[]{:S(2)}, u32[]{:S(2)}) collective-permute-start(bf16[64,2304]{1,0:T(8,128)(2,1)S(1)} %get-tuple-element.81), channel_id=1, source_target_pairs={{4,0},{1,5},{8,4},{5,9},{12,8},{9,13},{14,12},{13,15},{10,14},{15,... | collective-permute-start | bytes 884744 | tf_op jit(solution)/shard_map/ppermute | solution.py:295
  38.7 8.5 %copy-start.1 = (f32[384,512]{1,0:T(8,128)S(1)}, f32[384,512]{1,0:T(8,128)}, u32[]{:S(2)}) copy-start(f32[384,512]{1,0:T(8,128)} %copy-done) | copy-start | bytes 2359300
  42.3 9.4 %collective-permute-start.9 = (bf16[64,2304]{1,0:T(8,128)(2,1)S(1)}, bf16[64,2304]{1,0:T(8,128)(2,1)S(1)}, u32[]{:S(2)}, u32[]{:S(2)}) collective-permute-start(bf16[64,2304]{1,0:T(8,128)(2,1)S(1)} %slice.11), channel_id=1, source_target_pairs={{0,4},{5,1},{4,8},{9,5},{8,12},{13,9},{12,14},{15,13},{14,10},{11,... | collective-permute-start | bytes 884744 | tf_op jit(solution)/shard_map/ppermute | solution.py:323
  45.7 7.3 %collective-permute-start.10 = (bf16[64,2304]{1,0:T(8,128)(2,1)S(1)}, bf16[64,2304]{1,0:T(8,128)(2,1)S(1)}, u32[]{:S(2)}, u32[]{:S(2)}) collective-permute-start(bf16[64,2304]{1,0:T(8,128)(2,1)S(1)} %collective-permute-done.6.rest_1_.rest_2_), channel_id=1, source_target_pairs={{4,0},{1,5},{8,4},{5,9},{12,8},{9,13},{14,12},{13,15},{10,14},{15,... | collective-permute-start | bytes 884744 | tf_op jit(solution)/shard_map/ppermute | solution.py:324
  45.7 1.4 %collective-permute-start.7 = (f32[384,64]{1,0:T(8,128)S(1)}, f32[384,64]{1,0:T(8,128)S(1)}, u32[]{:S(2)}, u32[]{:S(2)}) collective-permute-start(f32[384,64]{1,0:T(8,128)S(1)} %shard_map.72.own_ref), channel_id=1, source_target_pairs={{0,1},{1,0},{2,3},{3,2},{4,5},{5,4},{6,7},{7,6},{8,9},{9,8},{10,11... | collective-permute-start | bytes 294920 | tf_op jit(solution)/shard_map/ppermute | solution.py:330
  53.6 1.4 %collective-permute-start.11 = (f32[192,128]{1,0:T(8,128)S(1)}, f32[192,128]{1,0:T(8,128)S(1)}, u32[]{:S(2)}, u32[]{:S(2)}) collective-permute-start(f32[192,128]{1,0:T(8,128)S(1)} %shard_map.77.own_ref), channel_id=1, source_target_pairs={{0,1},{1,0},{2,3},{3,2},{4,5},{5,4},{6,7},{7,6},{8,9},{9,8},{10,11... | collective-permute-start | bytes 294920 | tf_op jit(solution)/shard_map/ppermute | solution.py:364

commit v9 on v8

--- a/solution.py
+++ b/solution.py
@@ -168,14 +168,11 @@
     low = (total - high.astype(jnp.float32)).astype(jnp.bfloat16)
     rank = total.shape[1]
     far = far_ref[:, :rank]
-    b_all = jnp.concatenate(ups, axis=0)
-    out = None
-    for part in (low, high):
-        part = part.astype(jnp.float32)
-        wide = jnp.concatenate([jnp.where(far == s, part, 0.0).astype(jnp.bfloat16) for s in steps], axis=1)
-        product = jnp.dot(wide, b_all, preferred_element_type=jnp.float32)
-        out = product if out is None else out + product
-    return out
+    parts = [part.astype(jnp.float32) for part in (low, high)]
+    wide = [jnp.where(far == s, part, 0.0).astype(jnp.bfloat16) for part in parts for s in steps]
+    return jnp.dot(
+        jnp.concatenate(wide, axis=1), jnp.concatenate(ups * 2, axis=0), preferred_element_type=jnp.float32
+    )
 
 
 def ups_of(counts, refs, rank, keys):
@@ -201,9 +198,11 @@
     ups = ups_of(counts, rest[:-3], rank, keys)
     total = own_ref[...] + other_ref[...]
     copies = []
-    for i in range(2):
-        part = pl.ds(i * (rows // 2), rows // 2)
-        lifted = lift(steps, far_ref.at[part, :], total[:, i * rank : (i + 1) * rank], ups)
+    deep = rows // 4
+    for i in range(4):
+        part = pl.ds(i * deep, deep)
+        at, side = i % 2 * deep, i // 2 * rank
+        lifted = lift(steps, far_ref.at[part, :], total[at : at + deep, side : side + rank], ups)
         held[part, :] = (base_ref[part, :] + lifted).astype(jnp.bfloat16)
         copies.append(pltpu.make_async_copy(held.at[part, :], o_ref.at[part, :], sems.at[i]))
         copies[-1].start()
@@ -373,7 +372,7 @@
         other,
         base,
         *messages,
-        scratch=[pltpu.VMEM((rows, out_keys), jnp.bfloat16), pltpu.SemaphoreType.DMA((2,))],
+        scratch=[pltpu.VMEM((rows, out_keys), jnp.bfloat16), pltpu.SemaphoreType.DMA((4,))],
         out_space=HBM,
     )
 

time: 56.4 us -> 56.5 us (level)
  no operation moved by 1% of the time
where the time goes in v9:
time: 56.5 us; the launch traced here: 56.1 us
  Pallas kernels  25 us (44%)
  waiting for transfers between devices  18.1 us (32%)
  starting transfers between devices  11.7 us (21%)
  local copies, waits for them, and re-layouts  1.09 us (2%)
    pallas_call x15, Pallas kernels, call(): pl.pallas_call(kernel, in_specs=in_specs, out_specs=[out_space] * len(out...  25 us
    ppermute x3, waiting for transfers between devices, shards(): p = (lax.ppermute(p, both, forth),)  9.16 us
    ppermute x3, starting transfers between devices, shards(): p = (lax.ppermute(p, both, forth),)  7.93 us
    ppermute x2, waiting for transfers between devices, shards(): q = (lax.ppermute(q, both, back),)  4.17 us
    ppermute x1, starting transfers between devices, shards(): p = lax.ppermute(p, both, forth)  2.53 us
    ppermute x2, waiting for transfers between devices, shards(): other = lax.ppermute(total, 'tensor', swap)  1.76 us
    ppermute x2, waiting for transfers between devices, shards(): q = tuple((lax.ppermute(h, both, back) for h in (q[rank:], q[:rank])))[::-1]  1.39 us
  transfers between devices with their start and end apart: 12, of which 10 were waited for; matrix products, arithmetic and copies ran while one was open for 0% of the time, Pallas kernels for 38%

profile of v9, /device:TPU:0, one launch (start us, length us, event | category | flops | bytes accessed | tf_op | source)
XLA Modules:
  0.0 56.1 jit_solution(2577318553037156998)
XLA Ops:
  0.0 1.8 %shard_map.64.rest_0_ = bf16[128,2304]{1,0:T(8,128)(2,1)} custom-call(bf16[64,4096]{1,0:T(8,128)(2,1)} %bitcast.4, bf16[64,1024]{1,0:T(8,128)(2,1)} %bitcast.5), custom_call_target="tpu_custom_call" | custom-call | flops 1000 | bytes 1000 | tf_op jit(solution)/shard_map/pallas_call | solution.py:36
  1.8 3.1 %collective-permute-start = (bf16[128,2304]{1,0:T(8,128)(2,1)}, bf16[128,2304]{1,0:T(8,128)(2,1)}, u32[]{:S(2)}, u32[]{:S(2)}) collective-permute-start(bf16[128,2304]{1,0:T(8,128)(2,1)} %shard_map.64.rest_0_), channel_id=1, source_target_pairs={{0,4},{5,1},{4,8},{9,5},{8,12},{13,9},{12,14},{15,13},{14,10},{11,... | collective-permute-start | bytes 1769480 | tf_op jit(solution)/shard_map/ppermute | solution.py:296
  4.9 4.5 %shard_map.65 = (bf16[384,4096]{1,0:T(8,128)(2,1)S(1)}, f32[384,512]{1,0:T(8,128)}) custom-call(bf16[384,4096]{1,0:T(8,128)(2,1)} %x_hbm, bf16[4096,1024]{1,0:T(8,128)(2,1)} %w_hbm.2), custom_call_target="tpu_custom_call" | custom-call | flops 1000 | bytes 1000 | tf_op jit(solution)/shard_map/pallas_call | solution.py:36
  9.4 0.1 collective-permute-start.1
  9.5 0.1 collective-permute-start.3
  9.6 0.0 copy-start.3
  9.6 0.0 copy-start.2
  9.6 3.3 %shard_map.66.here_ref = f32[384,512]{1,0:T(8,128)S(1)} custom-call(bf16[384,4096]{1,0:T(8,128)(2,1)S(1)} %get-tuple-element.74.x_ref, bf16[4096,1024]{1,0:T(8,128)(2,1)} %w_hbm.2), custom_call_target="tpu_custom_call" | custom-call | flops 1000 | bytes 1000 | tf_op jit(solution)/shard_map/pallas_call | solution.py:36
  12.9 0.0 copy-start
  12.9 0.9 %copy-done = f32[384,512]{1,0:T(8,128)} copy-done((f32[384,512]{1,0:T(8,128)}, f32[384,512]{1,0:T(8,128)S(1)}, u32[]{:S(2)}) %copy-start) | copy-done | bytes 786456
  13.8 0.0 copy-done.3
  13.8 0.1 copy.7.index_ref
  13.9 0.0 copy-done.2
  13.9 0.9 %shard_map.67.far_ref = s32[384,128]{1,0:T(8,128)S(1)} custom-call(s32[384,1]{1,0:T(8,128)S(1)} %copy.7.index_ref, s32[8]{0:T(128)S(1)} %copy-done.2), custom_call_target="tpu_custom_call" | custom-call | flops 1000 | bytes 1000 | tf_op jit(solution)/shard_map/pallas_call | solution.py:36
  14.9 0.5 collective-permute-done.rest_0_.rest_1_
  15.4 2.5 %collective-permute-start.2 = (bf16[128,2304]{1,0:T(8,128)(2,1)}, bf16[128,2304]{1,0:T(8,128)(2,1)S(1)}, u32[]{:S(2)}, u32[]{:S(2)}) collective-permute-start(bf16[128,2304]{1,0:T(8,128)(2,1)} %collective-permute-done.rest_0_.rest_1_), channel_id=1, source_target_pairs={{0,4},{5,1},{4,8},{9,5},{8,12},{13,9},{12,14},{15,13},{14,10},{11,... | collective-permute-start | bytes 1769480 | tf_op jit(solution)/shard_map/ppermute | solution.py:296
  17.9 2.0 %shard_map.68.rest_1_ = f32[384,64]{1,0:T(8,128)S(1)} custom-call(bf16[384,4096]{1,0:T(8,128)(2,1)S(1)} %get-tuple-element.74.x_ref, s32[384,128]{1,0:T(8,128)S(1)} %shard_map.67.far_ref, bf16[128,2304]{1,0:T(8,128)(2,1)} %shard_map.64.rest_0_), custom_call_target="tpu_custom_call" | custom-call | flops 1000 | bytes 1000 | tf_op jit(solution)/shard_map/pallas_call | solution.py:36
  19.9 2.0 %shard_map.69.rest_1_ = f32[384,64]{1,0:T(8,128)S(1)} custom-call(bf16[384,4096]{1,0:T(8,128)(2,1)S(1)} %get-tuple-element.74.x_ref, s32[384,128]{1,0:T(8,128)S(1)} %shard_map.67.far_ref, bf16[128,2304]{1,0:T(8,128)(2,1)} %collective-permute-done.rest_0_.rest_1_, f32[384,64]{1,0:T(8,128)S(1)} %shard_map.68.rest_1_), custom_call_target="tpu_custom_call" | custom-call | flops 1000 | bytes 1000 | tf_op jit(solution)/shard_map/pallas_call | solution.py:36
  21.9 0.0 collective-permute-done.1.rest_0_.rest_2_
  22.0 0.1 collective-permute-start.4
  22.0 2.0 %shard_map.70.rest_1_ = f32[384,64]{1,0:T(8,128)S(1)} custom-call(bf16[384,4096]{1,0:T(8,128)(2,1)S(1)} %get-tuple-element.74.x_ref, s32[384,128]{1,0:T(8,128)S(1)} %shard_map.67.far_ref, bf16[128,2304]{1,0:T(8,128)(2,1)} %collective-permute-done.1.rest_0_.rest_2_, f32[384,64]{1,0:T(8,128)S(1)} %shard_map.69.rest_1_), custom_call_target="tpu_custom_call" | custom-call | flops 1000 | bytes 1000 | tf_op jit(solution)/shard_map/pallas_call | solution.py:36
  24.1 5.1 %collective-permute-done.2.rest_0_.rest_3_ = bf16[128,2304]{1,0:T(8,128)(2,1)S(1)} collective-permute-done((bf16[128,2304]{1,0:T(8,128)(2,1)}, bf16[128,2304]{1,0:T(8,128)(2,1)S(1)}, u32[]{:S(2)}, u32[]{:S(2)}) %collective-permute-start.2) | collective-permute-done | bytes 589856 | tf_op jit(solution)/shard_map/ppermute | solution.py:296
  29.2 2.4 %collective-permute-start.5 = (bf16[128,2304]{1,0:T(8,128)(2,1)S(1)}, bf16[128,2304]{1,0:T(8,128)(2,1)S(1)}, u32[]{:S(2)}, u32[]{:S(2)}) collective-permute-start(bf16[128,2304]{1,0:T(8,128)(2,1)S(1)} %collective-permute-done.2.rest_0_.rest_3_), channel_id=1, source_target_pairs={{0,4},{5,1},{4,8},{9,5},{8,12},{13,9},{12,14},{15,13},{14,10},{11,... | collective-permute-start | bytes 1769480 | tf_op jit(solution)/shard_map/ppermute | solution.py:293
  31.6 0.0 collective-permute-done.3.there_ref
  31.6 4.2 %collective-permute-done.4.rest_0_.rest_4_ = bf16[128,2304]{1,0:T(8,128)(2,1)S(1)} collective-permute-done((bf16[128,2304]{1,0:T(8,128)(2,1)}, bf16[128,2304]{1,0:T(8,128)(2,1)S(1)}, u32[]{:S(2)}, u32[]{:S(2)}) %collective-permute-start.4) | collective-permute-done | bytes 589856 | tf_op jit(solution)/shard_map/ppermute | solution.py:297
  35.7 1.0 %shard_map.71.rest_1_ = f32[384,64]{1,0:T(8,128)S(1)} custom-call(bf16[384,4096]{1,0:T(8,128)(2,1)S(1)} %get-tuple-element.74.x_ref, s32[384,128]{1,0:T(8,128)S(1)} %shard_map.67.far_ref, bf16[128,2304]{1,0:T(8,128)(2,1)S(1)} %collective-permute-done.2.rest_0_.rest_3_, f32[384,64]{1,0:T(8,128)S(1)} %shard_map.70.rest_1_), custom_call_target="tpu_custom_call" | custom-call | flops 1000 | bytes 1000 | tf_op jit(solution)/shard_map/pallas_call | solution.py:36
  36.7 0.1 collective-permute-start.6
  36.8 0.9 %collective-permute-start.8 = (bf16[64,2304]{1,0:T(8,128)(2,1)S(1)}, bf16[64,2304]{1,0:T(8,128)(2,1)S(1)}, u32[]{:S(2)}, u32[]{:S(2)}) collective-permute-start(bf16[64,2304]{1,0:T(8,128)(2,1)S(1)} %get-tuple-element.81), channel_id=1, source_target_pairs={{4,0},{1,5},{8,4},{5,9},{12,8},{9,13},{14,12},{13,15},{10,14},{15,... | collective-permute-start | bytes 884744 | tf_op jit(solution)/shard_map/ppermute | solution.py:294
  37.7 1.0 %shard_map.72.own_ref = f32[384,64]{1,0:T(8,128)S(1)} custom-call(bf16[384,4096]{1,0:T(8,128)(2,1)S(1)} %get-tuple-element.74.x_ref, s32[384,128]{1,0:T(8,128)S(1)} %shard_map.67.far_ref, bf16[128,2304]{1,0:T(8,128)(2,1)S(1)} %collective-permute-done.4.rest_0_.rest_4_, f32[384,64]{1,0:T(8,128)S(1)} %shard_map.71.rest_1_), custom_call_target="tpu_custom_call" | custom-call | flops 1000 | bytes 1000 | tf_op jit(solution)/shard_map/pallas_call | solution.py:36
  38.7 0.0 copy-start.1
  38.7 3.5 %collective-permute-done.5.rest_0_ = bf16[128,2304]{1,0:T(8,128)(2,1)S(1)} collective-permute-done((bf16[128,2304]{1,0:T(8,128)(2,1)S(1)}, bf16[128,2304]{1,0:T(8,128)(2,1)S(1)}, u32[]{:S(2)}, u32[]{:S(2)}) %collective-permute-start.5) | collective-permute-done | bytes 589856 | tf_op jit(solution)/shard_map/ppermute | solution.py:293
  42.3 2.5 %collective-permute-start.9 = (bf16[64,2304]{1,0:T(8,128)(2,1)S(1)}, bf16[64,2304]{1,0:T(8,128)(2,1)S(1)}, u32[]{:S(2)}, u32[]{:S(2)}) collective-permute-start(bf16[64,2304]{1,0:T(8,128)(2,1)S(1)} %slice.11), channel_id=1, source_target_pairs={{0,4},{5,1},{4,8},{9,5},{8,12},{13,9},{12,14},{15,13},{14,10},{11,... | collective-permute-start | bytes 884744 | tf_op jit(solution)/shard_map/ppermute | solution.py:322
  44.8 0.9 %collective-permute-done.6.rest_1_.rest_2_ = bf16[64,2304]{1,0:T(8,128)(2,1)S(1)} collective-permute-done((bf16[64,2304]{1,0:T(8,128)(2,1)S(1)}, bf16[64,2304]{1,0:T(8,128)(2,1)S(1)}, u32[]{:S(2)}, u32[]{:S(2)}) %collective-permute-start.6) | collective-permute-done | bytes 294944 | tf_op jit(solution)/shard_map/ppermute | solution.py:294
  45.7 0.0 collective-permute-start.10
  45.7 0.0 collective-permute-start.7
  45.7 1.0 %shard_map.74.rest_2_ = f32[384,64]{1,0:T(8,128)S(1)} custom-call(bf16[384,4096]{1,0:T(8,128)(2,1)S(1)} %get-tuple-element.74.x_ref, s32[384,128]{1,0:T(8,128)S(1)} %shard_map.67.far_ref, bf16[128,2304]{1,0:T(8,128)(2,1)S(1)} %collective-permute-done.5.rest_0_), custom_call_target="tpu_custom_call" | custom-call | flops 1000 | bytes 1000 | tf_op jit(solution)/shard_map/pallas_call | solution.py:36
  46.7 0.5 collective-permute-done.7.other_ref
  47.1 0.0 copy-done.1
  47.1 2.2 %shard_map.73.base_ref = f32[384,512]{1,0:T(8,128)S(1)} custom-call(s32[384,128]{1,0:T(8,128)S(1)} %shard_map.67.far_ref, f32[384,64]{1,0:T(8,128)S(1)} %shard_map.72.own_ref, f32[384,64]{1,0:T(8,128)S(1)} %collective-permute-done.7.other_ref, f32[384,512]{1,0:T(8,128)S(1)} %copy-done.1, f32[384,512]{1,0:T(8,128)} %collective-permute-done.3.there_ref, ...), custom_call_target="tpu_custom_call" | custom-call | flops 1000 | bytes 1000 | tf_op jit(solution)/shard_map/pallas_call | solution.py:36
  49.3 0.5 collective-permute-done.8.rest_0_.rest_1_
  49.8 1.0 %shard_map.75.rest_1_ = f32[384,64]{1,0:T(8,128)S(1)} custom-call(bf16[384,4096]{1,0:T(8,128)(2,1)S(1)} %get-tuple-element.74.x_ref, s32[384,128]{1,0:T(8,128)S(1)} %shard_map.67.far_ref, bf16[64,2304]{1,0:T(8,128)(2,1)S(1)} %collective-permute-done.8.rest_0_.rest_1_, bf16[64,2304]{1,0:T(8,128)(2,1)S(1)} %collective-permute-done.6.rest_1_.rest_2_, ...), custom_call_target="tpu_custom_call" | custom-call | flops 1000 | bytes 1000 | tf_op jit(solution)/shard_map/pallas_call | solution.py:36
  50.8 0.9 %collective-permute-done.9.m_ref.rest_3_ = bf16[64,2304]{1,0:T(8,128)(2,1)S(1)} collective-permute-done((bf16[64,2304]{1,0:T(8,128)(2,1)S(1)}, bf16[64,2304]{1,0:T(8,128)(2,1)S(1)}, u32[]{:S(2)}, u32[]{:S(2)}) %collective-permute-start.9) | collective-permute-done | bytes 294944 | tf_op jit(solution)/shard_map/ppermute | solution.py:322
  51.7 0.6 shard_map.76.rest_0_
  52.3 0.7 %collective-permute-done.10.m_ref.rest_4_ = bf16[64,2304]{1,0:T(8,128)(2,1)S(1)} collective-permute-done((bf16[64,2304]{1,0:T(8,128)(2,1)S(1)}, bf16[64,2304]{1,0:T(8,128)(2,1)S(1)}, u32[]{:S(2)}, u32[]{:S(2)}) %collective-permute-start.10) | collective-permute-done | bytes 294944 | tf_op jit(solution)/shard_map/ppermute | solution.py:323
  53.0 0.6 %shard_map.77.own_ref = f32[192,128]{1,0:T(8,128)S(1)} custom-call(bf16[384,4096]{1,0:T(8,128)(2,1)S(1)} %get-tuple-element.74.x_ref, s32[384,128]{1,0:T(8,128)S(1)} %shard_map.67.far_ref, bf16[64,2304]{1,0:T(8,128)(2,1)S(1)} %collective-permute-done.10.m_ref.rest_4_, f32[384,64]{1,0:T(8,128)S(1)} %shard_map.76.rest_0_, f32[384,64]{1,0:T(8,128)S(1)} %shard_map.75.rest_1_), custom_call_target="tpu_custom_call" | custom-call | flops 1000 | bytes 1000 | tf_op jit(solution)/shard_map/pallas_call | solution.py:36
  53.6 0.1 collective-permute-start.11
  53.7 1.3 %collective-permute-done.11.other_ref = f32[192,128]{1,0:T(8,128)S(1)} collective-permute-done((f32[192,128]{1,0:T(8,128)S(1)}, f32[192,128]{1,0:T(8,128)S(1)}, u32[]{:S(2)}, u32[]{:S(2)}) %collective-permute-start.11) | collective-permute-done | bytes 98336 | tf_op jit(solution)/shard_map/ppermute | solution.py:363
  55.0 1.2 %shard_map.78 = bf16[384,512]{1,0:T(8,128)(2,1)} custom-call(s32[384,128]{1,0:T(8,128)S(1)} %shard_map.67.far_ref, f32[192,128]{1,0:T(8,128)S(1)} %shard_map.77.own_ref, f32[192,128]{1,0:T(8,128)S(1)} %collective-permute-done.11.other_ref, f32[384,512]{1,0:T(8,128)S(1)} %shard_map.73.base_ref, bf16[128,2304]{1,0:T(8,128)(2,1)S(1)} %collective-permute-done.5.rest_0_, ...), custom_call_target="tpu_custom_call" | custom-call | flops 1000 | bytes 1000 | tf_op jit(solution)/shard_map/pallas_call | solution.py:36
  (2 shorter events, 0.1 us)
Async XLA Ops:
  1.8 13.6 %collective-permute-start = (bf16[128,2304]{1,0:T(8,128)(2,1)}, bf16[128,2304]{1,0:T(8,128)(2,1)}, u32[]{:S(2)}, u32[]{:S(2)}) collective-permute-start(bf16[128,2304]{1,0:T(8,128)(2,1)} %shard_map.64.rest_0_), channel_id=1, source_target_pairs={{0,4},{5,1},{4,8},{9,5},{8,12},{13,9},{12,14},{15,13},{14,10},{11,... | collective-permute-start | bytes 1769480 | tf_op jit(solution)/shard_map/ppermute | solution.py:296
  9.4 12.5 %collective-permute-start.1 = (bf16[128,2304]{1,0:T(8,128)(2,1)}, bf16[128,2304]{1,0:T(8,128)(2,1)}, u32[]{:S(2)}, u32[]{:S(2)}) collective-permute-start(bf16[128,2304]{1,0:T(8,128)(2,1)} %shard_map.64.rest_0_), channel_id=1, source_target_pairs={{4,0},{1,5},{8,4},{5,9},{12,8},{9,13},{14,12},{13,15},{10,14},{15,... | collective-permute-start | bytes 1769480 | tf_op jit(solution)/shard_map/ppermute | solution.py:297
  9.5 22.0 %collective-permute-start.3 = (f32[384,512]{1,0:T(8,128)}, f32[384,512]{1,0:T(8,128)}, u32[]{:S(2)}, u32[]{:S(2)}) collective-permute-start(f32[384,512]{1,0:T(8,128)} %get-tuple-element.46), channel_id=1, source_target_pairs={{0,1},{1,0},{2,3},{3,2},{4,5},{5,4},{6,7},{7,6},{8,9},{9,8},{10,11... | collective-permute-start | bytes 2359304 | tf_op jit(solution)/shard_map/ppermute | solution.py:262
  9.6 4.2 %copy-start.3 = (s32[384,1]{0,1:T(1,128)S(1)}, s32[384,1]{0,1:T(1,128)}, u32[]{:S(2)}) copy-start(s32[384,1]{0,1:T(1,128)} %param.7) | copy-start | bytes 4612
  9.6 4.3 %copy-start.2 = (s32[8]{0:T(128)S(1)}, s32[8]{0:T(128)}, u32[]{:S(2)}) copy-start(s32[8]{0:T(128)} %storage_ref.1) | copy-start | bytes 100
  12.9 0.9 %copy-start = (f32[384,512]{1,0:T(8,128)}, f32[384,512]{1,0:T(8,128)S(1)}, u32[]{:S(2)}) copy-start(f32[384,512]{1,0:T(8,128)S(1)} %shard_map.66.here_ref) | copy-start | bytes 2359300
  15.4 13.8 %collective-permute-start.2 = (bf16[128,2304]{1,0:T(8,128)(2,1)}, bf16[128,2304]{1,0:T(8,128)(2,1)S(1)}, u32[]{:S(2)}, u32[]{:S(2)}) collective-permute-start(bf16[128,2304]{1,0:T(8,128)(2,1)} %collective-permute-done.rest_0_.rest_1_), channel_id=1, source_target_pairs={{0,4},{5,1},{4,8},{9,5},{8,12},{13,9},{12,14},{15,13},{14,10},{11,... | collective-permute-start | bytes 1769480 | tf_op jit(solution)/shard_map/ppermute | solution.py:296
  22.0 13.8 %collective-permute-start.4 = (bf16[128,2304]{1,0:T(8,128)(2,1)}, bf16[128,2304]{1,0:T(8,128)(2,1)S(1)}, u32[]{:S(2)}, u32[]{:S(2)}) collective-permute-start(bf16[128,2304]{1,0:T(8,128)(2,1)} %collective-permute-done.1.rest_0_.rest_2_), channel_id=1, source_target_pairs={{4,0},{1,5},{8,4},{5,9},{12,8},{9,13},{14,12},{13,15},{10,14},{15,... | collective-permute-start | bytes 1769480 | tf_op jit(solution)/shard_map/ppermute | solution.py:297
  29.2 13.1 %collective-permute-start.5 = (bf16[128,2304]{1,0:T(8,128)(2,1)S(1)}, bf16[128,2304]{1,0:T(8,128)(2,1)S(1)}, u32[]{:S(2)}, u32[]{:S(2)}) collective-permute-start(bf16[128,2304]{1,0:T(8,128)(2,1)S(1)} %collective-permute-done.2.rest_0_.rest_3_), channel_id=1, source_target_pairs={{0,4},{5,1},{4,8},{9,5},{8,12},{13,9},{12,14},{15,13},{14,10},{11,... | collective-permute-start | bytes 1769480 | tf_op jit(solution)/shard_map/ppermute | solution.py:293
  36.7 9.0 %collective-permute-start.6 = (bf16[64,2304]{1,0:T(8,128)(2,1)S(1)}, bf16[64,2304]{1,0:T(8,128)(2,1)S(1)}, u32[]{:S(2)}, u32[]{:S(2)}) collective-permute-start(bf16[64,2304]{1,0:T(8,128)(2,1)S(1)} %get-tuple-element.82), channel_id=1, source_target_pairs={{4,0},{1,5},{8,4},{5,9},{12,8},{9,13},{14,12},{13,15},{10,14},{15,... | collective-permute-start | bytes 884744 | tf_op jit(solution)/shard_map/ppermute | solution.py:294
  36.8 13.0 %collective-permute-start.8 = (bf16[64,2304]{1,0:T(8,128)(2,1)S(1)}, bf16[64,2304]{1,0:T(8,128)(2,1)S(1)}, u32[]{:S(2)}, u32[]{:S(2)}) collective-permute-start(bf16[64,2304]{1,0:T(8,128)(2,1)S(1)} %get-tuple-element.81), channel_id=1, source_target_pairs={{4,0},{1,5},{8,4},{5,9},{12,8},{9,13},{14,12},{13,15},{10,14},{15,... | collective-permute-start | bytes 884744 | tf_op jit(solution)/shard_map/ppermute | solution.py:294
  38.7 8.5 %copy-start.1 = (f32[384,512]{1,0:T(8,128)S(1)}, f32[384,512]{1,0:T(8,128)}, u32[]{:S(2)}) copy-start(f32[384,512]{1,0:T(8,128)} %copy-done) | copy-start | bytes 2359300
  42.3 9.4 %collective-permute-start.9 = (bf16[64,2304]{1,0:T(8,128)(2,1)S(1)}, bf16[64,2304]{1,0:T(8,128)(2,1)S(1)}, u32[]{:S(2)}, u32[]{:S(2)}) collective-permute-start(bf16[64,2304]{1,0:T(8,128)(2,1)S(1)} %slice.11), channel_id=1, source_target_pairs={{0,4},{5,1},{4,8},{9,5},{8,12},{13,9},{12,14},{15,13},{14,10},{11,... | collective-permute-start | bytes 884744 | tf_op jit(solution)/shard_map/ppermute | solution.py:322
  45.7 7.3 %collective-permute-start.10 = (bf16[64,2304]{1,0:T(8,128)(2,1)S(1)}, bf16[64,2304]{1,0:T(8,128)(2,1)S(1)}, u32[]{:S(2)}, u32[]{:S(2)}) collective-permute-start(bf16[64,2304]{1,0:T(8,128)(2,1)S(1)} %collective-permute-done.6.rest_1_.rest_2_), channel_id=1, source_target_pairs={{4,0},{1,5},{8,4},{5,9},{12,8},{9,13},{14,12},{13,15},{10,14},{15,... | collective-permute-start | bytes 884744 | tf_op jit(solution)/shard_map/ppermute | solution.py:323
  45.7 1.4 %collective-permute-start.7 = (f32[384,64]{1,0:T(8,128)S(1)}, f32[384,64]{1,0:T(8,128)S(1)}, u32[]{:S(2)}, u32[]{:S(2)}) collective-permute-start(f32[384,64]{1,0:T(8,128)S(1)} %shard_map.72.own_ref), channel_id=1, source_target_pairs={{0,1},{1,0},{2,3},{3,2},{4,5},{5,4},{6,7},{7,6},{8,9},{9,8},{10,11... | collective-permute-start | bytes 294920 | tf_op jit(solution)/shard_map/ppermute | solution.py:329
  53.6 1.4 %collective-permute-start.11 = (f32[192,128]{1,0:T(8,128)S(1)}, f32[192,128]{1,0:T(8,128)S(1)}, u32[]{:S(2)}, u32[]{:S(2)}) collective-permute-start(f32[192,128]{1,0:T(8,128)S(1)} %shard_map.77.own_ref), channel_id=1, source_target_pairs={{0,1},{1,0},{2,3},{3,2},{4,5},{5,4},{6,7},{7,6},{8,9},{9,8},{10,11... | collective-permute-start | bytes 294920 | tf_op jit(solution)/shard_map/ppermute | solution.py:363

commit v10 on v9

--- a/solution.py
+++ b/solution.py
@@ -72,7 +72,7 @@
 
 def far_kernel(n, index_ref, storage_ref, o_ref):
     here = place_in(n, lax.axis_index("dp"))
-    way = 1 - 2 * lax.axis_index("tensor")
+    way = 2 * lax.axis_index("tensor") - 1
     index = index_ref[...]
 
     def look(j, far):
@@ -221,8 +221,8 @@
     forth, back = [], []
     for j in range(n):
         a, b = order[j], order[(j + 1) % n]
-        forth += [(2 * a, 2 * b), (2 * b + 1, 2 * a + 1)]
-        back += [(2 * b, 2 * a), (2 * a + 1, 2 * b + 1)]
+        back += [(2 * a, 2 * b), (2 * b + 1, 2 * a + 1)]
+        forth += [(2 * b, 2 * a), (2 * a + 1, 2 * b + 1)]
     swap = [(0, 1), (1, 0)]
     both = ("dp", "tensor")
 

time: 56.5 us -> 56.3 us (level)
    ppermute x3, waiting for transfers between devices: 9.16 us -> 8.43 us  [shards(): p = (lax.ppermute(p, both, forth),)]
where the time goes in v10:
time: 56.3 us; the launch traced here: 56 us
  Pallas kernels  25 us (44%)
  waiting for transfers between devices  17.8 us (32%)
  starting transfers between devices  11.9 us (21%)
  local copies, waits for them, and re-layouts  1.09 us (2%)
    pallas_call x15, Pallas kernels, call(): pl.pallas_call(kernel, in_specs=in_specs, out_specs=[out_space] * len(out...  25 us
    ppermute x3, waiting for transfers between devices, shards(): p = (lax.ppermute(p, both, forth),)  8.43 us
    ppermute x3, starting transfers between devices, shards(): p = (lax.ppermute(p, both, forth),)  7.85 us
    ppermute x2, waiting for transfers between devices, shards(): q = (lax.ppermute(q, both, back),)  4.3 us
    ppermute x1, starting transfers between devices, shards(): p = lax.ppermute(p, both, forth)  2.53 us
    ppermute x2, waiting for transfers between devices, shards(): other = lax.ppermute(total, 'tensor', swap)  1.76 us
    ppermute x2, waiting for transfers between devices, shards(): q = tuple((lax.ppermute(h, both, back) for h in (q[rank:], q[:rank])))[::-1]  1.66 us
    ppermute x2, starting transfers between devices, shards(): q = tuple((lax.ppermute(h, both, back) for h in (q[rank:], q[:rank])))[::-1]  1.22 us
  transfers between devices with their start and end apart: 12, of which 10 were waited for; matrix products, arithmetic and copies ran while one was open for 0% of the time, Pallas kernels for 38%

profile of v10, /device:TPU:0, one launch (start us, length us, event | category | flops | bytes accessed | tf_op | source)
XLA Modules:
  0.0 56.0 jit_solution(495649595721560798)
XLA Ops:
  0.0 1.8 %shard_map.64.rest_0_ = bf16[128,2304]{1,0:T(8,128)(2,1)} custom-call(bf16[64,4096]{1,0:T(8,128)(2,1)} %bitcast.4, bf16[64,1024]{1,0:T(8,128)(2,1)} %bitcast.5), custom_call_target="tpu_custom_call" | custom-call | flops 1000 | bytes 1000 | tf_op jit(solution)/shard_map/pallas_call | solution.py:36
  1.8 3.0 %collective-permute-start = (bf16[128,2304]{1,0:T(8,128)(2,1)}, bf16[128,2304]{1,0:T(8,128)(2,1)}, u32[]{:S(2)}, u32[]{:S(2)}) collective-permute-start(bf16[128,2304]{1,0:T(8,128)(2,1)} %shard_map.64.rest_0_), channel_id=1, source_target_pairs={{4,0},{1,5},{8,4},{5,9},{12,8},{9,13},{14,12},{13,15},{10,14},{15,... | collective-permute-start | bytes 1769480 | tf_op jit(solution)/shard_map/ppermute | solution.py:296
  4.8 4.5 %shard_map.65 = (bf16[384,4096]{1,0:T(8,128)(2,1)S(1)}, f32[384,512]{1,0:T(8,128)}) custom-call(bf16[384,4096]{1,0:T(8,128)(2,1)} %x_hbm, bf16[4096,1024]{1,0:T(8,128)(2,1)} %w_hbm.2), custom_call_target="tpu_custom_call" | custom-call | flops 1000 | bytes 1000 | tf_op jit(solution)/shard_map/pallas_call | solution.py:36
  9.4 0.2 collective-permute-start.1
  9.5 0.0 collective-permute-start.3
  9.5 0.0 copy-start.3
  9.5 0.0 copy-start.2
  9.5 3.3 %shard_map.66.here_ref = f32[384,512]{1,0:T(8,128)S(1)} custom-call(bf16[384,4096]{1,0:T(8,128)(2,1)S(1)} %get-tuple-element.74.x_ref, bf16[4096,1024]{1,0:T(8,128)(2,1)} %w_hbm.2), custom_call_target="tpu_custom_call" | custom-call | flops 1000 | bytes 1000 | tf_op jit(solution)/shard_map/pallas_call | solution.py:36
  12.8 0.0 copy-start
  12.8 0.9 %copy-done = f32[384,512]{1,0:T(8,128)} copy-done((f32[384,512]{1,0:T(8,128)}, f32[384,512]{1,0:T(8,128)S(1)}, u32[]{:S(2)}) %copy-start) | copy-done | bytes 786456
  13.7 0.0 copy-done.3
  13.7 0.1 copy.7.index_ref
  13.9 0.0 copy-done.2
  13.9 0.9 %shard_map.67.far_ref = s32[384,128]{1,0:T(8,128)S(1)} custom-call(s32[384,1]{1,0:T(8,128)S(1)} %copy.7.index_ref, s32[8]{0:T(128)S(1)} %copy-done.2), custom_call_target="tpu_custom_call" | custom-call | flops 1000 | bytes 1000 | tf_op jit(solution)/shard_map/pallas_call | solution.py:36
  14.8 0.4 collective-permute-done.rest_0_.rest_1_
  15.3 2.5 %collective-permute-start.2 = (bf16[128,2304]{1,0:T(8,128)(2,1)}, bf16[128,2304]{1,0:T(8,128)(2,1)S(1)}, u32[]{:S(2)}, u32[]{:S(2)}) collective-permute-start(bf16[128,2304]{1,0:T(8,128)(2,1)} %collective-permute-done.rest_0_.rest_1_), channel_id=1, source_target_pairs={{4,0},{1,5},{8,4},{5,9},{12,8},{9,13},{14,12},{13,15},{10,14},{15,... | collective-permute-start | bytes 1769480 | tf_op jit(solution)/shard_map/ppermute | solution.py:296
  17.7 2.0 %shard_map.68.rest_1_ = f32[384,64]{1,0:T(8,128)S(1)} custom-call(bf16[384,4096]{1,0:T(8,128)(2,1)S(1)} %get-tuple-element.74.x_ref, s32[384,128]{1,0:T(8,128)S(1)} %shard_map.67.far_ref, bf16[128,2304]{1,0:T(8,128)(2,1)} %shard_map.64.rest_0_), custom_call_target="tpu_custom_call" | custom-call | flops 1000 | bytes 1000 | tf_op jit(solution)/shard_map/pallas_call | solution.py:36
  19.8 2.0 %shard_map.69.rest_1_ = f32[384,64]{1,0:T(8,128)S(1)} custom-call(bf16[384,4096]{1,0:T(8,128)(2,1)S(1)} %get-tuple-element.74.x_ref, s32[384,128]{1,0:T(8,128)S(1)} %shard_map.67.far_ref, bf16[128,2304]{1,0:T(8,128)(2,1)} %collective-permute-done.rest_0_.rest_1_, f32[384,64]{1,0:T(8,128)S(1)} %shard_map.68.rest_1_), custom_call_target="tpu_custom_call" | custom-call | flops 1000 | bytes 1000 | tf_op jit(solution)/shard_map/pallas_call | solution.py:36
  21.8 0.0 collective-permute-done.1.rest_0_.rest_2_
  21.8 0.1 collective-permute-start.4
  21.9 2.0 %shard_map.70.rest_1_ = f32[384,64]{1,0:T(8,128)S(1)} custom-call(bf16[384,4096]{1,0:T(8,128)(2,1)S(1)} %get-tuple-element.74.x_ref, s32[384,128]{1,0:T(8,128)S(1)} %shard_map.67.far_ref, bf16[128,2304]{1,0:T(8,128)(2,1)} %collective-permute-done.1.rest_0_.rest_2_, f32[384,64]{1,0:T(8,128)S(1)} %shard_map.69.rest_1_), custom_call_target="tpu_custom_call" | custom-call | flops 1000 | bytes 1000 | tf_op jit(solution)/shard_map/pallas_call | solution.py:36
  23.9 5.0 %collective-permute-done.2.rest_0_.rest_3_ = bf16[128,2304]{1,0:T(8,128)(2,1)S(1)} collective-permute-done((bf16[128,2304]{1,0:T(8,128)(2,1)}, bf16[128,2304]{1,0:T(8,128)(2,1)S(1)}, u32[]{:S(2)}, u32[]{:S(2)}) %collective-permute-start.2) | collective-permute-done | bytes 589856 | tf_op jit(solution)/shard_map/ppermute | solution.py:296
  28.9 2.4 %collective-permute-start.5 = (bf16[128,2304]{1,0:T(8,128)(2,1)S(1)}, bf16[128,2304]{1,0:T(8,128)(2,1)S(1)}, u32[]{:S(2)}, u32[]{:S(2)}) collective-permute-start(bf16[128,2304]{1,0:T(8,128)(2,1)S(1)} %collective-permute-done.2.rest_0_.rest_3_), channel_id=1, source_target_pairs={{4,0},{1,5},{8,4},{5,9},{12,8},{9,13},{14,12},{13,15},{10,14},{15,... | collective-permute-start | bytes 1769480 | tf_op jit(solution)/shard_map/ppermute | solution.py:293
  31.3 0.0 collective-permute-done.3.there_ref
  31.3 4.3 %collective-permute-done.4.rest_0_.rest_4_ = bf16[128,2304]{1,0:T(8,128)(2,1)S(1)} collective-permute-done((bf16[128,2304]{1,0:T(8,128)(2,1)}, bf16[128,2304]{1,0:T(8,128)(2,1)S(1)}, u32[]{:S(2)}, u32[]{:S(2)}) %collective-permute-start.4) | collective-permute-done | bytes 589856 | tf_op jit(solution)/shard_map/ppermute | solution.py:297
  35.6 1.0 %shard_map.71.rest_1_ = f32[384,64]{1,0:T(8,128)S(1)} custom-call(bf16[384,4096]{1,0:T(8,128)(2,1)S(1)} %get-tuple-element.74.x_ref, s32[384,128]{1,0:T(8,128)S(1)} %shard_map.67.far_ref, bf16[128,2304]{1,0:T(8,128)(2,1)S(1)} %collective-permute-done.2.rest_0_.rest_3_, f32[384,64]{1,0:T(8,128)S(1)} %shard_map.70.rest_1_), custom_call_target="tpu_custom_call" | custom-call | flops 1000 | bytes 1000 | tf_op jit(solution)/shard_map/pallas_call | solution.py:36
  36.6 0.1 collective-permute-start.6
  36.6 1.2 %collective-permute-start.8 = (bf16[64,2304]{1,0:T(8,128)(2,1)S(1)}, bf16[64,2304]{1,0:T(8,128)(2,1)S(1)}, u32[]{:S(2)}, u32[]{:S(2)}) collective-permute-start(bf16[64,2304]{1,0:T(8,128)(2,1)S(1)} %get-tuple-element.81), channel_id=1, source_target_pairs={{0,4},{5,1},{4,8},{9,5},{8,12},{13,9},{12,14},{15,13},{14,10},{11,... | collective-permute-start | bytes 884744 | tf_op jit(solution)/shard_map/ppermute | solution.py:294
  37.8 1.0 %shard_map.72.own_ref = f32[384,64]{1,0:T(8,128)S(1)} custom-call(bf16[384,4096]{1,0:T(8,128)(2,1)S(1)} %get-tuple-element.74.x_ref, s32[384,128]{1,0:T(8,128)S(1)} %shard_map.67.far_ref, bf16[128,2304]{1,0:T(8,128)(2,1)S(1)} %collective-permute-done.4.rest_0_.rest_4_, f32[384,64]{1,0:T(8,128)S(1)} %shard_map.71.rest_1_), custom_call_target="tpu_custom_call" | custom-call | flops 1000 | bytes 1000 | tf_op jit(solution)/shard_map/pallas_call | solution.py:36
  38.8 0.0 copy-start.1
  38.8 3.0 %collective-permute-done.5.rest_0_ = bf16[128,2304]{1,0:T(8,128)(2,1)S(1)} collective-permute-done((bf16[128,2304]{1,0:T(8,128)(2,1)S(1)}, bf16[128,2304]{1,0:T(8,128)(2,1)S(1)}, u32[]{:S(2)}, u32[]{:S(2)}) %collective-permute-start.5) | collective-permute-done | bytes 589856 | tf_op jit(solution)/shard_map/ppermute | solution.py:293
  41.8 2.5 %collective-permute-start.9 = (bf16[64,2304]{1,0:T(8,128)(2,1)S(1)}, bf16[64,2304]{1,0:T(8,128)(2,1)S(1)}, u32[]{:S(2)}, u32[]{:S(2)}) collective-permute-start(bf16[64,2304]{1,0:T(8,128)(2,1)S(1)} %slice.11), channel_id=1, source_target_pairs={{4,0},{1,5},{8,4},{5,9},{12,8},{9,13},{14,12},{13,15},{10,14},{15,... | collective-permute-start | bytes 884744 | tf_op jit(solution)/shard_map/ppermute | solution.py:322
  44.4 1.1 %collective-permute-done.6.rest_1_.rest_2_ = bf16[64,2304]{1,0:T(8,128)(2,1)S(1)} collective-permute-done((bf16[64,2304]{1,0:T(8,128)(2,1)S(1)}, bf16[64,2304]{1,0:T(8,128)(2,1)S(1)}, u32[]{:S(2)}, u32[]{:S(2)}) %collective-permute-start.6) | collective-permute-done | bytes 294944 | tf_op jit(solution)/shard_map/ppermute | solution.py:294
  45.5 0.0 collective-permute-start.10
  45.5 0.0 collective-permute-start.7
  45.5 1.0 %shard_map.74.rest_2_ = f32[384,64]{1,0:T(8,128)S(1)} custom-call(bf16[384,4096]{1,0:T(8,128)(2,1)S(1)} %get-tuple-element.74.x_ref, s32[384,128]{1,0:T(8,128)S(1)} %shard_map.67.far_ref, bf16[128,2304]{1,0:T(8,128)(2,1)S(1)} %collective-permute-done.5.rest_0_), custom_call_target="tpu_custom_call" | custom-call | flops 1000 | bytes 1000 | tf_op jit(solution)/shard_map/pallas_call | solution.py:36
  46.4 0.5 collective-permute-done.7.other_ref
  46.9 0.0 copy-done.1
  46.9 2.2 %shard_map.73.base_ref = f32[384,512]{1,0:T(8,128)S(1)} custom-call(s32[384,128]{1,0:T(8,128)S(1)} %shard_map.67.far_ref, f32[384,64]{1,0:T(8,128)S(1)} %shard_map.72.own_ref, f32[384,64]{1,0:T(8,128)S(1)} %collective-permute-done.7.other_ref, f32[384,512]{1,0:T(8,128)S(1)} %copy-done.1, f32[384,512]{1,0:T(8,128)} %collective-permute-done.3.there_ref, ...), custom_call_target="tpu_custom_call" | custom-call | flops 1000 | bytes 1000 | tf_op jit(solution)/shard_map/pallas_call | solution.py:36
  49.1 0.6 %collective-permute-done.8.rest_0_.rest_1_ = bf16[64,2304]{1,0:T(8,128)(2,1)S(1)} collective-permute-done((bf16[64,2304]{1,0:T(8,128)(2,1)S(1)}, bf16[64,2304]{1,0:T(8,128)(2,1)S(1)}, u32[]{:S(2)}, u32[]{:S(2)}) %collective-permute-start.8) | collective-permute-done | bytes 294944 | tf_op jit(solution)/shard_map/ppermute | solution.py:294
  49.7 1.0 %shard_map.75.rest_1_ = f32[384,64]{1,0:T(8,128)S(1)} custom-call(bf16[384,4096]{1,0:T(8,128)(2,1)S(1)} %get-tuple-element.74.x_ref, s32[384,128]{1,0:T(8,128)S(1)} %shard_map.67.far_ref, bf16[64,2304]{1,0:T(8,128)(2,1)S(1)} %collective-permute-done.8.rest_0_.rest_1_, bf16[64,2304]{1,0:T(8,128)(2,1)S(1)} %collective-permute-done.6.rest_1_.rest_2_, ...), custom_call_target="tpu_custom_call" | custom-call | flops 1000 | bytes 1000 | tf_op jit(solution)/shard_map/pallas_call | solution.py:36
  50.6 0.8 %collective-permute-done.9.m_ref.rest_3_ = bf16[64,2304]{1,0:T(8,128)(2,1)S(1)} collective-permute-done((bf16[64,2304]{1,0:T(8,128)(2,1)S(1)}, bf16[64,2304]{1,0:T(8,128)(2,1)S(1)}, u32[]{:S(2)}, u32[]{:S(2)}) %collective-permute-start.9) | collective-permute-done | bytes 294944 | tf_op jit(solution)/shard_map/ppermute | solution.py:322
  51.4 0.6 shard_map.76.rest_0_
  52.0 0.9 %collective-permute-done.10.m_ref.rest_4_ = bf16[64,2304]{1,0:T(8,128)(2,1)S(1)} collective-permute-done((bf16[64,2304]{1,0:T(8,128)(2,1)S(1)}, bf16[64,2304]{1,0:T(8,128)(2,1)S(1)}, u32[]{:S(2)}, u32[]{:S(2)}) %collective-permute-start.10) | collective-permute-done | bytes 294944 | tf_op jit(solution)/shard_map/ppermute | solution.py:323
  52.8 0.6 %shard_map.77.own_ref = f32[192,128]{1,0:T(8,128)S(1)} custom-call(bf16[384,4096]{1,0:T(8,128)(2,1)S(1)} %get-tuple-element.74.x_ref, s32[384,128]{1,0:T(8,128)S(1)} %shard_map.67.far_ref, bf16[64,2304]{1,0:T(8,128)(2,1)S(1)} %collective-permute-done.10.m_ref.rest_4_, f32[384,64]{1,0:T(8,128)S(1)} %shard_map.76.rest_0_, f32[384,64]{1,0:T(8,128)S(1)} %shard_map.75.rest_1_), custom_call_target="tpu_custom_call" | custom-call | flops 1000 | bytes 1000 | tf_op jit(solution)/shard_map/pallas_call | solution.py:36
  53.5 0.1 collective-permute-start.11
  53.5 1.3 %collective-permute-done.11.other_ref = f32[192,128]{1,0:T(8,128)S(1)} collective-permute-done((f32[192,128]{1,0:T(8,128)S(1)}, f32[192,128]{1,0:T(8,128)S(1)}, u32[]{:S(2)}, u32[]{:S(2)}) %collective-permute-start.11) | collective-permute-done | bytes 98336 | tf_op jit(solution)/shard_map/ppermute | solution.py:363
  54.8 1.2 %shard_map.78 = bf16[384,512]{1,0:T(8,128)(2,1)} custom-call(s32[384,128]{1,0:T(8,128)S(1)} %shard_map.67.far_ref, f32[192,128]{1,0:T(8,128)S(1)} %shard_map.77.own_ref, f32[192,128]{1,0:T(8,128)S(1)} %collective-permute-done.11.other_ref, f32[384,512]{1,0:T(8,128)S(1)} %shard_map.73.base_ref, bf16[128,2304]{1,0:T(8,128)(2,1)S(1)} %collective-permute-done.5.rest_0_, ...), custom_call_target="tpu_custom_call" | custom-call | flops 1000 | bytes 1000 | tf_op jit(solution)/shard_map/pallas_call | solution.py:36
  (2 shorter events, 0.1 us)
Async XLA Ops:
  1.8 13.4 %collective-permute-start = (bf16[128,2304]{1,0:T(8,128)(2,1)}, bf16[128,2304]{1,0:T(8,128)(2,1)}, u32[]{:S(2)}, u32[]{:S(2)}) collective-permute-start(bf16[128,2304]{1,0:T(8,128)(2,1)} %shard_map.64.rest_0_), channel_id=1, source_target_pairs={{4,0},{1,5},{8,4},{5,9},{12,8},{9,13},{14,12},{13,15},{10,14},{15,... | collective-permute-start | bytes 1769480 | tf_op jit(solution)/shard_map/ppermute | solution.py:296
  9.4 12.4 %collective-permute-start.1 = (bf16[128,2304]{1,0:T(8,128)(2,1)}, bf16[128,2304]{1,0:T(8,128)(2,1)}, u32[]{:S(2)}, u32[]{:S(2)}) collective-permute-start(bf16[128,2304]{1,0:T(8,128)(2,1)} %shard_map.64.rest_0_), channel_id=1, source_target_pairs={{0,4},{5,1},{4,8},{9,5},{8,12},{13,9},{12,14},{15,13},{14,10},{11,... | collective-permute-start | bytes 1769480 | tf_op jit(solution)/shard_map/ppermute | solution.py:297
  9.5 21.8 %collective-permute-start.3 = (f32[384,512]{1,0:T(8,128)}, f32[384,512]{1,0:T(8,128)}, u32[]{:S(2)}, u32[]{:S(2)}) collective-permute-start(f32[384,512]{1,0:T(8,128)} %get-tuple-element.46), channel_id=1, source_target_pairs={{0,1},{1,0},{2,3},{3,2},{4,5},{5,4},{6,7},{7,6},{8,9},{9,8},{10,11... | collective-permute-start | bytes 2359304 | tf_op jit(solution)/shard_map/ppermute | solution.py:262
  9.5 4.2 %copy-start.3 = (s32[384,1]{0,1:T(1,128)S(1)}, s32[384,1]{0,1:T(1,128)}, u32[]{:S(2)}) copy-start(s32[384,1]{0,1:T(1,128)} %param.7) | copy-start | bytes 4612
  9.5 4.3 %copy-start.2 = (s32[8]{0:T(128)S(1)}, s32[8]{0:T(128)}, u32[]{:S(2)}) copy-start(s32[8]{0:T(128)} %storage_ref.1) | copy-start | bytes 100
  12.8 0.9 %copy-start = (f32[384,512]{1,0:T(8,128)}, f32[384,512]{1,0:T(8,128)S(1)}, u32[]{:S(2)}) copy-start(f32[384,512]{1,0:T(8,128)S(1)} %shard_map.66.here_ref) | copy-start | bytes 2359300
  15.3 13.6 %collective-permute-start.2 = (bf16[128,2304]{1,0:T(8,128)(2,1)}, bf16[128,2304]{1,0:T(8,128)(2,1)S(1)}, u32[]{:S(2)}, u32[]{:S(2)}) collective-permute-start(bf16[128,2304]{1,0:T(8,128)(2,1)} %collective-permute-done.rest_0_.rest_1_), channel_id=1, source_target_pairs={{4,0},{1,5},{8,4},{5,9},{12,8},{9,13},{14,12},{13,15},{10,14},{15,... | collective-permute-start | bytes 1769480 | tf_op jit(solution)/shard_map/ppermute | solution.py:296
  21.8 13.8 %collective-permute-start.4 = (bf16[128,2304]{1,0:T(8,128)(2,1)}, bf16[128,2304]{1,0:T(8,128)(2,1)S(1)}, u32[]{:S(2)}, u32[]{:S(2)}) collective-permute-start(bf16[128,2304]{1,0:T(8,128)(2,1)} %collective-permute-done.1.rest_0_.rest_2_), channel_id=1, source_target_pairs={{0,4},{5,1},{4,8},{9,5},{8,12},{13,9},{12,14},{15,13},{14,10},{11,... | collective-permute-start | bytes 1769480 | tf_op jit(solution)/shard_map/ppermute | solution.py:297
  28.9 12.9 %collective-permute-start.5 = (bf16[128,2304]{1,0:T(8,128)(2,1)S(1)}, bf16[128,2304]{1,0:T(8,128)(2,1)S(1)}, u32[]{:S(2)}, u32[]{:S(2)}) collective-permute-start(bf16[128,2304]{1,0:T(8,128)(2,1)S(1)} %collective-permute-done.2.rest_0_.rest_3_), channel_id=1, source_target_pairs={{4,0},{1,5},{8,4},{5,9},{12,8},{9,13},{14,12},{13,15},{10,14},{15,... | collective-permute-start | bytes 1769480 | tf_op jit(solution)/shard_map/ppermute | solution.py:293
  36.6 8.9 %collective-permute-start.6 = (bf16[64,2304]{1,0:T(8,128)(2,1)S(1)}, bf16[64,2304]{1,0:T(8,128)(2,1)S(1)}, u32[]{:S(2)}, u32[]{:S(2)}) collective-permute-start(bf16[64,2304]{1,0:T(8,128)(2,1)S(1)} %get-tuple-element.82), channel_id=1, source_target_pairs={{0,4},{5,1},{4,8},{9,5},{8,12},{13,9},{12,14},{15,13},{14,10},{11,... | collective-permute-start | bytes 884744 | tf_op jit(solution)/shard_map/ppermute | solution.py:294
  36.6 13.0 %collective-permute-start.8 = (bf16[64,2304]{1,0:T(8,128)(2,1)S(1)}, bf16[64,2304]{1,0:T(8,128)(2,1)S(1)}, u32[]{:S(2)}, u32[]{:S(2)}) collective-permute-start(bf16[64,2304]{1,0:T(8,128)(2,1)S(1)} %get-tuple-element.81), channel_id=1, source_target_pairs={{0,4},{5,1},{4,8},{9,5},{8,12},{13,9},{12,14},{15,13},{14,10},{11,... | collective-permute-start | bytes 884744 | tf_op jit(solution)/shard_map/ppermute | solution.py:294
  38.8 8.1 %copy-start.1 = (f32[384,512]{1,0:T(8,128)S(1)}, f32[384,512]{1,0:T(8,128)}, u32[]{:S(2)}) copy-start(f32[384,512]{1,0:T(8,128)} %copy-done) | copy-start | bytes 2359300
  41.8 9.6 %collective-permute-start.9 = (bf16[64,2304]{1,0:T(8,128)(2,1)S(1)}, bf16[64,2304]{1,0:T(8,128)(2,1)S(1)}, u32[]{:S(2)}, u32[]{:S(2)}) collective-permute-start(bf16[64,2304]{1,0:T(8,128)(2,1)S(1)} %slice.11), channel_id=1, source_target_pairs={{4,0},{1,5},{8,4},{5,9},{12,8},{9,13},{14,12},{13,15},{10,14},{15,... | collective-permute-start | bytes 884744 | tf_op jit(solution)/shard_map/ppermute | solution.py:322
  45.5 7.4 %collective-permute-start.10 = (bf16[64,2304]{1,0:T(8,128)(2,1)S(1)}, bf16[64,2304]{1,0:T(8,128)(2,1)S(1)}, u32[]{:S(2)}, u32[]{:S(2)}) collective-permute-start(bf16[64,2304]{1,0:T(8,128)(2,1)S(1)} %collective-permute-done.6.rest_1_.rest_2_), channel_id=1, source_target_pairs={{0,4},{5,1},{4,8},{9,5},{8,12},{13,9},{12,14},{15,13},{14,10},{11,... | collective-permute-start | bytes 884744 | tf_op jit(solution)/shard_map/ppermute | solution.py:323
  45.5 1.4 %collective-permute-start.7 = (f32[384,64]{1,0:T(8,128)S(1)}, f32[384,64]{1,0:T(8,128)S(1)}, u32[]{:S(2)}, u32[]{:S(2)}) collective-permute-start(f32[384,64]{1,0:T(8,128)S(1)} %shard_map.72.own_ref), channel_id=1, source_target_pairs={{0,1},{1,0},{2,3},{3,2},{4,5},{5,4},{6,7},{7,6},{8,9},{9,8},{10,11... | collective-permute-start | bytes 294920 | tf_op jit(solution)/shard_map/ppermute | solution.py:329
  53.5 1.4 %collective-permute-start.11 = (f32[192,128]{1,0:T(8,128)S(1)}, f32[192,128]{1,0:T(8,128)S(1)}, u32[]{:S(2)}, u32[]{:S(2)}) collective-permute-start(f32[192,128]{1,0:T(8,128)S(1)} %shard_map.77.own_ref), channel_id=1, source_target_pairs={{0,1},{1,0},{2,3},{3,2},{4,5},{5,4},{6,7},{7,6},{8,9},{9,8},{10,11... | collective-permute-start | bytes 294920 | tf_op jit(solution)/shard_map/ppermute | solution.py:363
